TPU v7x, 32 devices: a whole 2x2x4 slice. The times are simulated.
32 devices in a mesh: grp: 2 (over y), row: 4 (over z), col: 4 (over x, core).
Axes of the slice: x: 2, y: 2, z: 4, core: 2. Of those that a mesh axis runs over, the one named last changes fastest.
Arguments:
- frames: bfloat16 [16, 24576], P(None, ('grp', 'row', 'col')), parts along dimension 1, may hold values from -6 to 6
- vectors: bfloat16 [16, 24576], P(None, ('grp', 'row', 'col')), parts along dimension 1, may hold values from -8 to 8
- degrees: float32 [24576], P(('grp', 'row', 'col')), parts along dimension 0, may hold values from 1 to 10
- tile_table: int32 [16, 8, 2], replicated, may hold values from -1 to 15, as said below
Outputs:
- basis: float32 [16, 24576], P(None, ('grp', 'row', 'col')), parts along dimension 1
- ritz: float32 [32, 16], P('grp'), parts along dimension 0
There are 2 independent parts, one for each index of `grp`. A program takes and returns all parts, laid end to end along the dimension named above; an argument that names none is the same for every part. Nothing has to cross between parts.
Inputs may be any that keep to these rules, and one draw needn't show every extreme that they name: `tile_table`: row d lists the tiles computed by device d of row+col (index row * 4 + col): pairs (I, J) of frame blocks with I <= J, filled from the front, the remaining slots -1 in both entries. Every pair (I, I) is listed once, every other pair at most once, 76 pairs in all. Some device has all 8 slots filled.
All inputs are finite; a program needn't handle non-finite values.
Results may differ from a plain program's by a relative error of at most 0.0047.
Values may be sent and summed in bfloat16 or wider, within the bound.
No kernel may reach another device: no remote copies, remote signals or barrier semaphores. Data moves between devices by JAX's collectives and lax.ppermute only.
A program may use at most 64 MiB of HBM per device.

v0:
```python
import functools
import math

import jax
import jax.numpy as jnp
from jax import lax
from jax.experimental import pallas as pl
from jax.experimental.pallas import tpu as pltpu
from jax.sharding import PartitionSpec as P

unit = -math.log2(math.e) / 4.0

NT = (((1,), (1,)), ((), ()))
MIB = 1024 * 1024


def split3(x):
    high = x.astype(jnp.bfloat16).astype(jnp.float32)
    rest = x - high
    mid = rest.astype(jnp.bfloat16).astype(jnp.float32)
    low = (rest - mid).astype(jnp.bfloat16).astype(jnp.float32)
    return high, mid, low


def pack_kernel(
    frames_ref, vectors_in, degrees_ref, table_in,
    packed_ref, vectors_ref, root_ref, table_ref, degree_ref, sems,
):
    ncv = frames_ref.shape[0]
    copies = [
        pltpu.make_async_copy(vectors_in, vectors_ref, sems.at[0]),
        pltpu.make_async_copy(degrees_ref, degree_ref, sems.at[1]),
        pltpu.make_async_copy(frames_ref, packed_ref.at[pl.ds(0, ncv)], sems.at[2]),
        pltpu.make_async_copy(table_in, table_ref, sems.at[3]),
    ]
    for copy in copies:
        copy.start()
    copies[0].wait()
    copies[1].wait()
    root = lax.rsqrt(degree_ref[...])[None, :]
    root_ref[...] = root
    packed_ref[ncv:, :] = (vectors_ref[...].astype(jnp.float32) * root).astype(jnp.bfloat16)
    copies[2].wait()
    copies[3].wait()


def edge_rows(square, ones_first):
    high, mid, low = split3(square * unit)
    row = lax.broadcasted_iota(jnp.int32, (16, square.shape[1]), 0)
    base = 3 if ones_first else 0
    ones_at = 0 if ones_first else 3
    block = jnp.where((row >= ones_at) & (row < ones_at + 3), 1.0, 0.0)
    block = jnp.where(row == base, high, block)
    block = jnp.where(row == base + 1, mid, block)
    return jnp.where(row == base + 2, low, block)


def own_side(own):
    own = own.astype(jnp.float32)
    high, mid, low = split3(own * (-2.0 * unit))
    edge = edge_rows(jnp.sum(own * own, axis=0, keepdims=True), True)
    return jnp.concatenate([high, mid, low, edge], axis=0).astype(jnp.bfloat16)


def tile_image(side_ref, blocks):
    both = blocks[0] if len(blocks) == 1 else jnp.concatenate(blocks, axis=1)
    ncv = both.shape[0] // 2
    x, v = both[:ncv, :], both[ncv:, :]
    wide = x.astype(jnp.float32)
    edge = edge_rows(jnp.sum(wide * wide, axis=0, keepdims=True), False).astype(jnp.bfloat16)
    other = jnp.concatenate([x, x, x, edge], axis=0).T
    power = jnp.dot(other, side_ref[...], preferred_element_type=jnp.float32)
    kern = jnp.exp2(power).astype(jnp.bfloat16)
    return jnp.dot(v, kern, preferred_element_type=jnp.float32)


def own_kernel(packed_ref, side_ref, image_ref):
    side_ref[...] = own_side(packed_ref[: packed_ref.shape[0] // 2, :])
    image_ref[...] = tile_image(side_ref, [packed_ref[...]])


def add_blocks(places, sizes, table_ref, side_ref, blocks_ref, image_ref, list_ref):
    n_row, n_col = sizes
    my_row, my_col = lax.axis_index("row"), lax.axis_index("col")
    me = my_row * n_col + my_col
    first, second = table_ref[:, 0, :], table_ref[:, 1, :]
    other = jnp.where(first == me, second, jnp.where(second == me, first, -1))
    words = []
    for start in range(0, n_row * n_col, 16):
        bit = jnp.zeros(other.shape, jnp.float32)
        for b in range(16):
            bit = jnp.where(other == start + b, float(1 << b), bit)
        words.append(jnp.sum(bit).astype(jnp.int32))

    count = jnp.int32(0)
    for step, (row_bits, col_bits) in enumerate(places):
        block = (my_row ^ row_bits) * n_col + (my_col ^ col_bits)
        word = words[0]
        for w in range(1, len(words)):
            word = jnp.where(block // 16 == w, words[w], word)
        list_ref[count] = step
        count += (word >> (block % 16)) & 1

    def add_group(start, size):
        blocks = [blocks_ref[list_ref[start + k]] for k in range(size)]
        image_ref[...] += tile_image(side_ref, blocks)

    def add_triple(group, _):
        add_group(3 * group, 3)
        return 0

    def add_pair(group, _):
        add_group(3 * triples + 2 * group, 2)
        return 0

    triples = jnp.maximum(count // 3 - (count % 3 == 1).astype(jnp.int32), 0)
    rest = count - 3 * triples
    lax.fori_loop(0, triples, add_triple, 0)
    lax.fori_loop(0, rest // 2, add_pair, 0)

    @pl.when(rest == 1)
    def _():
        add_group(0, 1)


def part_kernel(places, sizes, table_ref, side_ref, blocks_ref, before_ref, image_ref, list_ref):
    image_ref[...] = before_ref[...]
    add_blocks(places, sizes, table_ref, side_ref, blocks_ref, image_ref, list_ref)


def last_kernel(
    places, sizes, table_ref, side_ref, blocks_ref, before_ref, vectors_ref, root_ref,
    applied_ref, gram_ref, image_ref, list_ref,
):
    image_ref[...] = before_ref[...]
    add_blocks(places, sizes, table_ref, side_ref, blocks_ref, image_ref, list_ref)
    n = vectors_ref.shape[0]
    applied = image_ref[...] * root_ref[...]
    applied_ref[...] = applied
    both = jnp.concatenate([applied, vectors_ref[...].astype(jnp.float32)], axis=0)
    gram = lax.dot_general(
        both, both, NT, precision=lax.Precision.HIGHEST, preferred_element_type=jnp.float32
    )
    wide = jnp.concatenate(
        [gram[:n, :n], gram[n:, :], jnp.zeros((n, n), jnp.float32)], axis=1
    )
    tile = jnp.concatenate([wide[: n // 2, :], wide[n // 2 :, :]], axis=1)
    for device in range(gram_ref.shape[0]):
        gram_ref[device] = tile


def inverse_factors(grams):
    n = grams[0].shape[0]
    half = 64
    tiles = range(n // 8)
    shape = (8, 2 * half)
    row = lax.broadcasted_iota(jnp.int32, shape, 0)
    lane = lax.broadcasted_iota(jnp.int32, shape, 1)
    columns = [
        [
            jnp.where(
                lane < half,
                jnp.broadcast_to(grams[0][8 * t : 8 * t + 8, j : j + 1], shape),
                jnp.broadcast_to(grams[1][8 * t : 8 * t + 8, j : j + 1], shape),
            )
            for t in tiles
        ]
        for j in range(n)
    ]
    right = [jnp.where(lane % half == row + 8 * t, 1.0, 0.0) for t in tiles]
    pivots = [jnp.ones(shape, jnp.float32) for t in tiles]
    for k in range(n):
        top, at = k // 8, k % 8
        pivot = columns[k][top][at : at + 1, :]
        pivots[top] = jnp.where(row == at, pivot, pivots[top])
        if k == n - 1:
            break
        scale = 1.0 / pivot
        factor = {t: columns[k][t] * scale for t in tiles if t >= top}
        factor[top] = jnp.where(row > at, factor[top], 0.0)
        for column in columns[k + 1 :] + [right]:
            line = column[top][at : at + 1, :]
            for t in factor:
                column[t] = column[t] - factor[t] * line
    result = jnp.concatenate([r * lax.rsqrt(p) for r, p in zip(right, pivots)], axis=0)
    return result[:, :n], result[:, half : half + n]


def finish_kernel(total_frames, grams_ref, applied_ref, basis_ref, ritz_ref):
    tile = grams_ref[0]
    for device in range(1, grams_ref.shape[0]):
        tile += grams_ref[device]
    n = applied_ref.shape[0]
    gram = jnp.concatenate([tile[:, : 4 * n], tile[:, 4 * n :]], axis=0)
    exact = functools.partial(
        lax.dot_general, precision=lax.Precision.HIGHEST, preferred_element_type=jnp.float32
    )
    plain = (((1,), (0,)), ((), ()))
    image_inverse, vector_inverse = inverse_factors([gram[:, :n], gram[:, 2 * n : 3 * n]])
    basis_ref[...] = exact(image_inverse * math.sqrt(total_frames), applied_ref[...], plain)
    half = exact(vector_inverse, gram[:, n : 2 * n], plain)
    ritz_ref[...] = exact(half, vector_inverse, NT)


def sent(x, hop):
    n_row, n_col = lax.axis_size("row"), lax.axis_size("col")
    pairs = [
        (r * n_col + c, (r ^ hop[0]) * n_col + (c ^ hop[1]))
        for r in range(n_row)
        for c in range(n_col)
    ]
    return lax.ppermute(x, ("row", "col"), pairs)


def beyond(offsets, hop):
    return [(r ^ hop[0], c ^ hop[1]) for r, c in offsets]


def exchange_plan(n_row, n_col):
    if (n_row, n_col) == (4, 4):
        direct = [(0, 3), (2, 1), (1, 1)]
        return direct, [((0, 3), [(1, 1), (2, 1)]), ((3, 1), [(0, 3)]), ((1, 1), [(2, 1)])]
    lines = [(r, 1) for r in range(1, n_row)]
    chips = [(0, c) for c in range(3, n_col, 2)]
    return chips + lines, [(chip, lines) for chip in chips]


def per_device(frames, vectors, degrees, tile_table):
    ncv, rows = frames.shape
    nvec = vectors.shape[0]
    n_row, n_col = lax.axis_size("row"), lax.axis_size("col")
    devices = n_row * n_col
    sizes = (n_row, n_col)
    vmem = pl.BlockSpec(memory_space=pltpu.VMEM)

    def call(kernel, name, outs, *args, limit=24, where=vmem, **keywords):
        shapes = [jax.ShapeDtypeStruct(*out) for out in outs]
        return pl.pallas_call(
            kernel,
            out_shape=shapes,
            in_specs=[where] * len(args),
            out_specs=[vmem] * len(outs),
            compiler_params=pltpu.CompilerParams(vmem_limit_bytes=limit * MIB),
            name=name,
            **keywords,
        )(*args)

    image_type = ((nvec, rows), jnp.float32)

    table = tile_table.transpose(1, 2, 0)
    packed, vectors, root, table = call(
        pack_kernel,
        "pack",
        [
            ((ncv + nvec, rows), jnp.bfloat16),
            (vectors.shape, vectors.dtype),
            ((1, rows), jnp.float32),
            (table.shape, table.dtype),
        ],
        *(
            pltpu.with_memory_space_constraint(x, pltpu.HBM)
            for x in (frames, vectors, degrees, table)
        ),
        where=pl.BlockSpec(memory_space=pltpu.HBM),
        scratch_shapes=[
            pltpu.VMEM(degrees.shape, degrees.dtype),
            pltpu.SemaphoreType.DMA((4,)),
        ],
    )
    core = (0, 1)
    direct, forwards = exchange_plan(n_row, n_col)
    held = {offset: sent(packed, offset) for offset in direct}
    side, image = call(
        own_kernel,
        "own",
        [((3 * ncv + 16, rows), jnp.bfloat16), image_type],
        packed,
    )

    def add(name, places, blocks, image):
        (image,) = call(
            functools.partial(part_kernel, places, sizes),
            name,
            [image_type],
            table,
            side,
            blocks,
            image,
            input_output_aliases={3: 0},
            scratch_shapes=[pltpu.SMEM((len(places) + 1,), jnp.int32)],
        )
        return image

    early, others = direct[0], direct[1:]
    held[early], image = lax.optimization_barrier((held[early], image))
    image = add("add_first", [early], held[early][None], image)
    rest, image = lax.optimization_barrier(([held[offset] for offset in direct], image))
    held.update(zip(direct, rest))
    across_places = []
    across = []
    for hop, offsets in forwards:
        across.append(sent(jnp.stack([held[offset] for offset in offsets]), hop))
        across_places += beyond(offsets, hop)
    near = jnp.stack([held[offset] for offset in others + [early]] + [packed])
    other_near = sent(near, core)
    image = add("add_near", others, near, image)
    image = add("add_core", beyond(others + [early, (0, 0)], core), other_near, image)
    across, image = lax.optimization_barrier((across, image))
    across = jnp.concatenate(across)
    far = sent(across, core)
    image = add("add_across", across_places, across, image)
    far_places = beyond(across_places, core)
    applied, gram = call(
        functools.partial(last_kernel, far_places, sizes),
        "add_far",
        [((nvec, rows), jnp.float32), ((devices, nvec // 2, 8 * nvec), jnp.float32)],
        table,
        side,
        far,
        image,
        vectors,
        root,
        scratch_shapes=[
            pltpu.VMEM(*image_type),
            pltpu.SMEM((len(far_places) + 1,), jnp.int32),
        ],
    )
    grams = lax.all_to_all(gram, ("row", "col"), 0, 0)
    basis, ritz = call(
        functools.partial(finish_kernel, rows * devices),
        "finish",
        [((nvec, rows), jnp.float32), ((nvec, nvec), jnp.float32)],
        grams,
        applied,
    )
    return (basis, ritz)


def solution(mesh):
    split = P(None, ("grp", "row", "col"))
    return jax.shard_map(
        per_device,
        mesh=mesh,
        in_specs=(split, split, P(("grp", "row", "col")), P()),
        out_specs=(split, P("grp", None)),
        check_vma=False,
    )
```

profile of v0, /device:TPU:0, one launch (start us, length us, event | category | flops | bytes accessed | tf_op | source)
XLA Modules:
  0.0 34.4 jit_solution(3196597250234060389)
XLA Ops:
  0.6 0.8 %pack.1 = (bf16[32,768]{1,0:T(8,128)(2,1)S(1)}, bf16[16,768]{1,0:T(8,128)(2,1)S(1)}, f32[1,768]{1,0:T(1,128)S(1)}, s32[8,2,16]{2,1,0:T(2,128)S(1)}) custom-call(bf16[16,768]{1,0:T(8,128)(2,1)} %frames_ref.1, bf16[16,768]{1,0:T(8,128)(2,1)} %vectors_in.1, f32[768]{0:T(1024)} %degrees_ref.1, s32[8,2,16]{2,1,0:T(2,128)} %bitcast.15), custom_call_target="tpu_custom_call" | custom-call | tf_op jit(solution)/shard_map/pack/pallas_call | solution.py:238
  1.4 2.4 %collective-permute-start = (bf16[32,768]{1,0:T(8,128)(2,1)S(1)}, bf16[32,768]{1,0:T(8,128)(2,1)S(1)}, u32[]{:S(2)}, u32[]{:S(2)}) collective-permute-start(bf16[32,768]{1,0:T(8,128)(2,1)S(1)} %get-tuple-element.21.packed_ref), channel_id=1, source_target_pairs={{0,3},{1,2},{2,1},{3,0},{4,7},{5,6},{6,5},{7,4},{8,11},{9,10},{10,... | collective-permute-start | bytes 147464 | tf_op jit(solution)/shard_map/ppermute | solution.py:212
  3.9 2.9 %collective-permute-start.1 = (bf16[32,768]{1,0:T(8,128)(2,1)S(1)}, bf16[32,768]{1,0:T(8,128)(2,1)S(1)}, u32[]{:S(2)}, u32[]{:S(2)}) collective-permute-start(bf16[32,768]{1,0:T(8,128)(2,1)S(1)} %get-tuple-element.21.packed_ref), channel_id=1, source_target_pairs={{0,9},{1,8},{2,11},{3,10},{4,13},{5,12},{6,15},{7,14},{8,1},{9,0},... | collective-permute-start | bytes 147464 | tf_op jit(solution)/shard_map/ppermute | solution.py:212
  6.8 1.0 %collective-permute-start.2 = (bf16[32,768]{1,0:T(8,128)(2,1)S(1)}, bf16[32,768]{1,0:T(8,128)(2,1)S(1)}, u32[]{:S(2)}, u32[]{:S(2)}) collective-permute-start(bf16[32,768]{1,0:T(8,128)(2,1)S(1)} %get-tuple-element.21.packed_ref), channel_id=1, source_target_pairs={{0,5},{1,4},{2,7},{3,6},{4,1},{5,0},{6,3},{7,2},{8,13},{9,12},{10,... | collective-permute-start | bytes 147464 | tf_op jit(solution)/shard_map/ppermute | solution.py:212
  7.8 0.7 %own.1 = (bf16[64,768]{1,0:T(8,128)(2,1)S(1)}, f32[16,768]{1,0:T(8,128)S(1)}) custom-call(bf16[32,768]{1,0:T(8,128)(2,1)S(1)} %get-tuple-element.21.packed_ref), custom_call_target="tpu_custom_call" | custom-call | tf_op jit(solution)/shard_map/own/pallas_call | solution.py:238
  8.4 0.0 collective-permute-done
  8.4 0.9 %add_first.1.before_ref = f32[16,768]{1,0:T(8,128)S(1)} custom-call(s32[8,2,16]{2,1,0:T(2,128)S(1)} %get-tuple-element.20.table_ref, bf16[64,768]{1,0:T(8,128)(2,1)S(1)} %get-tuple-element.22.side_ref, bf16[1,32,768]{2,1,0:T(8,128)(2,1)S(1)} %bitcast.7, f32[16,768]{1,0:T(8,128)S(1)} %get-tuple-element.25.before_ref), custom_call_target="tpu_custom_call", output_to_operand_aliasing={{}: (3, {})} | custom-call | tf_op jit(solution)/shard_map/add_first/pallas_call | solution.py:238
  9.3 0.0 collective-permute-done.1
  9.3 1.4 %collective-permute-done.2 = bf16[32,768]{1,0:T(8,128)(2,1)S(1)} collective-permute-done((bf16[32,768]{1,0:T(8,128)(2,1)S(1)}, bf16[32,768]{1,0:T(8,128)(2,1)S(1)}, u32[]{:S(2)}, u32[]{:S(2)}) %collective-permute-start.2) | collective-permute-done | bytes 49184 | tf_op jit(solution)/shard_map/ppermute | solution.py:212
  10.7 0.2 collective-permute-start.6
  10.9 0.6 %collective-permute-start.3 = (bf16[2,32,768]{2,1,0:T(8,128)(2,1)S(1)}, bf16[2,32,768]{2,1,0:T(8,128)(2,1)S(1)}, u32[]{:S(2)}, u32[]{:S(2)}) collective-permute-start(bf16[2,32,768]{2,1,0:T(8,128)(2,1)S(1)} %pad_maximum_fusion.1), channel_id=1, source_target_pairs={{0,3},{1,2},{2,1},{3,0},{4,7},{5,6},{6,5},{7,4},{8,11},{9,10},{10,... | collective-permute-start | bytes 294920 | tf_op jit(solution)/shard_map/ppermute | solution.py:212
  11.5 2.3 %collective-permute-start.4 = (bf16[1,32,768]{2,1,0:T(8,128)(2,1)S(1)}, bf16[1,32,768]{2,1,0:T(8,128)(2,1)S(1)}, u32[]{:S(2)}, u32[]{:S(2)}) collective-permute-start(bf16[1,32,768]{2,1,0:T(8,128)(2,1)S(1)} %bitcast.9), channel_id=1, source_target_pairs={{0,13},{1,12},{2,15},{3,14},{4,9},{5,8},{6,11},{7,10},{8,5},{9,4},... | collective-permute-start | bytes 147464 | tf_op jit(solution)/shard_map/ppermute | solution.py:212
  13.8 0.0 collective-permute-start.5
  13.8 0.9 %add_near.1.before_ref = f32[16,768]{1,0:T(8,128)S(1)} custom-call(s32[8,2,16]{2,1,0:T(2,128)S(1)} %get-tuple-element.20.table_ref, bf16[64,768]{1,0:T(8,128)(2,1)S(1)} %get-tuple-element.22.side_ref, bf16[4,32,768]{2,1,0:T(8,128)(2,1)S(1)} %pad_maximum_fusion.blocks_ref, f32[16,768]{1,0:T(8,128)S(1)} %add_first.1.before_ref), custom_call_target="tpu_custom_call", output_to_operand_aliasing={{}: (3, {})} | custom-call | tf_op jit(solution)/shard_map/add_near/pallas_call | solution.py:238
  14.7 0.0 collective-permute-done.6.blocks_ref
  14.7 1.8 %add_core.1.before_ref = f32[16,768]{1,0:T(8,128)S(1)} custom-call(s32[8,2,16]{2,1,0:T(2,128)S(1)} %get-tuple-element.20.table_ref, bf16[64,768]{1,0:T(8,128)(2,1)S(1)} %get-tuple-element.22.side_ref, bf16[4,32,768]{2,1,0:T(8,128)(2,1)S(1)} %collective-permute-done.6.blocks_ref, f32[16,768]{1,0:T(8,128)S(1)} %add_near.1.before_ref), custom_call_target="tpu_custom_call", output_to_operand_aliasing={{}: (3, {})} | custom-call | tf_op jit(solution)/shard_map/add_core/pallas_call | solution.py:238
  16.5 0.7 %collective-permute-done.4 = bf16[1,32,768]{2,1,0:T(8,128)(2,1)S(1)} collective-permute-done((bf16[1,32,768]{2,1,0:T(8,128)(2,1)S(1)}, bf16[1,32,768]{2,1,0:T(8,128)(2,1)S(1)}, u32[]{:S(2)}, u32[]{:S(2)}) %collective-permute-start.4) | collective-permute-done | bytes 49184 | tf_op jit(solution)/shard_map/ppermute | solution.py:212
  17.1 1.3 %collective-permute-done.5 = bf16[1,32,768]{2,1,0:T(8,128)(2,1)S(1)} collective-permute-done((bf16[1,32,768]{2,1,0:T(8,128)(2,1)S(1)}, bf16[1,32,768]{2,1,0:T(8,128)(2,1)S(1)}, u32[]{:S(2)}, u32[]{:S(2)}) %collective-permute-start.5) | collective-permute-done | bytes 49184 | tf_op jit(solution)/shard_map/ppermute | solution.py:212
  18.4 0.0 collective-permute-done.3
  18.5 0.2 collective-permute-start.7
  18.6 2.6 %add_across.1.before_ref = f32[16,768]{1,0:T(8,128)S(1)} custom-call(s32[8,2,16]{2,1,0:T(2,128)S(1)} %get-tuple-element.20.table_ref, bf16[64,768]{1,0:T(8,128)(2,1)S(1)} %get-tuple-element.22.side_ref, bf16[4,32,768]{2,1,0:T(8,128)(2,1)S(1)} %constant_dynamic-update-slice_fusion.blocks_ref, ...), custom_call_target="tpu_custom_call", output_to_operand_aliasing={{}: (3, {})} | custom-call | tf_op jit(solution)/shard_map/add_across/pallas_call | solution.py:238
  21.2 0.0 collective-permute-done.7.blocks_ref
  21.2 1.7 %add_far.1 = (f32[16,768]{1,0:T(8,128)S(1)}, f32[16,8,128]{2,1,0:T(8,128)S(1)}) custom-call(s32[8,2,16]{2,1,0:T(2,128)S(1)} %get-tuple-element.20.table_ref, bf16[64,768]{1,0:T(8,128)(2,1)S(1)} %get-tuple-element.22.side_ref, bf16[4,32,768]{2,1,0:T(8,128)(2,1)S(1)} %collective-permute-done.7.blocks_ref, f32[16,768]{1,0:T(8,128)S(1)} %add_across.1.before_ref, ...), custom_call_target="tpu_custom_call" | custom-call | tf_op jit(solution)/shard_map/add_far/pallas_call | solution.py:238
  22.9 10.2 %all_to_all.5.grams_ref = f32[16,8,128]{2,1,0:T(8,128)S(1)} all-to-all(f32[16,8,128]{2,1,0:T(8,128)S(1)} %get-tuple-element.36), channel_id=1, replica_groups=mesh['grp'=2,'row'=4,'col'=4] {'row','col'}, dimensions={0} | all-to-all | bytes 131072 | tf_op jit(solution)/shard_map/all_to_all | solution.py:328
  33.2 1.3 %finish.1 = (f32[16,768]{1,0:T(8,128)}, f32[16,16]{1,0:T(8,128)}) custom-call(f32[16,8,128]{2,1,0:T(8,128)S(1)} %all_to_all.5.grams_ref, f32[16,768]{1,0:T(8,128)S(1)} %get-tuple-element.37.applied_ref), custom_call_target="tpu_custom_call" | custom-call | tf_op jit(solution)/shard_map/finish/pallas_call | solution.py:238
  (5 shorter events, 0.1 us)
Async XLA Ops:
  1.4 7.0 %collective-permute-start = (bf16[32,768]{1,0:T(8,128)(2,1)S(1)}, bf16[32,768]{1,0:T(8,128)(2,1)S(1)}, u32[]{:S(2)}, u32[]{:S(2)}) collective-permute-start(bf16[32,768]{1,0:T(8,128)(2,1)S(1)} %get-tuple-element.21.packed_ref), channel_id=1, source_target_pairs={{0,3},{1,2},{2,1},{3,0},{4,7},{5,6},{6,5},{7,4},{8,11},{9,10},{10,... | collective-permute-start | bytes 147464 | tf_op jit(solution)/shard_map/ppermute | solution.py:212
  3.9 5.4 %collective-permute-start.1 = (bf16[32,768]{1,0:T(8,128)(2,1)S(1)}, bf16[32,768]{1,0:T(8,128)(2,1)S(1)}, u32[]{:S(2)}, u32[]{:S(2)}) collective-permute-start(bf16[32,768]{1,0:T(8,128)(2,1)S(1)} %get-tuple-element.21.packed_ref), channel_id=1, source_target_pairs={{0,9},{1,8},{2,11},{3,10},{4,13},{5,12},{6,15},{7,14},{8,1},{9,0},... | collective-permute-start | bytes 147464 | tf_op jit(solution)/shard_map/ppermute | solution.py:212
  6.8 3.9 %collective-permute-start.2 = (bf16[32,768]{1,0:T(8,128)(2,1)S(1)}, bf16[32,768]{1,0:T(8,128)(2,1)S(1)}, u32[]{:S(2)}, u32[]{:S(2)}) collective-permute-start(bf16[32,768]{1,0:T(8,128)(2,1)S(1)} %get-tuple-element.21.packed_ref), channel_id=1, source_target_pairs={{0,5},{1,4},{2,7},{3,6},{4,1},{5,0},{6,3},{7,2},{8,13},{9,12},{10,... | collective-permute-start | bytes 147464 | tf_op jit(solution)/shard_map/ppermute | solution.py:212
  10.7 4.0 %collective-permute-start.6 = (bf16[4,32,768]{2,1,0:T(8,128)(2,1)S(1)}, bf16[4,32,768]{2,1,0:T(8,128)(2,1)S(1)}, u32[]{:S(2)}, u32[]{:S(2)}) collective-permute-start(bf16[4,32,768]{2,1,0:T(8,128)(2,1)S(1)} %pad_maximum_fusion.blocks_ref), channel_id=1, source_target_pairs={{0,1},{1,0},{2,3},{3,2},{4,5},{5,4},{6,7},{7,6},{8,9},{9,8},{10,11... | collective-permute-start | bytes 589832 | tf_op jit(solution)/shard_map/ppermute | solution.py:212
  10.9 7.5 %collective-permute-start.3 = (bf16[2,32,768]{2,1,0:T(8,128)(2,1)S(1)}, bf16[2,32,768]{2,1,0:T(8,128)(2,1)S(1)}, u32[]{:S(2)}, u32[]{:S(2)}) collective-permute-start(bf16[2,32,768]{2,1,0:T(8,128)(2,1)S(1)} %pad_maximum_fusion.1), channel_id=1, source_target_pairs={{0,3},{1,2},{2,1},{3,0},{4,7},{5,6},{6,5},{7,4},{8,11},{9,10},{10,... | collective-permute-start | bytes 294920 | tf_op jit(solution)/shard_map/ppermute | solution.py:212
  11.5 5.6 %collective-permute-start.4 = (bf16[1,32,768]{2,1,0:T(8,128)(2,1)S(1)}, bf16[1,32,768]{2,1,0:T(8,128)(2,1)S(1)}, u32[]{:S(2)}, u32[]{:S(2)}) collective-permute-start(bf16[1,32,768]{2,1,0:T(8,128)(2,1)S(1)} %bitcast.9), channel_id=1, source_target_pairs={{0,13},{1,12},{2,15},{3,14},{4,9},{5,8},{6,11},{7,10},{8,5},{9,4},... | collective-permute-start | bytes 147464 | tf_op jit(solution)/shard_map/ppermute | solution.py:212
  13.8 4.6 %collective-permute-start.5 = (bf16[1,32,768]{2,1,0:T(8,128)(2,1)S(1)}, bf16[1,32,768]{2,1,0:T(8,128)(2,1)S(1)}, u32[]{:S(2)}, u32[]{:S(2)}) collective-permute-start(bf16[1,32,768]{2,1,0:T(8,128)(2,1)S(1)} %bitcast.12), channel_id=1, source_target_pairs={{0,5},{1,4},{2,7},{3,6},{4,1},{5,0},{6,3},{7,2},{8,13},{9,12},{10,... | collective-permute-start | bytes 147464 | tf_op jit(solution)/shard_map/ppermute | solution.py:212
  18.5 2.8 %collective-permute-start.7 = (bf16[4,32,768]{2,1,0:T(8,128)(2,1)S(1)}, bf16[4,32,768]{2,1,0:T(8,128)(2,1)S(1)}, u32[]{:S(2)}, u32[]{:S(2)}) collective-permute-start(bf16[4,32,768]{2,1,0:T(8,128)(2,1)S(1)} %constant_dynamic-update-slice_fusion.blocks_ref), channel_id=1, source_target_pairs={{0,1},{1,0},{2,3},{3,2},{4,5},{5,4},{6,7},{7,6},{8,9},{9,8},{10,11... | collective-permute-start | bytes 589832 | tf_op jit(solution)/shard_map/ppermute | solution.py:212
where the time goes:
time: 34.3 us; the launch traced here: 34.4 us
  Pallas kernels  10.6 us (31%)
  blocking collectives  10.2 us (30%)
  starting transfers between devices  9.6 us (28%)
  waiting for transfers between devices  3.32 us (10%)
  between operations  0.68 us (2%)
    pallas_call x8, Pallas kernels, call(): pl.pallas_call(kernel, out_shape=shapes, in_specs=[where] * len(args), ou...  10.6 us
    all_to_all x1, blocking collectives, per_device(): grams = lax.all_to_all(gram, ('row', 'col'), 0, 0)  10.2 us
    ppermute x8, starting transfers between devices, sent(): return lax.ppermute(x, ('row', 'col'), pairs)  9.6 us
    ppermute x8, waiting for transfers between devices, sent(): return lax.ppermute(x, ('row', 'col'), pairs)  3.32 us
  transfers between devices with their start and end apart: 8, of which 3 were waited for; matrix products, arithmetic and copies ran while one was open for 0% of the time, Pallas kernels for 20%

commit v1 on v0

--- a/solution.py
+++ b/solution.py
@@ -79,11 +79,15 @@
     image_ref[...] = tile_image(side_ref, [packed_ref[...]])
 
 
-def add_blocks(places, sizes, table_ref, side_ref, blocks_ref, image_ref, list_ref):
+def add_blocks(target, places, sizes, table_ref, side_ref, blocks_ref, image_ref, list_ref):
     n_row, n_col = sizes
     my_row, my_col = lax.axis_index("row"), lax.axis_index("col")
-    me = my_row * n_col + my_col
+
+    def number(offset):
+        return (my_row ^ offset[0]) * n_col + (my_col ^ offset[1])
+
     first, second = table_ref[:, 0, :], table_ref[:, 1, :]
+    me = number(target)
     other = jnp.where(first == me, second, jnp.where(second == me, first, -1))
     words = []
     for start in range(0, n_row * n_col, 16):
@@ -93,8 +97,8 @@
         words.append(jnp.sum(bit).astype(jnp.int32))
 
     count = jnp.int32(0)
-    for step, (row_bits, col_bits) in enumerate(places):
-        block = (my_row ^ row_bits) * n_col + (my_col ^ col_bits)
+    for step, place in enumerate(places):
+        block = number(place)
         word = words[0]
         for w in range(1, len(words)):
             word = jnp.where(block // 16 == w, words[w], word)
@@ -115,27 +119,41 @@
 
     triples = jnp.maximum(count // 3 - (count % 3 == 1).astype(jnp.int32), 0)
     rest = count - 3 * triples
-    lax.fori_loop(0, triples, add_triple, 0)
-    lax.fori_loop(0, rest // 2, add_pair, 0)
+    if len(places) >= 3:
+        lax.fori_loop(0, triples, add_triple, 0)
+    if len(places) >= 2:
+        lax.fori_loop(0, rest // 2, add_pair, 0)
 
     @pl.when(rest == 1)
     def _():
         add_group(0, 1)
 
 
-def part_kernel(places, sizes, table_ref, side_ref, blocks_ref, before_ref, image_ref, list_ref):
+def meet_kernel(
+    places, sizes, table_ref, side_ref, blocks_ref, before_ref, image_ref, partner_side_ref, list_ref
+):
+    partner_side_ref[...] = own_side(blocks_ref[0, : blocks_ref.shape[1] // 2, :])
     image_ref[...] = before_ref[...]
-    add_blocks(places, sizes, table_ref, side_ref, blocks_ref, image_ref, list_ref)
-
-
-def last_kernel(
-    places, sizes, table_ref, side_ref, blocks_ref, before_ref, vectors_ref, root_ref,
-    applied_ref, gram_ref, image_ref, list_ref,
+    add_blocks((0, 0), places, sizes, table_ref, side_ref, blocks_ref, image_ref, list_ref)
+
+
+def first_kernel(target, places, sizes, table_ref, side_ref, blocks_ref, image_ref, list_ref):
+    image_ref[...] = jnp.zeros_like(image_ref)
+    add_blocks(target, places, sizes, table_ref, side_ref, blocks_ref, image_ref, list_ref)
+
+
+def part_kernel(
+    target, places, sizes, table_ref, side_ref, blocks_ref, before_ref, image_ref, list_ref
 ):
     image_ref[...] = before_ref[...]
-    add_blocks(places, sizes, table_ref, side_ref, blocks_ref, image_ref, list_ref)
+    add_blocks(target, places, sizes, table_ref, side_ref, blocks_ref, image_ref, list_ref)
+
+
+def last_kernel(vectors_ref, root_ref, *refs):
+    *part_refs, applied_ref, gram_ref = refs
+    image = sum(part_ref[...] for part_ref in part_refs)
     n = vectors_ref.shape[0]
-    applied = image_ref[...] * root_ref[...]
+    applied = image * root_ref[...]
     applied_ref[...] = applied
     both = jnp.concatenate([applied, vectors_ref[...].astype(jnp.float32)], axis=0)
     gram = lax.dot_general(
@@ -216,15 +234,6 @@
     return [(r ^ hop[0], c ^ hop[1]) for r, c in offsets]
 
 
-def exchange_plan(n_row, n_col):
-    if (n_row, n_col) == (4, 4):
-        direct = [(0, 3), (2, 1), (1, 1)]
-        return direct, [((0, 3), [(1, 1), (2, 1)]), ((3, 1), [(0, 3)]), ((1, 1), [(2, 1)])]
-    lines = [(r, 1) for r in range(1, n_row)]
-    chips = [(0, c) for c in range(3, n_col, 2)]
-    return chips + lines, [(chip, lines) for chip in chips]
-
-
 def per_device(frames, vectors, degrees, tile_table):
     ncv, rows = frames.shape
     nvec = vectors.shape[0]
@@ -268,62 +277,80 @@
         ],
     )
     core = (0, 1)
-    direct, forwards = exchange_plan(n_row, n_col)
-    held = {offset: sent(packed, offset) for offset in direct}
-    side, image = call(
-        own_kernel,
-        "own",
-        [((3 * ncv + 16, rows), jnp.bfloat16), image_type],
-        packed,
-    )
-
-    def add(name, places, blocks, image):
-        (image,) = call(
-            functools.partial(part_kernel, places, sizes),
+    lines = [(r, 1) for r in range(n_row - 1, 0, -1)]
+    if n_row == 4:
+        lines = [(3, 1), (1, 1), (2, 1)]
+    partners = [(0, c) for c in range(3, n_col, 2)]
+    met = [sent(packed, hop) for hop in partners]
+    line = [sent(packed, hop) for hop in lines]
+
+    def call_blocks(kernel, name, outs, places, *args, **keywords):
+        return call(
+            functools.partial(kernel, places, sizes),
             name,
-            [image_type],
+            outs,
             table,
+            *args,
+            scratch_shapes=[pltpu.SMEM((len(places) + 1,), jnp.int32)],
+            **keywords,
+        )
+
+    side_type = ((3 * ncv + 16, rows), jnp.bfloat16)
+    side, image = call(own_kernel, "own", [side_type, image_type], packed)
+    met, image = lax.optimization_barrier((met, image))
+    sides = []
+    for hop, block in zip(partners, met):
+        image, partner_side = call_blocks(
+            meet_kernel,
+            "meet",
+            [image_type, side_type],
+            [hop],
             side,
-            blocks,
+            block[None],
             image,
             input_output_aliases={3: 0},
-            scratch_shapes=[pltpu.SMEM((len(places) + 1,), jnp.int32)],
         )
-        return image
-
-    early, others = direct[0], direct[1:]
-    held[early], image = lax.optimization_barrier((held[early], image))
-    image = add("add_first", [early], held[early][None], image)
-    rest, image = lax.optimization_barrier(([held[offset] for offset in direct], image))
-    held.update(zip(direct, rest))
-    across_places = []
-    across = []
-    for hop, offsets in forwards:
-        across.append(sent(jnp.stack([held[offset] for offset in offsets]), hop))
-        across_places += beyond(offsets, hop)
-    near = jnp.stack([held[offset] for offset in others + [early]] + [packed])
-    other_near = sent(near, core)
-    image = add("add_near", others, near, image)
-    image = add("add_core", beyond(others + [early, (0, 0)], core), other_near, image)
-    across, image = lax.optimization_barrier((across, image))
-    across = jnp.concatenate(across)
-    far = sent(across, core)
-    image = add("add_across", across_places, across, image)
-    far_places = beyond(across_places, core)
+        sides.append(partner_side)
+    line, image = lax.optimization_barrier((line, image))
+    near = jnp.stack(line)
+    other = sent(jnp.stack(line + met + [packed]), core)
+    other_lines = beyond(lines, core)
+    parts = []
+    for hop, partner_side in zip(partners, sides):
+        (part,) = call_blocks(
+            functools.partial(first_kernel, hop), "partner_near", [image_type], lines, partner_side, near
+        )
+        (part,) = call_blocks(
+            functools.partial(part_kernel, hop),
+            "partner_core",
+            [image_type],
+            other_lines,
+            partner_side,
+            other,
+            part,
+            input_output_aliases={3: 0},
+        )
+        parts.append(part)
+    parts, image = lax.optimization_barrier((parts, image))
+    received = [sent(part, hop) for hop, part in zip(partners, parts)]
+    (image,) = call_blocks(
+        functools.partial(part_kernel, (0, 0)),
+        "add_own",
+        [image_type],
+        lines + beyond(lines + partners + [(0, 0)], core),
+        side,
+        jnp.concatenate([near, other]),
+        image,
+        input_output_aliases={3: 0},
+    )
     applied, gram = call(
-        functools.partial(last_kernel, far_places, sizes),
-        "add_far",
+        last_kernel,
+        "last",
         [((nvec, rows), jnp.float32), ((devices, nvec // 2, 8 * nvec), jnp.float32)],
-        table,
-        side,
-        far,
-        image,
         vectors,
         root,
-        scratch_shapes=[
-            pltpu.VMEM(*image_type),
-            pltpu.SMEM((len(far_places) + 1,), jnp.int32),
-        ],
+        image,
+        *received,
     )
     grams = lax.all_to_all(gram, ("row", "col"), 0, 0)
     basis, ritz = call(

time: 34.3 us -> 32.5 us (0.948)
  starting transfers between devices: 9.6 us -> 7.57 us
  Pallas kernels: 10.6 us -> 9.78 us
  waiting for transfers between devices: 3.32 us -> 4.01 us
    ppermute x8 -> x6, starting transfers between devices: 9.6 us -> 7.57 us  [sent(): return lax.ppermute(x, ('row', 'col'), pairs)]
    pallas_call x8, Pallas kernels: 10.6 us -> 9.78 us  [call(): pl.pallas_call(kernel, out_shape=shapes, in_specs=[where] * len(args), ou...]
    ppermute x8 -> x6, waiting for transfers between devices: 3.32 us -> 4.01 us  [sent(): return lax.ppermute(x, ('row', 'col'), pairs)]
  transfers between devices with their start and end apart: 8 -> 6, of which waited for: 3 -> 3; matrix products, arithmetic and copies ran while one was open for 0% -> 0% of each run, Pallas kernels for 20% -> 17%
where the time goes in v1:
time: 32.5 us; the launch traced here: 32.6 us
  blocking collectives  10.4 us (32%)
  Pallas kernels  9.78 us (30%)
  starting transfers between devices  7.57 us (23%)
  waiting for transfers between devices  4.01 us (12%)
  between operations  0.71 us (2%)
    all_to_all x1, blocking collectives, per_device(): grams = lax.all_to_all(gram, ('row', 'col'), 0, 0)  10.4 us
    pallas_call x8, Pallas kernels, call(): pl.pallas_call(kernel, out_shape=shapes, in_specs=[where] * len(args), ou...  9.78 us
    ppermute x6, starting transfers between devices, sent(): return lax.ppermute(x, ('row', 'col'), pairs)  7.57 us
    ppermute x6, waiting for transfers between devices, sent(): return lax.ppermute(x, ('row', 'col'), pairs)  4.01 us
  transfers between devices with their start and end apart: 6, of which 3 were waited for; matrix products, arithmetic and copies ran while one was open for 0% of the time, Pallas kernels for 17%

profile of v1, /device:TPU:0, one launch (start us, length us, event | category | flops | bytes accessed | tf_op | source)
XLA Modules:
  0.0 32.6 jit_solution(12660463009971878452)
XLA Ops:
  0.6 0.8 %pack.1 = (bf16[32,768]{1,0:T(8,128)(2,1)S(1)}, bf16[16,768]{1,0:T(8,128)(2,1)S(1)}, f32[1,768]{1,0:T(1,128)S(1)}, s32[8,2,16]{2,1,0:T(2,128)S(1)}) custom-call(bf16[16,768]{1,0:T(8,128)(2,1)} %frames_ref.1, bf16[16,768]{1,0:T(8,128)(2,1)} %vectors_in.1, f32[768]{0:T(1024)} %degrees_ref.1, s32[8,2,16]{2,1,0:T(2,128)} %bitcast.18), custom_call_target="tpu_custom_call" | custom-call | tf_op jit(solution)/shard_map/pack/pallas_call | solution.py:247
  1.4 2.4 %collective-permute-start.3 = (bf16[32,768]{1,0:T(8,128)(2,1)S(1)}, bf16[32,768]{1,0:T(8,128)(2,1)S(1)}, u32[]{:S(2)}, u32[]{:S(2)}) collective-permute-start(bf16[32,768]{1,0:T(8,128)(2,1)S(1)} %get-tuple-element.23.packed_ref), channel_id=1, source_target_pairs={{0,3},{1,2},{2,1},{3,0},{4,7},{5,6},{6,5},{7,4},{8,11},{9,10},{10,... | collective-permute-start | bytes 147464 | tf_op jit(solution)/shard_map/ppermute | solution.py:230
  3.9 2.9 %collective-permute-start.2 = (bf16[32,768]{1,0:T(8,128)(2,1)S(1)}, bf16[32,768]{1,0:T(8,128)(2,1)S(1)}, u32[]{:S(2)}, u32[]{:S(2)}) collective-permute-start(bf16[32,768]{1,0:T(8,128)(2,1)S(1)} %get-tuple-element.23.packed_ref), channel_id=1, source_target_pairs={{0,9},{1,8},{2,11},{3,10},{4,13},{5,12},{6,15},{7,14},{8,1},{9,0},... | collective-permute-start | bytes 147464 | tf_op jit(solution)/shard_map/ppermute | solution.py:230
  6.8 1.0 %collective-permute-start.1 = (bf16[32,768]{1,0:T(8,128)(2,1)S(1)}, bf16[32,768]{1,0:T(8,128)(2,1)S(1)}, u32[]{:S(2)}, u32[]{:S(2)}) collective-permute-start(bf16[32,768]{1,0:T(8,128)(2,1)S(1)} %get-tuple-element.23.packed_ref), channel_id=1, source_target_pairs={{0,5},{1,4},{2,7},{3,6},{4,1},{5,0},{6,3},{7,2},{8,13},{9,12},{10,... | collective-permute-start | bytes 147464 | tf_op jit(solution)/shard_map/ppermute | solution.py:230
  7.8 0.5 %collective-permute-start = (bf16[32,768]{1,0:T(8,128)(2,1)S(1)}, bf16[32,768]{1,0:T(8,128)(2,1)S(1)}, u32[]{:S(2)}, u32[]{:S(2)}) collective-permute-start(bf16[32,768]{1,0:T(8,128)(2,1)S(1)} %get-tuple-element.23.packed_ref), channel_id=1, source_target_pairs={{0,13},{1,12},{2,15},{3,14},{4,9},{5,8},{6,11},{7,10},{8,5},{9,4},... | collective-permute-start | bytes 147464 | tf_op jit(solution)/shard_map/ppermute | solution.py:230
  8.3 0.7 %own.1 = (bf16[64,768]{1,0:T(8,128)(2,1)S(1)}, f32[16,768]{1,0:T(8,128)S(1)}) custom-call(bf16[32,768]{1,0:T(8,128)(2,1)S(1)} %get-tuple-element.23.packed_ref), custom_call_target="tpu_custom_call" | custom-call | tf_op jit(solution)/shard_map/own/pallas_call | solution.py:247
  8.9 0.0 collective-permute-done.3
  9.0 0.2 meet.1
  9.2 0.0 collective-permute-done.2
  9.2 1.5 %collective-permute-done.1 = bf16[32,768]{1,0:T(8,128)(2,1)S(1)} collective-permute-done((bf16[32,768]{1,0:T(8,128)(2,1)S(1)}, bf16[32,768]{1,0:T(8,128)(2,1)S(1)}, u32[]{:S(2)}, u32[]{:S(2)}) %collective-permute-start.1) | collective-permute-done | bytes 49184 | tf_op jit(solution)/shard_map/ppermute | solution.py:230
  10.7 2.4 %collective-permute-done = bf16[32,768]{1,0:T(8,128)(2,1)S(1)} collective-permute-done((bf16[32,768]{1,0:T(8,128)(2,1)S(1)}, bf16[32,768]{1,0:T(8,128)(2,1)S(1)}, u32[]{:S(2)}, u32[]{:S(2)}) %collective-permute-start) | collective-permute-done | bytes 49184 | tf_op jit(solution)/shard_map/ppermute | solution.py:230
  13.1 0.7 %collective-permute-start.4 = (bf16[5,32,768]{2,1,0:T(8,128)(2,1)S(1)}, bf16[5,32,768]{2,1,0:T(8,128)(2,1)S(1)}, u32[]{:S(2)}, u32[]{:S(2)}) collective-permute-start(bf16[5,32,768]{2,1,0:T(8,128)(2,1)S(1)} %bitcast_dynamic-update-slice_fusion), channel_id=1, source_target_pairs={{0,1},{1,0},{2,3},{3,2},{4,5},{5,4},{6,7},{7,6},{8,9},{9,8},{10,11... | collective-permute-start | bytes 737288 | tf_op jit(solution)/shard_map/ppermute | solution.py:230
  13.9 1.3 %partner_near.1.before_ref = f32[16,768]{1,0:T(8,128)S(1)} custom-call(s32[8,2,16]{2,1,0:T(2,128)S(1)} %get-tuple-element.22.table_ref, bf16[64,768]{1,0:T(8,128)(2,1)S(1)} %get-tuple-element.32.side_ref, bf16[3,32,768]{2,1,0:T(8,128)(2,1)S(1)} %pad_maximum_fusion.1.blocks_ref), custom_call_target="tpu_custom_call" | custom-call | tf_op jit(solution)/shard_map/partner_near/pallas_call | solution.py:247
  15.2 0.0 collective-permute-done.4.blocks_ref
  15.2 1.8 %partner_core.1 = f32[16,768]{1,0:T(8,128)S(1)} custom-call(s32[8,2,16]{2,1,0:T(2,128)S(1)} %get-tuple-element.22.table_ref, bf16[64,768]{1,0:T(8,128)(2,1)S(1)} %get-tuple-element.32.side_ref, bf16[5,32,768]{2,1,0:T(8,128)(2,1)S(1)} %collective-permute-done.4.blocks_ref, f32[16,768]{1,0:T(8,128)S(1)} %partner_near.1.before_ref), custom_call_target="tpu_custom_call", output_to_operand_aliasing={{}: (3, {})} | custom-call | tf_op jit(solution)/shard_map/partner_core/pallas_call | solution.py:247
  17.0 0.0 collective-permute-start.5
  17.1 3.4 %add_own.1.refs_0_ = f32[16,768]{1,0:T(8,128)S(1)} custom-call(s32[8,2,16]{2,1,0:T(2,128)S(1)} %get-tuple-element.22.table_ref, bf16[64,768]{1,0:T(8,128)(2,1)S(1)} %get-tuple-element.24.side_ref, bf16[8,32,768]{2,1,0:T(8,128)(2,1)S(1)} %pad_maximum_fusion.blocks_ref, f32[16,768]{1,0:T(8,128)S(1)} %get-tuple-element.34.before_ref), custom_call_target="tpu_custom_call", output_to_operand_aliasing={{}: (3, {})} | custom-call | tf_op jit(solution)/shard_map/add_own/pallas_call | solution.py:247
  20.4 0.1 collective-permute-done.5.refs_1_
  20.5 0.4 %last.1 = (f32[16,768]{1,0:T(8,128)S(1)}, f32[16,8,128]{2,1,0:T(8,128)S(1)}) custom-call(bf16[16,768]{1,0:T(8,128)(2,1)S(1)} %get-tuple-element.20.vectors_ref, f32[1,768]{1,0:T(1,128)S(1)} %get-tuple-element.21.root_ref, f32[16,768]{1,0:T(8,128)S(1)} %add_own.1.refs_0_, f32[16,768]{1,0:T(8,128)S(1)} %collective-permute-done.5.refs_1_), custom_call_target="tpu_custom_call" | custom-call | tf_op jit(solution)/shard_map/last/pallas_call | solution.py:247
  20.9 10.4 %all_to_all.5.grams_ref = f32[16,8,128]{2,1,0:T(8,128)S(1)} all-to-all(f32[16,8,128]{2,1,0:T(8,128)S(1)} %get-tuple-element.36), channel_id=1, replica_groups=mesh['grp'=2,'row'=4,'col'=4] {'row','col'}, dimensions={0} | all-to-all | bytes 131072 | tf_op jit(solution)/shard_map/all_to_all | solution.py:355
  31.3 1.3 %finish.1 = (f32[16,768]{1,0:T(8,128)}, f32[16,16]{1,0:T(8,128)}) custom-call(f32[16,8,128]{2,1,0:T(8,128)S(1)} %all_to_all.5.grams_ref, f32[16,768]{1,0:T(8,128)S(1)} %get-tuple-element.37.applied_ref), custom_call_target="tpu_custom_call" | custom-call | tf_op jit(solution)/shard_map/finish/pallas_call | solution.py:247
  (7 shorter events, 0.1 us)
Async XLA Ops:
  1.4 7.5 %collective-permute-start.3 = (bf16[32,768]{1,0:T(8,128)(2,1)S(1)}, bf16[32,768]{1,0:T(8,128)(2,1)S(1)}, u32[]{:S(2)}, u32[]{:S(2)}) collective-permute-start(bf16[32,768]{1,0:T(8,128)(2,1)S(1)} %get-tuple-element.23.packed_ref), channel_id=1, source_target_pairs={{0,3},{1,2},{2,1},{3,0},{4,7},{5,6},{6,5},{7,4},{8,11},{9,10},{10,... | collective-permute-start | bytes 147464 | tf_op jit(solution)/shard_map/ppermute | solution.py:230
  3.9 5.3 %collective-permute-start.2 = (bf16[32,768]{1,0:T(8,128)(2,1)S(1)}, bf16[32,768]{1,0:T(8,128)(2,1)S(1)}, u32[]{:S(2)}, u32[]{:S(2)}) collective-permute-start(bf16[32,768]{1,0:T(8,128)(2,1)S(1)} %get-tuple-element.23.packed_ref), channel_id=1, source_target_pairs={{0,9},{1,8},{2,11},{3,10},{4,13},{5,12},{6,15},{7,14},{8,1},{9,0},... | collective-permute-start | bytes 147464 | tf_op jit(solution)/shard_map/ppermute | solution.py:230
  6.8 3.9 %collective-permute-start.1 = (bf16[32,768]{1,0:T(8,128)(2,1)S(1)}, bf16[32,768]{1,0:T(8,128)(2,1)S(1)}, u32[]{:S(2)}, u32[]{:S(2)}) collective-permute-start(bf16[32,768]{1,0:T(8,128)(2,1)S(1)} %get-tuple-element.23.packed_ref), channel_id=1, source_target_pairs={{0,5},{1,4},{2,7},{3,6},{4,1},{5,0},{6,3},{7,2},{8,13},{9,12},{10,... | collective-permute-start | bytes 147464 | tf_op jit(solution)/shard_map/ppermute | solution.py:230
  7.8 5.3 %collective-permute-start = (bf16[32,768]{1,0:T(8,128)(2,1)S(1)}, bf16[32,768]{1,0:T(8,128)(2,1)S(1)}, u32[]{:S(2)}, u32[]{:S(2)}) collective-permute-start(bf16[32,768]{1,0:T(8,128)(2,1)S(1)} %get-tuple-element.23.packed_ref), channel_id=1, source_target_pairs={{0,13},{1,12},{2,15},{3,14},{4,9},{5,8},{6,11},{7,10},{8,5},{9,4},... | collective-permute-start | bytes 147464 | tf_op jit(solution)/shard_map/ppermute | solution.py:230
  13.1 2.1 %collective-permute-start.4 = (bf16[5,32,768]{2,1,0:T(8,128)(2,1)S(1)}, bf16[5,32,768]{2,1,0:T(8,128)(2,1)S(1)}, u32[]{:S(2)}, u32[]{:S(2)}) collective-permute-start(bf16[5,32,768]{2,1,0:T(8,128)(2,1)S(1)} %bitcast_dynamic-update-slice_fusion), channel_id=1, source_target_pairs={{0,1},{1,0},{2,3},{3,2},{4,5},{5,4},{6,7},{7,6},{8,9},{9,8},{10,11... | collective-permute-start | bytes 737288 | tf_op jit(solution)/shard_map/ppermute | solution.py:230
  17.0 3.5 %collective-permute-start.5 = (f32[16,768]{1,0:T(8,128)S(1)}, f32[16,768]{1,0:T(8,128)S(1)}, u32[]{:S(2)}, u32[]{:S(2)}) collective-permute-start(f32[16,768]{1,0:T(8,128)S(1)} %partner_core.1), channel_id=1, source_target_pairs={{0,3},{1,2},{2,1},{3,0},{4,7},{5,6},{6,5},{7,4},{8,11},{9,10},{10,... | collective-permute-start | bytes 147464 | tf_op jit(solution)/shard_map/ppermute | solution.py:230

commit v2 on v1

--- a/solution.py
+++ b/solution.py
@@ -295,6 +295,21 @@
             **keywords,
         )
 
+    def add_part(name, target, places, side, blocks, part):
+        kernel = part_kernel if part is not None else first_kernel
+        before = [] if part is None else [part]
+        (part,) = call_blocks(
+            functools.partial(kernel, target),
+            name,
+            [image_type],
+            places,
+            side,
+            blocks,
+            *before,
+            input_output_aliases={3: 0} if before else {},
+        )
+        return part
+
     side_type = ((3 * ncv + 16, rows), jnp.bfloat16)
     side, image = call(own_kernel, "own", [side_type, image_type], packed)
     met, image = lax.optimization_barrier((met, image))
@@ -311,38 +326,25 @@
             input_output_aliases={3: 0},
         )
         sides.append(partner_side)
-    line, image = lax.optimization_barrier((line, image))
-    near = jnp.stack(line)
-    other = sent(jnp.stack(line + met + [packed]), core)
-    other_lines = beyond(lines, core)
-    parts = []
-    for hop, partner_side in zip(partners, sides):
-        (part,) = call_blocks(
-            functools.partial(first_kernel, hop), "partner_near", [image_type], lines, partner_side, near
-        )
-        (part,) = call_blocks(
-            functools.partial(part_kernel, hop),
-            "partner_core",
-            [image_type],
-            other_lines,
-            partner_side,
-            other,
-            part,
-            input_output_aliases={3: 0},
-        )
-        parts.append(part)
+    early, image = lax.optimization_barrier((line[1:], image))
+    held, held_at = early + met + [packed], lines[1:] + partners + [(0, 0)]
+    near = jnp.stack(held)
+    other = sent(near, core)
+    parts = [None for _ in partners]
+    for blocks, offsets in ((near, lines[1:]), (other, beyond(lines[1:], core))):
+        for k, hop in enumerate(partners):
+            parts[k] = add_part("partner", hop, offsets, sides[k], blocks, parts[k])
+    late, parts, image = lax.optimization_barrier((line[:1], parts, image))
+    late = jnp.stack(late)
+    other_late = sent(late, core)
+    for blocks, offsets in ((late, lines[:1]), (other_late, beyond(lines[:1], core))):
+        for k, hop in enumerate(partners):
+            parts[k] = add_part("partner_late", hop, offsets, sides[k], blocks, parts[k])
     parts, image = lax.optimization_barrier((parts, image))
     received = [sent(part, hop) for hop, part in zip(partners, parts)]
-    (image,) = call_blocks(
-        functools.partial(part_kernel, (0, 0)),
-        "add_own",
-        [image_type],
-        lines + beyond(lines + partners + [(0, 0)], core),
-        side,
-        jnp.concatenate([near, other]),
-        image,
-        input_output_aliases={3: 0},
-    )
+    own_places = lines[1:] + beyond(held_at, core) + lines[:1] + beyond(lines[:1], core)
+    blocks = jnp.concatenate([near[: n_row - 2], other, late, other_late])
+    image = add_part("add_own", (0, 0), own_places, side, blocks, image)
     applied, gram = call(
         last_kernel,
         "last",

time: 32.5 us -> 31.9 us (0.982)
  waiting for transfers between devices: 4.01 us -> 3.17 us
  starting transfers between devices: 7.57 us -> 7.22 us
    ppermute x6 -> x7, waiting for transfers between devices: 4.01 us -> 3.17 us  [sent(): return lax.ppermute(x, ('row', 'col'), pairs)]
    ppermute x6 -> x7, starting transfers between devices: 7.57 us -> 7.22 us  [sent(): return lax.ppermute(x, ('row', 'col'), pairs)]
    pallas_call x8 -> x10, Pallas kernels: 9.78 us -> 9.89 us  [call(): pl.pallas_call(kernel, out_shape=shapes, in_specs=[where] * len(args), ou...]
  transfers between devices with their start and end apart: 6 -> 7, of which waited for: 3 -> 3; matrix products, arithmetic and copies ran while one was open for 0% -> 0% of each run, Pallas kernels for 17% -> 21%
where the time goes in v2:
time: 31.9 us; the launch traced here: 31.8 us
  blocking collectives  10.7 us (34%)
  Pallas kernels  9.89 us (31%)
  starting transfers between devices  7.22 us (23%)
  waiting for transfers between devices  3.17 us (10%)
  between operations  0.7 us (2%)
    all_to_all x1, blocking collectives, per_device(): grams = lax.all_to_all(gram, ('row', 'col'), 0, 0)  10.7 us
    pallas_call x10, Pallas kernels, call(): pl.pallas_call(kernel, out_shape=shapes, in_specs=[where] * len(args), ou...  9.89 us
    ppermute x7, starting transfers between devices, sent(): return lax.ppermute(x, ('row', 'col'), pairs)  7.22 us
    ppermute x7, waiting for transfers between devices, sent(): return lax.ppermute(x, ('row', 'col'), pairs)  3.17 us
  transfers between devices with their start and end apart: 7, of which 3 were waited for; matrix products, arithmetic and copies ran while one was open for 0% of the time, Pallas kernels for 21%

profile of v2, /device:TPU:0, one launch (start us, length us, event | category | flops | bytes accessed | tf_op | source)
XLA Modules:
  0.0 31.8 jit_solution(12292106550857470885)
XLA Ops:
  0.6 0.8 %pack.1 = (bf16[32,768]{1,0:T(8,128)(2,1)S(1)}, bf16[16,768]{1,0:T(8,128)(2,1)S(1)}, f32[1,768]{1,0:T(1,128)S(1)}, s32[8,2,16]{2,1,0:T(2,128)S(1)}) custom-call(bf16[16,768]{1,0:T(8,128)(2,1)} %frames_ref.1, bf16[16,768]{1,0:T(8,128)(2,1)} %vectors_in.1, f32[768]{0:T(1024)} %degrees_ref.1, s32[8,2,16]{2,1,0:T(2,128)} %bitcast.16), custom_call_target="tpu_custom_call" | custom-call | tf_op jit(solution)/shard_map/pack/pallas_call | solution.py:247
  1.4 2.4 %collective-permute-start.2 = (bf16[32,768]{1,0:T(8,128)(2,1)S(1)}, bf16[32,768]{1,0:T(8,128)(2,1)S(1)}, u32[]{:S(2)}, u32[]{:S(2)}) collective-permute-start(bf16[32,768]{1,0:T(8,128)(2,1)S(1)} %get-tuple-element.25.packed_ref), channel_id=1, source_target_pairs={{0,3},{1,2},{2,1},{3,0},{4,7},{5,6},{6,5},{7,4},{8,11},{9,10},{10,... | collective-permute-start | bytes 147464 | tf_op jit(solution)/shard_map/ppermute | solution.py:230
  3.9 2.9 %collective-permute-start.1 = (bf16[32,768]{1,0:T(8,128)(2,1)S(1)}, bf16[32,768]{1,0:T(8,128)(2,1)S(1)}, u32[]{:S(2)}, u32[]{:S(2)}) collective-permute-start(bf16[32,768]{1,0:T(8,128)(2,1)S(1)} %get-tuple-element.25.packed_ref), channel_id=1, source_target_pairs={{0,9},{1,8},{2,11},{3,10},{4,13},{5,12},{6,15},{7,14},{8,1},{9,0},... | collective-permute-start | bytes 147464 | tf_op jit(solution)/shard_map/ppermute | solution.py:230
  6.8 1.0 %collective-permute-start = (bf16[32,768]{1,0:T(8,128)(2,1)S(1)}, bf16[32,768]{1,0:T(8,128)(2,1)S(1)}, u32[]{:S(2)}, u32[]{:S(2)}) collective-permute-start(bf16[32,768]{1,0:T(8,128)(2,1)S(1)} %get-tuple-element.25.packed_ref), channel_id=1, source_target_pairs={{0,5},{1,4},{2,7},{3,6},{4,1},{5,0},{6,3},{7,2},{8,13},{9,12},{10,... | collective-permute-start | bytes 147464 | tf_op jit(solution)/shard_map/ppermute | solution.py:230
  7.8 0.5 %collective-permute-start.4 = (bf16[32,768]{1,0:T(8,128)(2,1)S(1)}, bf16[32,768]{1,0:T(8,128)(2,1)S(1)}, u32[]{:S(2)}, u32[]{:S(2)}) collective-permute-start(bf16[32,768]{1,0:T(8,128)(2,1)S(1)} %get-tuple-element.25.packed_ref), channel_id=1, source_target_pairs={{0,13},{1,12},{2,15},{3,14},{4,9},{5,8},{6,11},{7,10},{8,5},{9,4},... | collective-permute-start | bytes 147464 | tf_op jit(solution)/shard_map/ppermute | solution.py:230
  8.3 0.7 %own.1 = (bf16[64,768]{1,0:T(8,128)(2,1)S(1)}, f32[16,768]{1,0:T(8,128)S(1)}) custom-call(bf16[32,768]{1,0:T(8,128)(2,1)S(1)} %get-tuple-element.25.packed_ref), custom_call_target="tpu_custom_call" | custom-call | tf_op jit(solution)/shard_map/own/pallas_call | solution.py:247
  8.9 0.0 collective-permute-done.2
  9.0 0.2 meet.1
  9.2 0.0 collective-permute-done.1
  9.2 1.5 %collective-permute-done = bf16[32,768]{1,0:T(8,128)(2,1)S(1)} collective-permute-done((bf16[32,768]{1,0:T(8,128)(2,1)S(1)}, bf16[32,768]{1,0:T(8,128)(2,1)S(1)}, u32[]{:S(2)}, u32[]{:S(2)}) %collective-permute-start) | collective-permute-done | bytes 49184 | tf_op jit(solution)/shard_map/ppermute | solution.py:230
  10.7 0.2 collective-permute-start.3
  10.9 1.3 %partner.2.before_ref = f32[16,768]{1,0:T(8,128)S(1)} custom-call(s32[8,2,16]{2,1,0:T(2,128)S(1)} %get-tuple-element.24.table_ref, bf16[64,768]{1,0:T(8,128)(2,1)S(1)} %get-tuple-element.33.side_ref, bf16[4,32,768]{2,1,0:T(8,128)(2,1)S(1)} %pad_maximum_fusion.blocks_ref), custom_call_target="tpu_custom_call" | custom-call | tf_op jit(solution)/shard_map/partner/pallas_call | solution.py:247
  12.2 0.0 collective-permute-done.3.blocks_ref
  12.2 1.3 %partner.3.before_ref = f32[16,768]{1,0:T(8,128)S(1)} custom-call(s32[8,2,16]{2,1,0:T(2,128)S(1)} %get-tuple-element.24.table_ref, bf16[64,768]{1,0:T(8,128)(2,1)S(1)} %get-tuple-element.33.side_ref, bf16[4,32,768]{2,1,0:T(8,128)(2,1)S(1)} %collective-permute-done.3.blocks_ref, f32[16,768]{1,0:T(8,128)S(1)} %partner.2.before_ref), custom_call_target="tpu_custom_call", output_to_operand_aliasing={{}: (3, {})} | custom-call | tf_op jit(solution)/shard_map/partner/pallas_call | solution.py:247
  13.6 0.0 collective-permute-done.4
  13.6 0.2 collective-permute-start.5
  13.8 0.2 partner_late.2.before_ref
  14.0 0.8 %collective-permute-done.5.blocks_ref = bf16[1,32,768]{2,1,0:T(8,128)(2,1)S(1)} collective-permute-done((bf16[1,32,768]{2,1,0:T(8,128)(2,1)S(1)}, bf16[1,32,768]{2,1,0:T(8,128)(2,1)S(1)}, u32[]{:S(2)}, u32[]{:S(2)}) %collective-permute-start.5) | collective-permute-done | bytes 49184 | tf_op jit(solution)/shard_map/ppermute | solution.py:230
  14.8 0.9 %partner_late.3 = f32[16,768]{1,0:T(8,128)S(1)} custom-call(s32[8,2,16]{2,1,0:T(2,128)S(1)} %get-tuple-element.24.table_ref, bf16[64,768]{1,0:T(8,128)(2,1)S(1)} %get-tuple-element.33.side_ref, bf16[1,32,768]{2,1,0:T(8,128)(2,1)S(1)} %collective-permute-done.5.blocks_ref, f32[16,768]{1,0:T(8,128)S(1)} %partner_late.2.before_ref), custom_call_target="tpu_custom_call", output_to_operand_aliasing={{}: (3, {})} | custom-call | tf_op jit(solution)/shard_map/partner_late/pallas_call | solution.py:247
  15.7 0.0 collective-permute-start.6
  15.7 2.9 %add_own.1.refs_0_ = f32[16,768]{1,0:T(8,128)S(1)} custom-call(s32[8,2,16]{2,1,0:T(2,128)S(1)} %get-tuple-element.24.table_ref, bf16[64,768]{1,0:T(8,128)(2,1)S(1)} %get-tuple-element.26.side_ref, bf16[8,32,768]{2,1,0:T(8,128)(2,1)S(1)} %constant_dynamic-update-slice_fusion.blocks_ref, ...), custom_call_target="tpu_custom_call", output_to_operand_aliasing={{}: (3, {})} | custom-call | tf_op jit(solution)/shard_map/add_own/pallas_call | solution.py:247
  18.6 0.8 %collective-permute-done.6.refs_1_ = f32[16,768]{1,0:T(8,128)S(1)} collective-permute-done((f32[16,768]{1,0:T(8,128)S(1)}, f32[16,768]{1,0:T(8,128)S(1)}, u32[]{:S(2)}, u32[]{:S(2)}) %collective-permute-start.6) | collective-permute-done | bytes 49184 | tf_op jit(solution)/shard_map/ppermute | solution.py:230
  19.4 0.4 %last.1 = (f32[16,768]{1,0:T(8,128)S(1)}, f32[16,8,128]{2,1,0:T(8,128)S(1)}) custom-call(bf16[16,768]{1,0:T(8,128)(2,1)S(1)} %get-tuple-element.22.vectors_ref, f32[1,768]{1,0:T(1,128)S(1)} %get-tuple-element.23.root_ref, f32[16,768]{1,0:T(8,128)S(1)} %add_own.1.refs_0_, f32[16,768]{1,0:T(8,128)S(1)} %collective-permute-done.6.refs_1_), custom_call_target="tpu_custom_call" | custom-call | tf_op jit(solution)/shard_map/last/pallas_call | solution.py:247
  19.8 10.7 %all_to_all.5.grams_ref = f32[16,8,128]{2,1,0:T(8,128)S(1)} all-to-all(f32[16,8,128]{2,1,0:T(8,128)S(1)} %get-tuple-element.40), channel_id=1, replica_groups=mesh['grp'=2,'row'=4,'col'=4] {'row','col'}, dimensions={0} | all-to-all | bytes 131072 | tf_op jit(solution)/shard_map/all_to_all | solution.py:357
  30.5 1.3 %finish.1 = (f32[16,768]{1,0:T(8,128)}, f32[16,16]{1,0:T(8,128)}) custom-call(f32[16,8,128]{2,1,0:T(8,128)S(1)} %all_to_all.5.grams_ref, f32[16,768]{1,0:T(8,128)S(1)} %get-tuple-element.41.applied_ref), custom_call_target="tpu_custom_call" | custom-call | tf_op jit(solution)/shard_map/finish/pallas_call | solution.py:247
  (6 shorter events, 0.1 us)
Async XLA Ops:
  1.4 7.5 %collective-permute-start.2 = (bf16[32,768]{1,0:T(8,128)(2,1)S(1)}, bf16[32,768]{1,0:T(8,128)(2,1)S(1)}, u32[]{:S(2)}, u32[]{:S(2)}) collective-permute-start(bf16[32,768]{1,0:T(8,128)(2,1)S(1)} %get-tuple-element.25.packed_ref), channel_id=1, source_target_pairs={{0,3},{1,2},{2,1},{3,0},{4,7},{5,6},{6,5},{7,4},{8,11},{9,10},{10,... | collective-permute-start | bytes 147464 | tf_op jit(solution)/shard_map/ppermute | solution.py:230
  3.9 5.3 %collective-permute-start.1 = (bf16[32,768]{1,0:T(8,128)(2,1)S(1)}, bf16[32,768]{1,0:T(8,128)(2,1)S(1)}, u32[]{:S(2)}, u32[]{:S(2)}) collective-permute-start(bf16[32,768]{1,0:T(8,128)(2,1)S(1)} %get-tuple-element.25.packed_ref), channel_id=1, source_target_pairs={{0,9},{1,8},{2,11},{3,10},{4,13},{5,12},{6,15},{7,14},{8,1},{9,0},... | collective-permute-start | bytes 147464 | tf_op jit(solution)/shard_map/ppermute | solution.py:230
  6.8 3.9 %collective-permute-start = (bf16[32,768]{1,0:T(8,128)(2,1)S(1)}, bf16[32,768]{1,0:T(8,128)(2,1)S(1)}, u32[]{:S(2)}, u32[]{:S(2)}) collective-permute-start(bf16[32,768]{1,0:T(8,128)(2,1)S(1)} %get-tuple-element.25.packed_ref), channel_id=1, source_target_pairs={{0,5},{1,4},{2,7},{3,6},{4,1},{5,0},{6,3},{7,2},{8,13},{9,12},{10,... | collective-permute-start | bytes 147464 | tf_op jit(solution)/shard_map/ppermute | solution.py:230
  7.8 5.8 %collective-permute-start.4 = (bf16[32,768]{1,0:T(8,128)(2,1)S(1)}, bf16[32,768]{1,0:T(8,128)(2,1)S(1)}, u32[]{:S(2)}, u32[]{:S(2)}) collective-permute-start(bf16[32,768]{1,0:T(8,128)(2,1)S(1)} %get-tuple-element.25.packed_ref), channel_id=1, source_target_pairs={{0,13},{1,12},{2,15},{3,14},{4,9},{5,8},{6,11},{7,10},{8,5},{9,4},... | collective-permute-start | bytes 147464 | tf_op jit(solution)/shard_map/ppermute | solution.py:230
  10.7 1.5 %collective-permute-start.3 = (bf16[4,32,768]{2,1,0:T(8,128)(2,1)S(1)}, bf16[4,32,768]{2,1,0:T(8,128)(2,1)S(1)}, u32[]{:S(2)}, u32[]{:S(2)}) collective-permute-start(bf16[4,32,768]{2,1,0:T(8,128)(2,1)S(1)} %pad_maximum_fusion.blocks_ref), channel_id=1, source_target_pairs={{0,1},{1,0},{2,3},{3,2},{4,5},{5,4},{6,7},{7,6},{8,9},{9,8},{10,11... | collective-permute-start | bytes 589832 | tf_op jit(solution)/shard_map/ppermute | solution.py:230
  13.6 1.2 %collective-permute-start.5 = (bf16[1,32,768]{2,1,0:T(8,128)(2,1)S(1)}, bf16[1,32,768]{2,1,0:T(8,128)(2,1)S(1)}, u32[]{:S(2)}, u32[]{:S(2)}) collective-permute-start(bf16[1,32,768]{2,1,0:T(8,128)(2,1)S(1)} %bitcast.12), channel_id=1, source_target_pairs={{0,1},{1,0},{2,3},{3,2},{4,5},{5,4},{6,7},{7,6},{8,9},{9,8},{10,11... | collective-permute-start | bytes 147464 | tf_op jit(solution)/shard_map/ppermute | solution.py:230
  15.7 3.8 %collective-permute-start.6 = (f32[16,768]{1,0:T(8,128)S(1)}, f32[16,768]{1,0:T(8,128)S(1)}, u32[]{:S(2)}, u32[]{:S(2)}) collective-permute-start(f32[16,768]{1,0:T(8,128)S(1)} %partner_late.3), channel_id=1, source_target_pairs={{0,3},{1,2},{2,1},{3,0},{4,7},{5,6},{6,5},{7,4},{8,11},{9,10},{10,... | collective-permute-start | bytes 147464 | tf_op jit(solution)/shard_map/ppermute | solution.py:230

commit v3 on v2

--- a/solution.py
+++ b/solution.py
@@ -129,12 +129,8 @@
         add_group(0, 1)
 
 
-def meet_kernel(
-    places, sizes, table_ref, side_ref, blocks_ref, before_ref, image_ref, partner_side_ref, list_ref
-):
-    partner_side_ref[...] = own_side(blocks_ref[0, : blocks_ref.shape[1] // 2, :])
-    image_ref[...] = before_ref[...]
-    add_blocks((0, 0), places, sizes, table_ref, side_ref, blocks_ref, image_ref, list_ref)
+def side_kernel(block_ref, side_ref):
+    side_ref[...] = own_side(block_ref[: block_ref.shape[0] // 2, :])
 
 
 def first_kernel(target, places, sizes, table_ref, side_ref, blocks_ref, image_ref, list_ref):
@@ -282,7 +278,7 @@
         lines = [(3, 1), (1, 1), (2, 1)]
     partners = [(0, c) for c in range(3, n_col, 2)]
     met = [sent(packed, hop) for hop in partners]
-    line = [sent(packed, hop) for hop in lines]
+    line = [sent(packed, hop) for hop in lines[1:]]
 
     def call_blocks(kernel, name, outs, places, *args, **keywords):
         return call(
@@ -312,21 +308,11 @@
 
     side_type = ((3 * ncv + 16, rows), jnp.bfloat16)
     side, image = call(own_kernel, "own", [side_type, image_type], packed)
+    ready, image = lax.optimization_barrier((packed, image))
+    line = [sent(ready, hop) for hop in lines[:1]] + line
     met, image = lax.optimization_barrier((met, image))
-    sides = []
-    for hop, block in zip(partners, met):
-        image, partner_side = call_blocks(
-            meet_kernel,
-            "meet",
-            [image_type, side_type],
-            [hop],
-            side,
-            block[None],
-            image,
-            input_output_aliases={3: 0},
-        )
-        sides.append(partner_side)
-    early, image = lax.optimization_barrier((line[1:], image))
+    sides = [call(side_kernel, "side", [side_type], block)[0] for block in met]
+    early, sides = lax.optimization_barrier((line[1:], sides))
     held, held_at = early + met + [packed], lines[1:] + partners + [(0, 0)]
     near = jnp.stack(held)
     other = sent(near, core)
@@ -342,8 +328,8 @@
             parts[k] = add_part("partner_late", hop, offsets, sides[k], blocks, parts[k])
     parts, image = lax.optimization_barrier((parts, image))
     received = [sent(part, hop) for hop, part in zip(partners, parts)]
-    own_places = lines[1:] + beyond(held_at, core) + lines[:1] + beyond(lines[:1], core)
-    blocks = jnp.concatenate([near[: n_row - 2], other, late, other_late])
+    own_places = held_at[:-1] + beyond(held_at, core) + lines[:1] + beyond(lines[:1], core)
+    blocks = jnp.concatenate([near[:-1], other, late, other_late])
     image = add_part("add_own", (0, 0), own_places, side, blocks, image)
     applied, gram = call(
         last_kernel,

time: 31.9 us -> 32.3 us (1.013)
  Pallas kernels: 9.89 us -> 9.05 us
  waiting for transfers between devices: 3.17 us -> 3.94 us
  starting transfers between devices: 7.22 us -> 7.7 us
    pallas_call x10, Pallas kernels: 9.89 us -> 9.05 us  [call(): pl.pallas_call(kernel, out_shape=shapes, in_specs=[where] * len(args), ou...]
    ppermute x7, waiting for transfers between devices: 3.17 us -> 3.94 us  [sent(): return lax.ppermute(x, ('row', 'col'), pairs)]
    ppermute x7, starting transfers between devices: 7.22 us -> 7.7 us  [sent(): return lax.ppermute(x, ('row', 'col'), pairs)]
  transfers between devices with their start and end apart: 7 -> 7, of which waited for: 3 -> 4; matrix products, arithmetic and copies ran while one was open for 0% -> 0% of each run, Pallas kernels for 21% -> 18%
where the time goes in v3:
time: 32.3 us; the launch traced here: 32.4 us
  blocking collectives  11 us (34%)
  Pallas kernels  9.05 us (28%)
  starting transfers between devices  7.7 us (24%)
  waiting for transfers between devices  3.94 us (12%)
  between operations  0.69 us (2%)
    all_to_all x1, blocking collectives, per_device(): grams = lax.all_to_all(gram, ('row', 'col'), 0, 0)  11 us
    pallas_call x10, Pallas kernels, call(): pl.pallas_call(kernel, out_shape=shapes, in_specs=[where] * len(args), ou...  9.05 us
    ppermute x7, starting transfers between devices, sent(): return lax.ppermute(x, ('row', 'col'), pairs)  7.7 us
    ppermute x7, waiting for transfers between devices, sent(): return lax.ppermute(x, ('row', 'col'), pairs)  3.94 us
  transfers between devices with their start and end apart: 7, of which 4 were waited for; matrix products, arithmetic and copies ran while one was open for 0% of the time, Pallas kernels for 18%

profile of v3, /device:TPU:0, one launch (start us, length us, event | category | flops | bytes accessed | tf_op | source)
XLA Modules:
  0.0 32.4 jit_solution(3224065307183806903)
XLA Ops:
  0.6 0.8 %pack.1 = (bf16[32,768]{1,0:T(8,128)(2,1)S(1)}, bf16[16,768]{1,0:T(8,128)(2,1)S(1)}, f32[1,768]{1,0:T(1,128)S(1)}, s32[8,2,16]{2,1,0:T(2,128)S(1)}) custom-call(bf16[16,768]{1,0:T(8,128)(2,1)} %frames_ref.1, bf16[16,768]{1,0:T(8,128)(2,1)} %vectors_in.1, f32[768]{0:T(1024)} %degrees_ref.1, s32[8,2,16]{2,1,0:T(2,128)} %bitcast.16), custom_call_target="tpu_custom_call" | custom-call | tf_op jit(solution)/shard_map/pack/pallas_call | solution.py:243
  1.4 2.4 %collective-permute-start.2 = (bf16[32,768]{1,0:T(8,128)(2,1)S(1)}, bf16[32,768]{1,0:T(8,128)(2,1)S(1)}, u32[]{:S(2)}, u32[]{:S(2)}) collective-permute-start(bf16[32,768]{1,0:T(8,128)(2,1)S(1)} %get-tuple-element.32.packed_ref), channel_id=1, source_target_pairs={{0,3},{1,2},{2,1},{3,0},{4,7},{5,6},{6,5},{7,4},{8,11},{9,10},{10,... | collective-permute-start | bytes 147464 | tf_op jit(solution)/shard_map/ppermute | solution.py:226
  3.9 2.9 %collective-permute-start.1 = (bf16[32,768]{1,0:T(8,128)(2,1)S(1)}, bf16[32,768]{1,0:T(8,128)(2,1)S(1)}, u32[]{:S(2)}, u32[]{:S(2)}) collective-permute-start(bf16[32,768]{1,0:T(8,128)(2,1)S(1)} %get-tuple-element.32.packed_ref), channel_id=1, source_target_pairs={{0,9},{1,8},{2,11},{3,10},{4,13},{5,12},{6,15},{7,14},{8,1},{9,0},... | collective-permute-start | bytes 147464 | tf_op jit(solution)/shard_map/ppermute | solution.py:226
  6.8 1.0 %collective-permute-start = (bf16[32,768]{1,0:T(8,128)(2,1)S(1)}, bf16[32,768]{1,0:T(8,128)(2,1)S(1)}, u32[]{:S(2)}, u32[]{:S(2)}) collective-permute-start(bf16[32,768]{1,0:T(8,128)(2,1)S(1)} %get-tuple-element.32.packed_ref), channel_id=1, source_target_pairs={{0,5},{1,4},{2,7},{3,6},{4,1},{5,0},{6,3},{7,2},{8,13},{9,12},{10,... | collective-permute-start | bytes 147464 | tf_op jit(solution)/shard_map/ppermute | solution.py:226
  7.8 0.7 %own.1 = (bf16[64,768]{1,0:T(8,128)(2,1)S(1)}, f32[16,768]{1,0:T(8,128)S(1)}) custom-call(bf16[32,768]{1,0:T(8,128)(2,1)S(1)} %get-tuple-element.32.packed_ref), custom_call_target="tpu_custom_call" | custom-call | tf_op jit(solution)/shard_map/own/pallas_call | solution.py:243
  8.4 0.5 %collective-permute-start.4 = (bf16[32,768]{1,0:T(8,128)(2,1)S(1)}, bf16[32,768]{1,0:T(8,128)(2,1)S(1)}, u32[]{:S(2)}, u32[]{:S(2)}) collective-permute-start(bf16[32,768]{1,0:T(8,128)(2,1)S(1)} %get-tuple-element.32.packed_ref), channel_id=1, source_target_pairs={{0,13},{1,12},{2,15},{3,14},{4,9},{5,8},{6,11},{7,10},{8,5},{9,4},... | collective-permute-start | bytes 147464 | tf_op jit(solution)/shard_map/ppermute | solution.py:226
  9.0 0.0 collective-permute-done.2.block_ref
  9.0 0.0 collective-permute-done.1
  9.0 1.7 %collective-permute-done = bf16[32,768]{1,0:T(8,128)(2,1)S(1)} collective-permute-done((bf16[32,768]{1,0:T(8,128)(2,1)S(1)}, bf16[32,768]{1,0:T(8,128)(2,1)S(1)}, u32[]{:S(2)}, u32[]{:S(2)}) %collective-permute-start) | collective-permute-done | bytes 49184 | tf_op jit(solution)/shard_map/ppermute | solution.py:226
  10.7 0.2 collective-permute-start.3
  10.9 0.9 %partner.2.before_ref = f32[16,768]{1,0:T(8,128)S(1)} custom-call(s32[8,2,16]{2,1,0:T(2,128)S(1)} %get-tuple-element.24.table_ref, bf16[64,768]{1,0:T(8,128)(2,1)S(1)} %side.1.side_ref, bf16[4,32,768]{2,1,0:T(8,128)(2,1)S(1)} %pad_maximum_fusion.blocks_ref), custom_call_target="tpu_custom_call" | custom-call | tf_op jit(solution)/shard_map/partner/pallas_call | solution.py:243
  11.8 0.4 %collective-permute-done.3.blocks_ref = bf16[4,32,768]{2,1,0:T(8,128)(2,1)S(1)} collective-permute-done((bf16[4,32,768]{2,1,0:T(8,128)(2,1)S(1)}, bf16[4,32,768]{2,1,0:T(8,128)(2,1)S(1)}, u32[]{:S(2)}, u32[]{:S(2)}) %collective-permute-start.3) | collective-permute-done | bytes 196640 | tf_op jit(solution)/shard_map/ppermute | solution.py:226
  12.2 0.9 %partner.3.before_ref = f32[16,768]{1,0:T(8,128)S(1)} custom-call(s32[8,2,16]{2,1,0:T(2,128)S(1)} %get-tuple-element.24.table_ref, bf16[64,768]{1,0:T(8,128)(2,1)S(1)} %side.1.side_ref, bf16[4,32,768]{2,1,0:T(8,128)(2,1)S(1)} %collective-permute-done.3.blocks_ref, f32[16,768]{1,0:T(8,128)S(1)} %partner.2.before_ref), custom_call_target="tpu_custom_call", output_to_operand_aliasing={{}: (3, {})} | custom-call | tf_op jit(solution)/shard_map/partner/pallas_call | solution.py:243
  13.1 0.6 %collective-permute-done.4 = bf16[32,768]{1,0:T(8,128)(2,1)S(1)} collective-permute-done((bf16[32,768]{1,0:T(8,128)(2,1)S(1)}, bf16[32,768]{1,0:T(8,128)(2,1)S(1)}, u32[]{:S(2)}, u32[]{:S(2)}) %collective-permute-start.4) | collective-permute-done | bytes 49184 | tf_op jit(solution)/shard_map/ppermute | solution.py:226
  13.8 0.7 %collective-permute-start.5 = (bf16[1,32,768]{2,1,0:T(8,128)(2,1)S(1)}, bf16[1,32,768]{2,1,0:T(8,128)(2,1)S(1)}, u32[]{:S(2)}, u32[]{:S(2)}) collective-permute-start(bf16[1,32,768]{2,1,0:T(8,128)(2,1)S(1)} %bitcast.12), channel_id=1, source_target_pairs={{0,1},{1,0},{2,3},{3,2},{4,5},{5,4},{6,7},{7,6},{8,9},{9,8},{10,11... | collective-permute-start | bytes 147464 | tf_op jit(solution)/shard_map/ppermute | solution.py:226
  14.5 0.9 %partner_late.2.before_ref = f32[16,768]{1,0:T(8,128)S(1)} custom-call(s32[8,2,16]{2,1,0:T(2,128)S(1)} %get-tuple-element.24.table_ref, bf16[64,768]{1,0:T(8,128)(2,1)S(1)} %side.1.side_ref, bf16[1,32,768]{2,1,0:T(8,128)(2,1)S(1)} %bitcast.13, f32[16,768]{1,0:T(8,128)S(1)} %partner.3.before_ref), custom_call_target="tpu_custom_call", output_to_operand_aliasing={{}: (3, {})} | custom-call | tf_op jit(solution)/shard_map/partner_late/pallas_call | solution.py:243
  15.3 0.0 collective-permute-done.5.blocks_ref
  15.3 0.9 %partner_late.3 = f32[16,768]{1,0:T(8,128)S(1)} custom-call(s32[8,2,16]{2,1,0:T(2,128)S(1)} %get-tuple-element.24.table_ref, bf16[64,768]{1,0:T(8,128)(2,1)S(1)} %side.1.side_ref, bf16[1,32,768]{2,1,0:T(8,128)(2,1)S(1)} %collective-permute-done.5.blocks_ref, f32[16,768]{1,0:T(8,128)S(1)} %partner_late.2.before_ref), custom_call_target="tpu_custom_call", output_to_operand_aliasing={{}: (3, {})} | custom-call | tf_op jit(solution)/shard_map/partner_late/pallas_call | solution.py:243
  16.2 0.0 collective-permute-start.6
  16.2 2.4 %add_own.1.refs_0_ = f32[16,768]{1,0:T(8,128)S(1)} custom-call(s32[8,2,16]{2,1,0:T(2,128)S(1)} %get-tuple-element.24.table_ref, bf16[64,768]{1,0:T(8,128)(2,1)S(1)} %get-tuple-element.26.side_ref, bf16[9,32,768]{2,1,0:T(8,128)(2,1)S(1)} %constant_dynamic-update-slice_fusion.blocks_ref, ...), custom_call_target="tpu_custom_call", output_to_operand_aliasing={{}: (3, {})} | custom-call | tf_op jit(solution)/shard_map/add_own/pallas_call | solution.py:243
  18.7 1.1 %collective-permute-done.6.refs_1_ = f32[16,768]{1,0:T(8,128)S(1)} collective-permute-done((f32[16,768]{1,0:T(8,128)S(1)}, f32[16,768]{1,0:T(8,128)S(1)}, u32[]{:S(2)}, u32[]{:S(2)}) %collective-permute-start.6) | collective-permute-done | bytes 49184 | tf_op jit(solution)/shard_map/ppermute | solution.py:226
  19.8 0.4 %last.1 = (f32[16,768]{1,0:T(8,128)S(1)}, f32[16,8,128]{2,1,0:T(8,128)S(1)}) custom-call(bf16[16,768]{1,0:T(8,128)(2,1)S(1)} %get-tuple-element.22.vectors_ref, f32[1,768]{1,0:T(1,128)S(1)} %get-tuple-element.23.root_ref, f32[16,768]{1,0:T(8,128)S(1)} %add_own.1.refs_0_, f32[16,768]{1,0:T(8,128)S(1)} %collective-permute-done.6.refs_1_), custom_call_target="tpu_custom_call" | custom-call | tf_op jit(solution)/shard_map/last/pallas_call | solution.py:243
  20.2 11.0 %all_to_all.5.grams_ref = f32[16,8,128]{2,1,0:T(8,128)S(1)} all-to-all(f32[16,8,128]{2,1,0:T(8,128)S(1)} %get-tuple-element.40), channel_id=1, replica_groups=mesh['grp'=2,'row'=4,'col'=4] {'row','col'}, dimensions={0} | all-to-all | bytes 131072 | tf_op jit(solution)/shard_map/all_to_all | solution.py:343
  31.2 1.3 %finish.1 = (f32[16,768]{1,0:T(8,128)}, f32[16,16]{1,0:T(8,128)}) custom-call(f32[16,8,128]{2,1,0:T(8,128)S(1)} %all_to_all.5.grams_ref, f32[16,768]{1,0:T(8,128)S(1)} %get-tuple-element.41.applied_ref), custom_call_target="tpu_custom_call" | custom-call | tf_op jit(solution)/shard_map/finish/pallas_call | solution.py:243
  (8 shorter events, 0.1 us)
Async XLA Ops:
  1.4 7.5 %collective-permute-start.2 = (bf16[32,768]{1,0:T(8,128)(2,1)S(1)}, bf16[32,768]{1,0:T(8,128)(2,1)S(1)}, u32[]{:S(2)}, u32[]{:S(2)}) collective-permute-start(bf16[32,768]{1,0:T(8,128)(2,1)S(1)} %get-tuple-element.32.packed_ref), channel_id=1, source_target_pairs={{0,3},{1,2},{2,1},{3,0},{4,7},{5,6},{6,5},{7,4},{8,11},{9,10},{10,... | collective-permute-start | bytes 147464 | tf_op jit(solution)/shard_map/ppermute | solution.py:226
  3.9 5.1 %collective-permute-start.1 = (bf16[32,768]{1,0:T(8,128)(2,1)S(1)}, bf16[32,768]{1,0:T(8,128)(2,1)S(1)}, u32[]{:S(2)}, u32[]{:S(2)}) collective-permute-start(bf16[32,768]{1,0:T(8,128)(2,1)S(1)} %get-tuple-element.32.packed_ref), channel_id=1, source_target_pairs={{0,9},{1,8},{2,11},{3,10},{4,13},{5,12},{6,15},{7,14},{8,1},{9,0},... | collective-permute-start | bytes 147464 | tf_op jit(solution)/shard_map/ppermute | solution.py:226
  6.8 3.9 %collective-permute-start = (bf16[32,768]{1,0:T(8,128)(2,1)S(1)}, bf16[32,768]{1,0:T(8,128)(2,1)S(1)}, u32[]{:S(2)}, u32[]{:S(2)}) collective-permute-start(bf16[32,768]{1,0:T(8,128)(2,1)S(1)} %get-tuple-element.32.packed_ref), channel_id=1, source_target_pairs={{0,5},{1,4},{2,7},{3,6},{4,1},{5,0},{6,3},{7,2},{8,13},{9,12},{10,... | collective-permute-start | bytes 147464 | tf_op jit(solution)/shard_map/ppermute | solution.py:226
  8.4 5.3 %collective-permute-start.4 = (bf16[32,768]{1,0:T(8,128)(2,1)S(1)}, bf16[32,768]{1,0:T(8,128)(2,1)S(1)}, u32[]{:S(2)}, u32[]{:S(2)}) collective-permute-start(bf16[32,768]{1,0:T(8,128)(2,1)S(1)} %get-tuple-element.32.packed_ref), channel_id=1, source_target_pairs={{0,13},{1,12},{2,15},{3,14},{4,9},{5,8},{6,11},{7,10},{8,5},{9,4},... | collective-permute-start | bytes 147464 | tf_op jit(solution)/shard_map/ppermute | solution.py:226
  10.7 1.5 %collective-permute-start.3 = (bf16[4,32,768]{2,1,0:T(8,128)(2,1)S(1)}, bf16[4,32,768]{2,1,0:T(8,128)(2,1)S(1)}, u32[]{:S(2)}, u32[]{:S(2)}) collective-permute-start(bf16[4,32,768]{2,1,0:T(8,128)(2,1)S(1)} %pad_maximum_fusion.blocks_ref), channel_id=1, source_target_pairs={{0,1},{1,0},{2,3},{3,2},{4,5},{5,4},{6,7},{7,6},{8,9},{9,8},{10,11... | collective-permute-start | bytes 589832 | tf_op jit(solution)/shard_map/ppermute | solution.py:226
  13.8 1.6 %collective-permute-start.5 = (bf16[1,32,768]{2,1,0:T(8,128)(2,1)S(1)}, bf16[1,32,768]{2,1,0:T(8,128)(2,1)S(1)}, u32[]{:S(2)}, u32[]{:S(2)}) collective-permute-start(bf16[1,32,768]{2,1,0:T(8,128)(2,1)S(1)} %bitcast.12), channel_id=1, source_target_pairs={{0,1},{1,0},{2,3},{3,2},{4,5},{5,4},{6,7},{7,6},{8,9},{9,8},{10,11... | collective-permute-start | bytes 147464 | tf_op jit(solution)/shard_map/ppermute | solution.py:226
  16.2 3.6 %collective-permute-start.6 = (f32[16,768]{1,0:T(8,128)S(1)}, f32[16,768]{1,0:T(8,128)S(1)}, u32[]{:S(2)}, u32[]{:S(2)}) collective-permute-start(f32[16,768]{1,0:T(8,128)S(1)} %partner_late.3), channel_id=1, source_target_pairs={{0,3},{1,2},{2,1},{3,0},{4,7},{5,6},{6,5},{7,4},{8,11},{9,10},{10,... | collective-permute-start | bytes 147464 | tf_op jit(solution)/shard_map/ppermute | solution.py:226

commit v4 on v3

--- a/solution.py
+++ b/solution.py
@@ -278,7 +278,7 @@
         lines = [(3, 1), (1, 1), (2, 1)]
     partners = [(0, c) for c in range(3, n_col, 2)]
     met = [sent(packed, hop) for hop in partners]
-    line = [sent(packed, hop) for hop in lines[1:]]
+    line = [sent(packed, hop) for hop in lines]
 
     def call_blocks(kernel, name, outs, places, *args, **keywords):
         return call(
@@ -308,11 +308,8 @@
 
     side_type = ((3 * ncv + 16, rows), jnp.bfloat16)
     side, image = call(own_kernel, "own", [side_type, image_type], packed)
-    ready, image = lax.optimization_barrier((packed, image))
-    line = [sent(ready, hop) for hop in lines[:1]] + line
-    met, image = lax.optimization_barrier((met, image))
+    met, early, image = lax.optimization_barrier((met, line[1:], image))
     sides = [call(side_kernel, "side", [side_type], block)[0] for block in met]
-    early, sides = lax.optimization_barrier((line[1:], sides))
     held, held_at = early + met + [packed], lines[1:] + partners + [(0, 0)]
     near = jnp.stack(held)
     other = sent(near, core)

time: 32.3 us -> 32.3 us (level)
  Pallas kernels: 9.05 us -> 7.48 us
  starting transfers between devices: 7.7 us -> 8.48 us
  blocking collectives: 11 us -> 11.5 us
    pallas_call x10, Pallas kernels: 9.05 us -> 7.48 us  [call(): pl.pallas_call(kernel, out_shape=shapes, in_specs=[where] * len(args), ou...]
    ppermute x7, starting transfers between devices: 7.7 us -> 8.48 us  [sent(): return lax.ppermute(x, ('row', 'col'), pairs)]
    all_to_all x1, blocking collectives: 11 us -> 11.5 us  [per_device(): grams = lax.all_to_all(gram, ('row', 'col'), 0, 0)]
  transfers between devices with their start and end apart: 7 -> 7, of which waited for: 4 -> 3; matrix products, arithmetic and copies ran while one was open for 0% -> 0% of each run, Pallas kernels for 18% -> 13%
where the time goes in v4:
time: 32.3 us; the launch traced here: 32.4 us
  blocking collectives  11.5 us (36%)
  starting transfers between devices  8.48 us (26%)
  Pallas kernels  7.48 us (23%)
  waiting for transfers between devices  4.16 us (13%)
  between operations  0.68 us (2%)
    all_to_all x1, blocking collectives, per_device(): grams = lax.all_to_all(gram, ('row', 'col'), 0, 0)  11.5 us
    ppermute x7, starting transfers between devices, sent(): return lax.ppermute(x, ('row', 'col'), pairs)  8.48 us
    pallas_call x10, Pallas kernels, call(): pl.pallas_call(kernel, out_shape=shapes, in_specs=[where] * len(args), ou...  7.48 us
    ppermute x7, waiting for transfers between devices, sent(): return lax.ppermute(x, ('row', 'col'), pairs)  4.16 us
  transfers between devices with their start and end apart: 7, of which 3 were waited for; matrix products, arithmetic and copies ran while one was open for 0% of the time, Pallas kernels for 13%

profile of v4, /device:TPU:0, one launch (start us, length us, event | category | flops | bytes accessed | tf_op | source)
XLA Modules:
  0.0 32.4 jit_solution(12157568183505647904)
XLA Ops:
  0.6 0.8 %pack.1 = (bf16[32,768]{1,0:T(8,128)(2,1)S(1)}, bf16[16,768]{1,0:T(8,128)(2,1)S(1)}, f32[1,768]{1,0:T(1,128)S(1)}, s32[8,2,16]{2,1,0:T(2,128)S(1)}) custom-call(bf16[16,768]{1,0:T(8,128)(2,1)} %frames_ref.1, bf16[16,768]{1,0:T(8,128)(2,1)} %vectors_in.1, f32[768]{0:T(1024)} %degrees_ref.1, s32[8,2,16]{2,1,0:T(2,128)} %bitcast.16), custom_call_target="tpu_custom_call" | custom-call | tf_op jit(solution)/shard_map/pack/pallas_call | solution.py:243
  1.4 3.5 %collective-permute-start.2 = (bf16[32,768]{1,0:T(8,128)(2,1)S(1)}, bf16[32,768]{1,0:T(8,128)(2,1)S(1)}, u32[]{:S(2)}, u32[]{:S(2)}) collective-permute-start(bf16[32,768]{1,0:T(8,128)(2,1)S(1)} %get-tuple-element.22.packed_ref), channel_id=1, source_target_pairs={{0,9},{1,8},{2,11},{3,10},{4,13},{5,12},{6,15},{7,14},{8,1},{9,0},... | collective-permute-start | bytes 147464 | tf_op jit(solution)/shard_map/ppermute | solution.py:226
  5.0 1.9 %collective-permute-start.1 = (bf16[32,768]{1,0:T(8,128)(2,1)S(1)}, bf16[32,768]{1,0:T(8,128)(2,1)S(1)}, u32[]{:S(2)}, u32[]{:S(2)}) collective-permute-start(bf16[32,768]{1,0:T(8,128)(2,1)S(1)} %get-tuple-element.22.packed_ref), channel_id=1, source_target_pairs={{0,5},{1,4},{2,7},{3,6},{4,1},{5,0},{6,3},{7,2},{8,13},{9,12},{10,... | collective-permute-start | bytes 147464 | tf_op jit(solution)/shard_map/ppermute | solution.py:226
  6.8 0.9 %collective-permute-start = (bf16[32,768]{1,0:T(8,128)(2,1)S(1)}, bf16[32,768]{1,0:T(8,128)(2,1)S(1)}, u32[]{:S(2)}, u32[]{:S(2)}) collective-permute-start(bf16[32,768]{1,0:T(8,128)(2,1)S(1)} %get-tuple-element.22.packed_ref), channel_id=1, source_target_pairs={{0,3},{1,2},{2,1},{3,0},{4,7},{5,6},{6,5},{7,4},{8,11},{9,10},{10,... | collective-permute-start | bytes 147464 | tf_op jit(solution)/shard_map/ppermute | solution.py:226
  7.8 0.5 %collective-permute-start.4 = (bf16[32,768]{1,0:T(8,128)(2,1)S(1)}, bf16[32,768]{1,0:T(8,128)(2,1)S(1)}, u32[]{:S(2)}, u32[]{:S(2)}) collective-permute-start(bf16[32,768]{1,0:T(8,128)(2,1)S(1)} %get-tuple-element.22.packed_ref), channel_id=1, source_target_pairs={{0,13},{1,12},{2,15},{3,14},{4,9},{5,8},{6,11},{7,10},{8,5},{9,4},... | collective-permute-start | bytes 147464 | tf_op jit(solution)/shard_map/ppermute | solution.py:226
  8.3 0.7 %own.1 = (bf16[64,768]{1,0:T(8,128)(2,1)S(1)}, f32[16,768]{1,0:T(8,128)S(1)}) custom-call(bf16[32,768]{1,0:T(8,128)(2,1)S(1)} %get-tuple-element.22.packed_ref), custom_call_target="tpu_custom_call" | custom-call | tf_op jit(solution)/shard_map/own/pallas_call | solution.py:243
  8.9 0.0 collective-permute-done.2
  8.9 0.0 collective-permute-done.1
  9.0 1.9 %collective-permute-done.block_ref = bf16[32,768]{1,0:T(8,128)(2,1)S(1)} collective-permute-done((bf16[32,768]{1,0:T(8,128)(2,1)S(1)}, bf16[32,768]{1,0:T(8,128)(2,1)S(1)}, u32[]{:S(2)}, u32[]{:S(2)}) %collective-permute-start) | collective-permute-done | bytes 49184 | tf_op jit(solution)/shard_map/ppermute | solution.py:226
  10.9 0.2 collective-permute-start.3
  11.1 0.9 %partner.2.before_ref = f32[16,768]{1,0:T(8,128)S(1)} custom-call(s32[8,2,16]{2,1,0:T(2,128)S(1)} %get-tuple-element.21.table_ref, bf16[64,768]{1,0:T(8,128)(2,1)S(1)} %side.1.side_ref, bf16[4,32,768]{2,1,0:T(8,128)(2,1)S(1)} %pad_maximum_fusion.blocks_ref), custom_call_target="tpu_custom_call" | custom-call | tf_op jit(solution)/shard_map/partner/pallas_call | solution.py:243
  12.0 0.4 %collective-permute-done.3.blocks_ref = bf16[4,32,768]{2,1,0:T(8,128)(2,1)S(1)} collective-permute-done((bf16[4,32,768]{2,1,0:T(8,128)(2,1)S(1)}, bf16[4,32,768]{2,1,0:T(8,128)(2,1)S(1)}, u32[]{:S(2)}, u32[]{:S(2)}) %collective-permute-start.3) | collective-permute-done | bytes 196640 | tf_op jit(solution)/shard_map/ppermute | solution.py:226
  12.4 0.9 %partner.3.before_ref = f32[16,768]{1,0:T(8,128)S(1)} custom-call(s32[8,2,16]{2,1,0:T(2,128)S(1)} %get-tuple-element.21.table_ref, bf16[64,768]{1,0:T(8,128)(2,1)S(1)} %side.1.side_ref, bf16[4,32,768]{2,1,0:T(8,128)(2,1)S(1)} %collective-permute-done.3.blocks_ref, f32[16,768]{1,0:T(8,128)S(1)} %partner.2.before_ref), custom_call_target="tpu_custom_call", output_to_operand_aliasing={{}: (3, {})} | custom-call | tf_op jit(solution)/shard_map/partner/pallas_call | solution.py:243
  13.3 0.0 collective-permute-done.4
  13.3 0.5 %collective-permute-start.5 = (bf16[1,32,768]{2,1,0:T(8,128)(2,1)S(1)}, bf16[1,32,768]{2,1,0:T(8,128)(2,1)S(1)}, u32[]{:S(2)}, u32[]{:S(2)}) collective-permute-start(bf16[1,32,768]{2,1,0:T(8,128)(2,1)S(1)} %bitcast.12), channel_id=1, source_target_pairs={{0,1},{1,0},{2,3},{3,2},{4,5},{5,4},{6,7},{7,6},{8,9},{9,8},{10,11... | collective-permute-start | bytes 147464 | tf_op jit(solution)/shard_map/ppermute | solution.py:226
  13.8 0.9 %partner_late.2.before_ref = f32[16,768]{1,0:T(8,128)S(1)} custom-call(s32[8,2,16]{2,1,0:T(2,128)S(1)} %get-tuple-element.21.table_ref, bf16[64,768]{1,0:T(8,128)(2,1)S(1)} %side.1.side_ref, bf16[1,32,768]{2,1,0:T(8,128)(2,1)S(1)} %bitcast.13, f32[16,768]{1,0:T(8,128)S(1)} %partner.3.before_ref), custom_call_target="tpu_custom_call", output_to_operand_aliasing={{}: (3, {})} | custom-call | tf_op jit(solution)/shard_map/partner_late/pallas_call | solution.py:243
  14.7 0.0 collective-permute-done.5.blocks_ref
  14.7 0.9 %partner_late.3 = f32[16,768]{1,0:T(8,128)S(1)} custom-call(s32[8,2,16]{2,1,0:T(2,128)S(1)} %get-tuple-element.21.table_ref, bf16[64,768]{1,0:T(8,128)(2,1)S(1)} %side.1.side_ref, bf16[1,32,768]{2,1,0:T(8,128)(2,1)S(1)} %collective-permute-done.5.blocks_ref, f32[16,768]{1,0:T(8,128)S(1)} %partner_late.2.before_ref), custom_call_target="tpu_custom_call", output_to_operand_aliasing={{}: (3, {})} | custom-call | tf_op jit(solution)/shard_map/partner_late/pallas_call | solution.py:243
  15.5 1.0 %collective-permute-start.6 = (f32[16,768]{1,0:T(8,128)S(1)}, f32[16,768]{1,0:T(8,128)S(1)}, u32[]{:S(2)}, u32[]{:S(2)}) collective-permute-start(f32[16,768]{1,0:T(8,128)S(1)} %partner_late.3), channel_id=1, source_target_pairs={{0,3},{1,2},{2,1},{3,0},{4,7},{5,6},{6,5},{7,4},{8,11},{9,10},{10,... | collective-permute-start | bytes 147464 | tf_op jit(solution)/shard_map/ppermute | solution.py:226
  16.5 0.9 %add_own.1.refs_0_ = f32[16,768]{1,0:T(8,128)S(1)} custom-call(s32[8,2,16]{2,1,0:T(2,128)S(1)} %get-tuple-element.21.table_ref, bf16[64,768]{1,0:T(8,128)(2,1)S(1)} %get-tuple-element.23.side_ref, bf16[9,32,768]{2,1,0:T(8,128)(2,1)S(1)} %constant_dynamic-update-slice_fusion.blocks_ref, ...), custom_call_target="tpu_custom_call", output_to_operand_aliasing={{}: (3, {})} | custom-call | tf_op jit(solution)/shard_map/add_own/pallas_call | solution.py:243
  17.4 1.9 %collective-permute-done.6.refs_1_ = f32[16,768]{1,0:T(8,128)S(1)} collective-permute-done((f32[16,768]{1,0:T(8,128)S(1)}, f32[16,768]{1,0:T(8,128)S(1)}, u32[]{:S(2)}, u32[]{:S(2)}) %collective-permute-start.6) | collective-permute-done | bytes 49184 | tf_op jit(solution)/shard_map/ppermute | solution.py:226
  19.2 0.4 %last.1 = (f32[16,768]{1,0:T(8,128)S(1)}, f32[16,8,128]{2,1,0:T(8,128)S(1)}) custom-call(bf16[16,768]{1,0:T(8,128)(2,1)S(1)} %get-tuple-element.19.vectors_ref, f32[1,768]{1,0:T(1,128)S(1)} %get-tuple-element.20.root_ref, f32[16,768]{1,0:T(8,128)S(1)} %add_own.1.refs_0_, f32[16,768]{1,0:T(8,128)S(1)} %collective-permute-done.6.refs_1_), custom_call_target="tpu_custom_call" | custom-call | tf_op jit(solution)/shard_map/last/pallas_call | solution.py:243
  19.6 11.5 %all_to_all.5.grams_ref = f32[16,8,128]{2,1,0:T(8,128)S(1)} all-to-all(f32[16,8,128]{2,1,0:T(8,128)S(1)} %get-tuple-element.34), channel_id=1, replica_groups=mesh['grp'=2,'row'=4,'col'=4] {'row','col'}, dimensions={0} | all-to-all | bytes 131072 | tf_op jit(solution)/shard_map/all_to_all | solution.py:340
  31.1 1.3 %finish.1 = (f32[16,768]{1,0:T(8,128)}, f32[16,16]{1,0:T(8,128)}) custom-call(f32[16,8,128]{2,1,0:T(8,128)S(1)} %all_to_all.5.grams_ref, f32[16,768]{1,0:T(8,128)S(1)} %get-tuple-element.35.applied_ref), custom_call_target="tpu_custom_call" | custom-call | tf_op jit(solution)/shard_map/finish/pallas_call | solution.py:243
  (8 shorter events, 0.1 us)
Async XLA Ops:
  1.4 7.5 %collective-permute-start.2 = (bf16[32,768]{1,0:T(8,128)(2,1)S(1)}, bf16[32,768]{1,0:T(8,128)(2,1)S(1)}, u32[]{:S(2)}, u32[]{:S(2)}) collective-permute-start(bf16[32,768]{1,0:T(8,128)(2,1)S(1)} %get-tuple-element.22.packed_ref), channel_id=1, source_target_pairs={{0,9},{1,8},{2,11},{3,10},{4,13},{5,12},{6,15},{7,14},{8,1},{9,0},... | collective-permute-start | bytes 147464 | tf_op jit(solution)/shard_map/ppermute | solution.py:226
  5.0 4.0 %collective-permute-start.1 = (bf16[32,768]{1,0:T(8,128)(2,1)S(1)}, bf16[32,768]{1,0:T(8,128)(2,1)S(1)}, u32[]{:S(2)}, u32[]{:S(2)}) collective-permute-start(bf16[32,768]{1,0:T(8,128)(2,1)S(1)} %get-tuple-element.22.packed_ref), channel_id=1, source_target_pairs={{0,5},{1,4},{2,7},{3,6},{4,1},{5,0},{6,3},{7,2},{8,13},{9,12},{10,... | collective-permute-start | bytes 147464 | tf_op jit(solution)/shard_map/ppermute | solution.py:226
  6.8 4.0 %collective-permute-start = (bf16[32,768]{1,0:T(8,128)(2,1)S(1)}, bf16[32,768]{1,0:T(8,128)(2,1)S(1)}, u32[]{:S(2)}, u32[]{:S(2)}) collective-permute-start(bf16[32,768]{1,0:T(8,128)(2,1)S(1)} %get-tuple-element.22.packed_ref), channel_id=1, source_target_pairs={{0,3},{1,2},{2,1},{3,0},{4,7},{5,6},{6,5},{7,4},{8,11},{9,10},{10,... | collective-permute-start | bytes 147464 | tf_op jit(solution)/shard_map/ppermute | solution.py:226
  7.8 5.5 %collective-permute-start.4 = (bf16[32,768]{1,0:T(8,128)(2,1)S(1)}, bf16[32,768]{1,0:T(8,128)(2,1)S(1)}, u32[]{:S(2)}, u32[]{:S(2)}) collective-permute-start(bf16[32,768]{1,0:T(8,128)(2,1)S(1)} %get-tuple-element.22.packed_ref), channel_id=1, source_target_pairs={{0,13},{1,12},{2,15},{3,14},{4,9},{5,8},{6,11},{7,10},{8,5},{9,4},... | collective-permute-start | bytes 147464 | tf_op jit(solution)/shard_map/ppermute | solution.py:226
  10.9 1.5 %collective-permute-start.3 = (bf16[4,32,768]{2,1,0:T(8,128)(2,1)S(1)}, bf16[4,32,768]{2,1,0:T(8,128)(2,1)S(1)}, u32[]{:S(2)}, u32[]{:S(2)}) collective-permute-start(bf16[4,32,768]{2,1,0:T(8,128)(2,1)S(1)} %pad_maximum_fusion.blocks_ref), channel_id=1, source_target_pairs={{0,1},{1,0},{2,3},{3,2},{4,5},{5,4},{6,7},{7,6},{8,9},{9,8},{10,11... | collective-permute-start | bytes 589832 | tf_op jit(solution)/shard_map/ppermute | solution.py:226
  13.3 1.4 %collective-permute-start.5 = (bf16[1,32,768]{2,1,0:T(8,128)(2,1)S(1)}, bf16[1,32,768]{2,1,0:T(8,128)(2,1)S(1)}, u32[]{:S(2)}, u32[]{:S(2)}) collective-permute-start(bf16[1,32,768]{2,1,0:T(8,128)(2,1)S(1)} %bitcast.12), channel_id=1, source_target_pairs={{0,1},{1,0},{2,3},{3,2},{4,5},{5,4},{6,7},{7,6},{8,9},{9,8},{10,11... | collective-permute-start | bytes 147464 | tf_op jit(solution)/shard_map/ppermute | solution.py:226
  15.5 3.7 %collective-permute-start.6 = (f32[16,768]{1,0:T(8,128)S(1)}, f32[16,768]{1,0:T(8,128)S(1)}, u32[]{:S(2)}, u32[]{:S(2)}) collective-permute-start(f32[16,768]{1,0:T(8,128)S(1)} %partner_late.3), channel_id=1, source_target_pairs={{0,3},{1,2},{2,1},{3,0},{4,7},{5,6},{6,5},{7,4},{8,11},{9,10},{10,... | collective-permute-start | bytes 147464 | tf_op jit(solution)/shard_map/ppermute | solution.py:226

commit v5 on v4

--- a/solution.py
+++ b/solution.py
@@ -200,7 +200,7 @@
     return result[:, :n], result[:, half : half + n]
 
 
-def finish_kernel(total_frames, grams_ref, applied_ref, basis_ref, ritz_ref):
+def finish_kernel(total_frames, grams_ref, applied_ref, basis_out, ritz_out, basis_ref, ritz_ref, sems):
     tile = grams_ref[0]
     for device in range(1, grams_ref.shape[0]):
         tile += grams_ref[device]
@@ -212,8 +212,16 @@
     plain = (((1,), (0,)), ((), ()))
     image_inverse, vector_inverse = inverse_factors([gram[:, :n], gram[:, 2 * n : 3 * n]])
     basis_ref[...] = exact(image_inverse * math.sqrt(total_frames), applied_ref[...], plain)
+    copies = [
+        pltpu.make_async_copy(basis_ref, basis_out, sems.at[0]),
+        pltpu.make_async_copy(ritz_ref, ritz_out, sems.at[1]),
+    ]
+    copies[0].start()
     half = exact(vector_inverse, gram[:, n : 2 * n], plain)
     ritz_ref[...] = exact(half, vector_inverse, NT)
+    copies[1].start()
+    for copy in copies:
+        copy.wait()
 
 
 def sent(x, hop):
@@ -238,13 +246,13 @@
     sizes = (n_row, n_col)
     vmem = pl.BlockSpec(memory_space=pltpu.VMEM)
 
-    def call(kernel, name, outs, *args, limit=24, where=vmem, **keywords):
+    def call(kernel, name, outs, *args, limit=24, where=vmem, to=vmem, **keywords):
         shapes = [jax.ShapeDtypeStruct(*out) for out in outs]
         return pl.pallas_call(
             kernel,
             out_shape=shapes,
             in_specs=[where] * len(args),
-            out_specs=[vmem] * len(outs),
+            out_specs=[to] * len(outs),
             compiler_params=pltpu.CompilerParams(vmem_limit_bytes=limit * MIB),
             name=name,
             **keywords,
@@ -308,8 +316,9 @@
 
     side_type = ((3 * ncv + 16, rows), jnp.bfloat16)
     side, image = call(own_kernel, "own", [side_type, image_type], packed)
-    met, early, image = lax.optimization_barrier((met, line[1:], image))
+    met, image = lax.optimization_barrier((met, image))
     sides = [call(side_kernel, "side", [side_type], block)[0] for block in met]
+    early, sides = lax.optimization_barrier((line[1:], sides))
     held, held_at = early + met + [packed], lines[1:] + partners + [(0, 0)]
     near = jnp.stack(held)
     other = sent(near, core)
@@ -320,13 +329,19 @@
     late, parts, image = lax.optimization_barrier((line[:1], parts, image))
     late = jnp.stack(late)
     other_late = sent(late, core)
-    for blocks, offsets in ((late, lines[:1]), (other_late, beyond(lines[:1], core))):
-        for k, hop in enumerate(partners):
-            parts[k] = add_part("partner_late", hop, offsets, sides[k], blocks, parts[k])
+    for k, hop in enumerate(partners):
+        parts[k] = add_part("partner_late", hop, lines[:1], sides[k], late, parts[k])
+    parts, image = lax.optimization_barrier((parts, image))
+    image = add_part("add_met", (0, 0), partners, side, jnp.stack(met), image)
+    other_late, parts, image = lax.optimization_barrier((other_late, parts, image))
+    for k, hop in enumerate(partners):
+        parts[k] = add_part(
+            "partner_late", hop, beyond(lines[:1], core), sides[k], other_late, parts[k]
+        )
     parts, image = lax.optimization_barrier((parts, image))
     received = [sent(part, hop) for hop, part in zip(partners, parts)]
-    own_places = held_at[:-1] + beyond(held_at, core) + lines[:1] + beyond(lines[:1], core)
-    blocks = jnp.concatenate([near[:-1], other, late, other_late])
+    own_places = lines[1:] + beyond(held_at, core) + lines[:1] + beyond(lines[:1], core)
+    blocks = jnp.concatenate([near[: n_row - 2], other, late, other_late])
     image = add_part("add_own", (0, 0), own_places, side, blocks, image)
     applied, gram = call(
         last_kernel,
@@ -344,6 +359,12 @@
         [((nvec, rows), jnp.float32), ((nvec, nvec), jnp.float32)],
         grams,
         applied,
+        to=pl.BlockSpec(memory_space=pltpu.HBM),
+        scratch_shapes=[
+            pltpu.VMEM((nvec, rows), jnp.float32),
+            pltpu.VMEM((nvec, nvec), jnp.float32),
+            pltpu.SemaphoreType.DMA((2,)),
+        ],
     )
     return (basis, ritz)
 

time: 32.3 us -> 31.9 us (0.988); the launches traced: 32.4 us -> 31.4 us
  Pallas kernels: 7.48 us -> 10.4 us
  blocking collectives: 11.5 us -> 9.66 us
  waiting for transfers between devices: 4.16 us -> 2.94 us
  starting transfers between devices: 8.48 us -> 7.66 us
    pallas_call x10 -> x11, Pallas kernels: 7.48 us -> 10.4 us  [call(): pl.pallas_call(kernel, out_shape=shapes, in_specs=[where] * len(args), ou...]
    all_to_all x1, blocking collectives: 11.5 us -> 9.66 us  [per_device(): grams = lax.all_to_all(gram, ('row', 'col'), 0, 0)]
    ppermute x7, waiting for transfers between devices: 4.16 us -> 2.94 us  [sent(): return lax.ppermute(x, ('row', 'col'), pairs)]
    ppermute x7, starting transfers between devices: 8.48 us -> 7.66 us  [sent(): return lax.ppermute(x, ('row', 'col'), pairs)]
  transfers between devices with their start and end apart: 7 -> 7, of which waited for: 3 -> 3; matrix products, arithmetic and copies ran while one was open for 0% -> 0% of each run, Pallas kernels for 13% -> 22%
where the time goes in v5:
time: 31.9 us; the launch traced here: 31.4 us
  Pallas kernels  10.4 us (33%)
  blocking collectives  9.66 us (30%)
  starting transfers between devices  7.66 us (24%)
  waiting for transfers between devices  2.94 us (9%)
  between operations  0.69 us (2%)
    pallas_call x11, Pallas kernels, call(): pl.pallas_call(kernel, out_shape=shapes, in_specs=[where] * len(args), ou...  10.4 us
    all_to_all x1, blocking collectives, per_device(): grams = lax.all_to_all(gram, ('row', 'col'), 0, 0)  9.66 us
    ppermute x7, starting transfers between devices, sent(): return lax.ppermute(x, ('row', 'col'), pairs)  7.66 us
    ppermute x7, waiting for transfers between devices, sent(): return lax.ppermute(x, ('row', 'col'), pairs)  2.94 us
  transfers between devices with their start and end apart: 7, of which 3 were waited for; matrix products, arithmetic and copies ran while one was open for 0% of the time, Pallas kernels for 22%

profile of v5, /device:TPU:0, one launch (start us, length us, event | category | flops | bytes accessed | tf_op | source)
XLA Modules:
  0.0 31.4 jit_solution(10351908983722097259)
XLA Ops:
  0.6 0.8 %pack.1 = (bf16[32,768]{1,0:T(8,128)(2,1)S(1)}, bf16[16,768]{1,0:T(8,128)(2,1)S(1)}, f32[1,768]{1,0:T(1,128)S(1)}, s32[8,2,16]{2,1,0:T(2,128)S(1)}) custom-call(bf16[16,768]{1,0:T(8,128)(2,1)} %frames_ref.1, bf16[16,768]{1,0:T(8,128)(2,1)} %vectors_in.1, f32[768]{0:T(1024)} %degrees_ref.1, s32[8,2,16]{2,1,0:T(2,128)} %bitcast.16), custom_call_target="tpu_custom_call" | custom-call | tf_op jit(solution)/shard_map/pack/pallas_call | solution.py:251
  1.4 2.4 %collective-permute-start.2 = (bf16[32,768]{1,0:T(8,128)(2,1)S(1)}, bf16[32,768]{1,0:T(8,128)(2,1)S(1)}, u32[]{:S(2)}, u32[]{:S(2)}) collective-permute-start(bf16[32,768]{1,0:T(8,128)(2,1)S(1)} %get-tuple-element.28.packed_ref), channel_id=1, source_target_pairs={{0,3},{1,2},{2,1},{3,0},{4,7},{5,6},{6,5},{7,4},{8,11},{9,10},{10,... | collective-permute-start | bytes 147464 | tf_op jit(solution)/shard_map/ppermute | solution.py:234
  3.9 2.9 %collective-permute-start.1 = (bf16[32,768]{1,0:T(8,128)(2,1)S(1)}, bf16[32,768]{1,0:T(8,128)(2,1)S(1)}, u32[]{:S(2)}, u32[]{:S(2)}) collective-permute-start(bf16[32,768]{1,0:T(8,128)(2,1)S(1)} %get-tuple-element.28.packed_ref), channel_id=1, source_target_pairs={{0,9},{1,8},{2,11},{3,10},{4,13},{5,12},{6,15},{7,14},{8,1},{9,0},... | collective-permute-start | bytes 147464 | tf_op jit(solution)/shard_map/ppermute | solution.py:234
  6.8 1.0 %collective-permute-start = (bf16[32,768]{1,0:T(8,128)(2,1)S(1)}, bf16[32,768]{1,0:T(8,128)(2,1)S(1)}, u32[]{:S(2)}, u32[]{:S(2)}) collective-permute-start(bf16[32,768]{1,0:T(8,128)(2,1)S(1)} %get-tuple-element.28.packed_ref), channel_id=1, source_target_pairs={{0,5},{1,4},{2,7},{3,6},{4,1},{5,0},{6,3},{7,2},{8,13},{9,12},{10,... | collective-permute-start | bytes 147464 | tf_op jit(solution)/shard_map/ppermute | solution.py:234
  7.8 0.5 %collective-permute-start.4 = (bf16[32,768]{1,0:T(8,128)(2,1)S(1)}, bf16[32,768]{1,0:T(8,128)(2,1)S(1)}, u32[]{:S(2)}, u32[]{:S(2)}) collective-permute-start(bf16[32,768]{1,0:T(8,128)(2,1)S(1)} %get-tuple-element.28.packed_ref), channel_id=1, source_target_pairs={{0,13},{1,12},{2,15},{3,14},{4,9},{5,8},{6,11},{7,10},{8,5},{9,4},... | collective-permute-start | bytes 147464 | tf_op jit(solution)/shard_map/ppermute | solution.py:234
  8.3 0.7 %own.1 = (bf16[64,768]{1,0:T(8,128)(2,1)S(1)}, f32[16,768]{1,0:T(8,128)S(1)}) custom-call(bf16[32,768]{1,0:T(8,128)(2,1)S(1)} %get-tuple-element.28.packed_ref), custom_call_target="tpu_custom_call" | custom-call | tf_op jit(solution)/shard_map/own/pallas_call | solution.py:251
  8.9 0.0 collective-permute-done.2.block_ref
  9.0 0.0 collective-permute-done.1
  9.0 1.7 %collective-permute-done = bf16[32,768]{1,0:T(8,128)(2,1)S(1)} collective-permute-done((bf16[32,768]{1,0:T(8,128)(2,1)S(1)}, bf16[32,768]{1,0:T(8,128)(2,1)S(1)}, u32[]{:S(2)}, u32[]{:S(2)}) %collective-permute-start) | collective-permute-done | bytes 49184 | tf_op jit(solution)/shard_map/ppermute | solution.py:234
  10.7 0.2 collective-permute-start.3
  10.9 0.9 %partner.2.before_ref = f32[16,768]{1,0:T(8,128)S(1)} custom-call(s32[8,2,16]{2,1,0:T(2,128)S(1)} %get-tuple-element.27.table_ref, bf16[64,768]{1,0:T(8,128)(2,1)S(1)} %side.1.side_ref, bf16[4,32,768]{2,1,0:T(8,128)(2,1)S(1)} %pad_maximum_fusion.blocks_ref), custom_call_target="tpu_custom_call" | custom-call | tf_op jit(solution)/shard_map/partner/pallas_call | solution.py:251
  11.8 0.5 %collective-permute-done.3.blocks_ref = bf16[4,32,768]{2,1,0:T(8,128)(2,1)S(1)} collective-permute-done((bf16[4,32,768]{2,1,0:T(8,128)(2,1)S(1)}, bf16[4,32,768]{2,1,0:T(8,128)(2,1)S(1)}, u32[]{:S(2)}, u32[]{:S(2)}) %collective-permute-start.3) | collective-permute-done | bytes 196640 | tf_op jit(solution)/shard_map/ppermute | solution.py:234
  12.2 0.9 %partner.3.before_ref = f32[16,768]{1,0:T(8,128)S(1)} custom-call(s32[8,2,16]{2,1,0:T(2,128)S(1)} %get-tuple-element.27.table_ref, bf16[64,768]{1,0:T(8,128)(2,1)S(1)} %side.1.side_ref, bf16[4,32,768]{2,1,0:T(8,128)(2,1)S(1)} %collective-permute-done.3.blocks_ref, f32[16,768]{1,0:T(8,128)S(1)} %partner.2.before_ref), custom_call_target="tpu_custom_call", output_to_operand_aliasing={{}: (3, {})} | custom-call | tf_op jit(solution)/shard_map/partner/pallas_call | solution.py:251
  13.1 0.0 collective-permute-done.4
  13.1 0.7 %collective-permute-start.5 = (bf16[1,32,768]{2,1,0:T(8,128)(2,1)S(1)}, bf16[1,32,768]{2,1,0:T(8,128)(2,1)S(1)}, u32[]{:S(2)}, u32[]{:S(2)}) collective-permute-start(bf16[1,32,768]{2,1,0:T(8,128)(2,1)S(1)} %bitcast.12), channel_id=1, source_target_pairs={{0,1},{1,0},{2,3},{3,2},{4,5},{5,4},{6,7},{7,6},{8,9},{9,8},{10,11... | collective-permute-start | bytes 147464 | tf_op jit(solution)/shard_map/ppermute | solution.py:234
  13.8 0.9 %partner_late.2.before_ref = f32[16,768]{1,0:T(8,128)S(1)} custom-call(s32[8,2,16]{2,1,0:T(2,128)S(1)} %get-tuple-element.27.table_ref, bf16[64,768]{1,0:T(8,128)(2,1)S(1)} %side.1.side_ref, bf16[1,32,768]{2,1,0:T(8,128)(2,1)S(1)} %bitcast.13, f32[16,768]{1,0:T(8,128)S(1)} %partner.3.before_ref), custom_call_target="tpu_custom_call", output_to_operand_aliasing={{}: (3, {})} | custom-call | tf_op jit(solution)/shard_map/partner_late/pallas_call | solution.py:251
  14.7 0.9 %add_met.1.before_ref = f32[16,768]{1,0:T(8,128)S(1)} custom-call(s32[8,2,16]{2,1,0:T(2,128)S(1)} %get-tuple-element.27.table_ref, bf16[64,768]{1,0:T(8,128)(2,1)S(1)} %get-tuple-element.29.side_ref, bf16[1,32,768]{2,1,0:T(8,128)(2,1)S(1)} %bitcast.10, f32[16,768]{1,0:T(8,128)S(1)} %get-tuple-element.40.before_ref), custom_call_target="tpu_custom_call", output_to_operand_aliasing={{}: (3, {})} | custom-call | tf_op jit(solution)/shard_map/add_met/pallas_call | solution.py:251
  15.5 0.0 collective-permute-done.5.blocks_ref
  15.5 0.9 %partner_late.3 = f32[16,768]{1,0:T(8,128)S(1)} custom-call(s32[8,2,16]{2,1,0:T(2,128)S(1)} %get-tuple-element.27.table_ref, bf16[64,768]{1,0:T(8,128)(2,1)S(1)} %side.1.side_ref, bf16[1,32,768]{2,1,0:T(8,128)(2,1)S(1)} %collective-permute-done.5.blocks_ref, f32[16,768]{1,0:T(8,128)S(1)} %partner_late.2.before_ref), custom_call_target="tpu_custom_call", output_to_operand_aliasing={{}: (3, {})} | custom-call | tf_op jit(solution)/shard_map/partner_late/pallas_call | solution.py:251
  16.4 0.0 collective-permute-start.6
  16.4 2.9 %add_own.1.refs_0_ = f32[16,768]{1,0:T(8,128)S(1)} custom-call(s32[8,2,16]{2,1,0:T(2,128)S(1)} %get-tuple-element.27.table_ref, bf16[64,768]{1,0:T(8,128)(2,1)S(1)} %get-tuple-element.29.side_ref, bf16[8,32,768]{2,1,0:T(8,128)(2,1)S(1)} %constant_dynamic-update-slice_fusion.blocks_ref, f32[16,768]{1,0:T(8,128)S(1)} %add_met.1.before_ref), custom_call_target="tpu_custom_call", output_to_operand_aliasing={{}: (3, {})} | custom-call | tf_op jit(solution)/shard_map/add_own/pallas_call | solution.py:251
  19.3 0.8 %collective-permute-done.6.refs_1_ = f32[16,768]{1,0:T(8,128)S(1)} collective-permute-done((f32[16,768]{1,0:T(8,128)S(1)}, f32[16,768]{1,0:T(8,128)S(1)}, u32[]{:S(2)}, u32[]{:S(2)}) %collective-permute-start.6) | collective-permute-done | bytes 49184 | tf_op jit(solution)/shard_map/ppermute | solution.py:234
  20.1 0.4 %last.1 = (f32[16,768]{1,0:T(8,128)S(1)}, f32[16,8,128]{2,1,0:T(8,128)S(1)}) custom-call(bf16[16,768]{1,0:T(8,128)(2,1)S(1)} %get-tuple-element.25.vectors_ref, f32[1,768]{1,0:T(1,128)S(1)} %get-tuple-element.26.root_ref, f32[16,768]{1,0:T(8,128)S(1)} %add_own.1.refs_0_, f32[16,768]{1,0:T(8,128)S(1)} %collective-permute-done.6.refs_1_), custom_call_target="tpu_custom_call" | custom-call | tf_op jit(solution)/shard_map/last/pallas_call | solution.py:251
  20.4 9.7 %all_to_all.5.grams_ref = f32[16,8,128]{2,1,0:T(8,128)S(1)} all-to-all(f32[16,8,128]{2,1,0:T(8,128)S(1)} %get-tuple-element.46), channel_id=1, replica_groups=mesh['grp'=2,'row'=4,'col'=4] {'row','col'}, dimensions={0} | all-to-all | bytes 131072 | tf_op jit(solution)/shard_map/all_to_all | solution.py:355
  30.1 1.3 %finish.1 = (f32[16,768]{1,0:T(8,128)}, f32[16,16]{1,0:T(8,128)}) custom-call(f32[16,8,128]{2,1,0:T(8,128)S(1)} %all_to_all.5.grams_ref, f32[16,768]{1,0:T(8,128)S(1)} %get-tuple-element.47.applied_ref), custom_call_target="tpu_custom_call" | custom-call | tf_op jit(solution)/shard_map/finish/pallas_call | solution.py:251
  (7 shorter events, 0.1 us)
Async XLA Ops:
  1.4 7.5 %collective-permute-start.2 = (bf16[32,768]{1,0:T(8,128)(2,1)S(1)}, bf16[32,768]{1,0:T(8,128)(2,1)S(1)}, u32[]{:S(2)}, u32[]{:S(2)}) collective-permute-start(bf16[32,768]{1,0:T(8,128)(2,1)S(1)} %get-tuple-element.28.packed_ref), channel_id=1, source_target_pairs={{0,3},{1,2},{2,1},{3,0},{4,7},{5,6},{6,5},{7,4},{8,11},{9,10},{10,... | collective-permute-start | bytes 147464 | tf_op jit(solution)/shard_map/ppermute | solution.py:234
  3.9 5.1 %collective-permute-start.1 = (bf16[32,768]{1,0:T(8,128)(2,1)S(1)}, bf16[32,768]{1,0:T(8,128)(2,1)S(1)}, u32[]{:S(2)}, u32[]{:S(2)}) collective-permute-start(bf16[32,768]{1,0:T(8,128)(2,1)S(1)} %get-tuple-element.28.packed_ref), channel_id=1, source_target_pairs={{0,9},{1,8},{2,11},{3,10},{4,13},{5,12},{6,15},{7,14},{8,1},{9,0},... | collective-permute-start | bytes 147464 | tf_op jit(solution)/shard_map/ppermute | solution.py:234
  6.8 3.9 %collective-permute-start = (bf16[32,768]{1,0:T(8,128)(2,1)S(1)}, bf16[32,768]{1,0:T(8,128)(2,1)S(1)}, u32[]{:S(2)}, u32[]{:S(2)}) collective-permute-start(bf16[32,768]{1,0:T(8,128)(2,1)S(1)} %get-tuple-element.28.packed_ref), channel_id=1, source_target_pairs={{0,5},{1,4},{2,7},{3,6},{4,1},{5,0},{6,3},{7,2},{8,13},{9,12},{10,... | collective-permute-start | bytes 147464 | tf_op jit(solution)/shard_map/ppermute | solution.py:234
  7.8 5.3 %collective-permute-start.4 = (bf16[32,768]{1,0:T(8,128)(2,1)S(1)}, bf16[32,768]{1,0:T(8,128)(2,1)S(1)}, u32[]{:S(2)}, u32[]{:S(2)}) collective-permute-start(bf16[32,768]{1,0:T(8,128)(2,1)S(1)} %get-tuple-element.28.packed_ref), channel_id=1, source_target_pairs={{0,13},{1,12},{2,15},{3,14},{4,9},{5,8},{6,11},{7,10},{8,5},{9,4},... | collective-permute-start | bytes 147464 | tf_op jit(solution)/shard_map/ppermute | solution.py:234
  10.7 1.5 %collective-permute-start.3 = (bf16[4,32,768]{2,1,0:T(8,128)(2,1)S(1)}, bf16[4,32,768]{2,1,0:T(8,128)(2,1)S(1)}, u32[]{:S(2)}, u32[]{:S(2)}) collective-permute-start(bf16[4,32,768]{2,1,0:T(8,128)(2,1)S(1)} %pad_maximum_fusion.blocks_ref), channel_id=1, source_target_pairs={{0,1},{1,0},{2,3},{3,2},{4,5},{5,4},{6,7},{7,6},{8,9},{9,8},{10,11... | collective-permute-start | bytes 589832 | tf_op jit(solution)/shard_map/ppermute | solution.py:234
  13.1 2.4 %collective-permute-start.5 = (bf16[1,32,768]{2,1,0:T(8,128)(2,1)S(1)}, bf16[1,32,768]{2,1,0:T(8,128)(2,1)S(1)}, u32[]{:S(2)}, u32[]{:S(2)}) collective-permute-start(bf16[1,32,768]{2,1,0:T(8,128)(2,1)S(1)} %bitcast.12), channel_id=1, source_target_pairs={{0,1},{1,0},{2,3},{3,2},{4,5},{5,4},{6,7},{7,6},{8,9},{9,8},{10,11... | collective-permute-start | bytes 147464 | tf_op jit(solution)/shard_map/ppermute | solution.py:234
  16.4 3.7 %collective-permute-start.6 = (f32[16,768]{1,0:T(8,128)S(1)}, f32[16,768]{1,0:T(8,128)S(1)}, u32[]{:S(2)}, u32[]{:S(2)}) collective-permute-start(f32[16,768]{1,0:T(8,128)S(1)} %partner_late.3), channel_id=1, source_target_pairs={{0,3},{1,2},{2,1},{3,0},{4,7},{5,6},{6,5},{7,4},{8,11},{9,10},{10,... | collective-permute-start | bytes 147464 | tf_op jit(solution)/shard_map/ppermute | solution.py:234

commit v6 on v5

--- a/solution.py
+++ b/solution.py
@@ -283,7 +283,7 @@
     core = (0, 1)
     lines = [(r, 1) for r in range(n_row - 1, 0, -1)]
     if n_row == 4:
-        lines = [(3, 1), (1, 1), (2, 1)]
+        lines = [(1, 1), (2, 1), (3, 1)]
     partners = [(0, c) for c in range(3, n_col, 2)]
     met = [sent(packed, hop) for hop in partners]
     line = [sent(packed, hop) for hop in lines]

time: 31.9 us -> 33.6 us (1.053)
  Pallas kernels: 10.4 us -> 7.68 us
  waiting for transfers between devices: 2.94 us -> 5.23 us
  starting transfers between devices: 7.66 us -> 8.73 us
  blocking collectives: 9.66 us -> 10.5 us
    pallas_call x11, Pallas kernels: 10.4 us -> 7.68 us  [call(): pl.pallas_call(kernel, out_shape=shapes, in_specs=[where] * len(args), ou...]
    ppermute x7, waiting for transfers between devices: 2.94 us -> 5.23 us  [sent(): return lax.ppermute(x, ('row', 'col'), pairs)]
    ppermute x7, starting transfers between devices: 7.66 us -> 8.73 us  [sent(): return lax.ppermute(x, ('row', 'col'), pairs)]
    all_to_all x1, blocking collectives: 9.66 us -> 10.5 us  [per_device(): grams = lax.all_to_all(gram, ('row', 'col'), 0, 0)]
  transfers between devices with their start and end apart: 7 -> 7, of which waited for: 3 -> 4; matrix products, arithmetic and copies ran while one was open for 0% -> 0% of each run, Pallas kernels for 22% -> 15%
where the time goes in v6:
time: 33.6 us; the launch traced here: 32.9 us
  blocking collectives  10.5 us (31%)
  starting transfers between devices  8.73 us (26%)
  Pallas kernels  7.68 us (23%)
  waiting for transfers between devices  5.23 us (16%)
  between operations  0.7 us (2%)
    all_to_all x1, blocking collectives, per_device(): grams = lax.all_to_all(gram, ('row', 'col'), 0, 0)  10.5 us
    ppermute x7, starting transfers between devices, sent(): return lax.ppermute(x, ('row', 'col'), pairs)  8.73 us
    pallas_call x11, Pallas kernels, call(): pl.pallas_call(kernel, out_shape=shapes, in_specs=[where] * len(args), ou...  7.68 us
    ppermute x7, waiting for transfers between devices, sent(): return lax.ppermute(x, ('row', 'col'), pairs)  5.23 us
  transfers between devices with their start and end apart: 7, of which 4 were waited for; matrix products, arithmetic and copies ran while one was open for 0% of the time, Pallas kernels for 15%

profile of v6, /device:TPU:0, one launch (start us, length us, event | category | flops | bytes accessed | tf_op | source)
XLA Modules:
  0.0 32.9 jit_solution(16939549456312200604)
XLA Ops:
  0.6 0.8 %pack.1 = (bf16[32,768]{1,0:T(8,128)(2,1)S(1)}, bf16[16,768]{1,0:T(8,128)(2,1)S(1)}, f32[1,768]{1,0:T(1,128)S(1)}, s32[8,2,16]{2,1,0:T(2,128)S(1)}) custom-call(bf16[16,768]{1,0:T(8,128)(2,1)} %frames_ref.1, bf16[16,768]{1,0:T(8,128)(2,1)} %vectors_in.1, f32[768]{0:T(1024)} %degrees_ref.1, s32[8,2,16]{2,1,0:T(2,128)} %bitcast.16), custom_call_target="tpu_custom_call" | custom-call | tf_op jit(solution)/shard_map/pack/pallas_call | solution.py:251
  1.4 2.4 %collective-permute-start.2 = (bf16[32,768]{1,0:T(8,128)(2,1)S(1)}, bf16[32,768]{1,0:T(8,128)(2,1)S(1)}, u32[]{:S(2)}, u32[]{:S(2)}) collective-permute-start(bf16[32,768]{1,0:T(8,128)(2,1)S(1)} %get-tuple-element.28.packed_ref), channel_id=1, source_target_pairs={{0,3},{1,2},{2,1},{3,0},{4,7},{5,6},{6,5},{7,4},{8,11},{9,10},{10,... | collective-permute-start | bytes 147464 | tf_op jit(solution)/shard_map/ppermute | solution.py:234
  3.9 3.9 %collective-permute-start.1 = (bf16[32,768]{1,0:T(8,128)(2,1)S(1)}, bf16[32,768]{1,0:T(8,128)(2,1)S(1)}, u32[]{:S(2)}, u32[]{:S(2)}) collective-permute-start(bf16[32,768]{1,0:T(8,128)(2,1)S(1)} %get-tuple-element.28.packed_ref), channel_id=1, source_target_pairs={{0,13},{1,12},{2,15},{3,14},{4,9},{5,8},{6,11},{7,10},{8,5},{9,4},... | collective-permute-start | bytes 147464 | tf_op jit(solution)/shard_map/ppermute | solution.py:234
  7.8 0.0 collective-permute-start
  7.8 0.5 %collective-permute-start.4 = (bf16[32,768]{1,0:T(8,128)(2,1)S(1)}, bf16[32,768]{1,0:T(8,128)(2,1)S(1)}, u32[]{:S(2)}, u32[]{:S(2)}) collective-permute-start(bf16[32,768]{1,0:T(8,128)(2,1)S(1)} %get-tuple-element.28.packed_ref), channel_id=1, source_target_pairs={{0,5},{1,4},{2,7},{3,6},{4,1},{5,0},{6,3},{7,2},{8,13},{9,12},{10,... | collective-permute-start | bytes 147464 | tf_op jit(solution)/shard_map/ppermute | solution.py:234
  8.3 0.7 %own.1 = (bf16[64,768]{1,0:T(8,128)(2,1)S(1)}, f32[16,768]{1,0:T(8,128)S(1)}) custom-call(bf16[32,768]{1,0:T(8,128)(2,1)S(1)} %get-tuple-element.28.packed_ref), custom_call_target="tpu_custom_call" | custom-call | tf_op jit(solution)/shard_map/own/pallas_call | solution.py:251
  8.9 0.0 collective-permute-done.2.block_ref
  9.0 0.9 %collective-permute-done.1 = bf16[32,768]{1,0:T(8,128)(2,1)S(1)} collective-permute-done((bf16[32,768]{1,0:T(8,128)(2,1)S(1)}, bf16[32,768]{1,0:T(8,128)(2,1)S(1)}, u32[]{:S(2)}, u32[]{:S(2)}) %collective-permute-start.1) | collective-permute-done | bytes 49184 | tf_op jit(solution)/shard_map/ppermute | solution.py:234
  9.9 2.9 %collective-permute-done = bf16[32,768]{1,0:T(8,128)(2,1)S(1)} collective-permute-done((bf16[32,768]{1,0:T(8,128)(2,1)S(1)}, bf16[32,768]{1,0:T(8,128)(2,1)S(1)}, u32[]{:S(2)}, u32[]{:S(2)}) %collective-permute-start) | collective-permute-done | bytes 49184 | tf_op jit(solution)/shard_map/ppermute | solution.py:234
  12.9 0.1 collective-permute-start.3
  13.0 0.2 partner.2.before_ref
  13.2 1.2 %collective-permute-done.3.blocks_ref = bf16[4,32,768]{2,1,0:T(8,128)(2,1)S(1)} collective-permute-done((bf16[4,32,768]{2,1,0:T(8,128)(2,1)S(1)}, bf16[4,32,768]{2,1,0:T(8,128)(2,1)S(1)}, u32[]{:S(2)}, u32[]{:S(2)}) %collective-permute-start.3) | collective-permute-done | bytes 196640 | tf_op jit(solution)/shard_map/ppermute | solution.py:234
  14.4 1.3 %partner.3.before_ref = f32[16,768]{1,0:T(8,128)S(1)} custom-call(s32[8,2,16]{2,1,0:T(2,128)S(1)} %get-tuple-element.27.table_ref, bf16[64,768]{1,0:T(8,128)(2,1)S(1)} %side.1.side_ref, bf16[4,32,768]{2,1,0:T(8,128)(2,1)S(1)} %collective-permute-done.3.blocks_ref, f32[16,768]{1,0:T(8,128)S(1)} %partner.2.before_ref), custom_call_target="tpu_custom_call", output_to_operand_aliasing={{}: (3, {})} | custom-call | tf_op jit(solution)/shard_map/partner/pallas_call | solution.py:251
  15.7 0.0 collective-permute-done.4
  15.7 0.1 collective-permute-start.5
  15.9 0.2 partner_late.2.before_ref
  16.1 0.9 %add_met.1.before_ref = f32[16,768]{1,0:T(8,128)S(1)} custom-call(s32[8,2,16]{2,1,0:T(2,128)S(1)} %get-tuple-element.27.table_ref, bf16[64,768]{1,0:T(8,128)(2,1)S(1)} %get-tuple-element.29.side_ref, bf16[1,32,768]{2,1,0:T(8,128)(2,1)S(1)} %bitcast.10, f32[16,768]{1,0:T(8,128)S(1)} %get-tuple-element.40.before_ref), custom_call_target="tpu_custom_call", output_to_operand_aliasing={{}: (3, {})} | custom-call | tf_op jit(solution)/shard_map/add_met/pallas_call | solution.py:251
  17.0 0.0 collective-permute-done.5.blocks_ref
  17.0 0.2 partner_late.3
  17.2 1.6 %collective-permute-start.6 = (f32[16,768]{1,0:T(8,128)S(1)}, f32[16,768]{1,0:T(8,128)S(1)}, u32[]{:S(2)}, u32[]{:S(2)}) collective-permute-start(f32[16,768]{1,0:T(8,128)S(1)} %partner_late.3), channel_id=1, source_target_pairs={{0,3},{1,2},{2,1},{3,0},{4,7},{5,6},{6,5},{7,4},{8,11},{9,10},{10,... | collective-permute-start | bytes 147464 | tf_op jit(solution)/shard_map/ppermute | solution.py:234
  18.8 1.8 %add_own.1.refs_0_ = f32[16,768]{1,0:T(8,128)S(1)} custom-call(s32[8,2,16]{2,1,0:T(2,128)S(1)} %get-tuple-element.27.table_ref, bf16[64,768]{1,0:T(8,128)(2,1)S(1)} %get-tuple-element.29.side_ref, bf16[8,32,768]{2,1,0:T(8,128)(2,1)S(1)} %constant_dynamic-update-slice_fusion.blocks_ref, f32[16,768]{1,0:T(8,128)S(1)} %add_met.1.before_ref), custom_call_target="tpu_custom_call", output_to_operand_aliasing={{}: (3, {})} | custom-call | tf_op jit(solution)/shard_map/add_own/pallas_call | solution.py:251
  20.6 0.2 collective-permute-done.6.refs_1_
  20.7 0.4 %last.1 = (f32[16,768]{1,0:T(8,128)S(1)}, f32[16,8,128]{2,1,0:T(8,128)S(1)}) custom-call(bf16[16,768]{1,0:T(8,128)(2,1)S(1)} %get-tuple-element.25.vectors_ref, f32[1,768]{1,0:T(1,128)S(1)} %get-tuple-element.26.root_ref, f32[16,768]{1,0:T(8,128)S(1)} %add_own.1.refs_0_, f32[16,768]{1,0:T(8,128)S(1)} %collective-permute-done.6.refs_1_), custom_call_target="tpu_custom_call" | custom-call | tf_op jit(solution)/shard_map/last/pallas_call | solution.py:251
  21.1 10.5 %all_to_all.5.grams_ref = f32[16,8,128]{2,1,0:T(8,128)S(1)} all-to-all(f32[16,8,128]{2,1,0:T(8,128)S(1)} %get-tuple-element.46), channel_id=1, replica_groups=mesh['grp'=2,'row'=4,'col'=4] {'row','col'}, dimensions={0} | all-to-all | bytes 131072 | tf_op jit(solution)/shard_map/all_to_all | solution.py:355
  31.6 1.3 %finish.1 = (f32[16,768]{1,0:T(8,128)}, f32[16,16]{1,0:T(8,128)}) custom-call(f32[16,8,128]{2,1,0:T(8,128)S(1)} %all_to_all.5.grams_ref, f32[16,768]{1,0:T(8,128)S(1)} %get-tuple-element.47.applied_ref), custom_call_target="tpu_custom_call" | custom-call | tf_op jit(solution)/shard_map/finish/pallas_call | solution.py:251
  (7 shorter events, 0.1 us)
Async XLA Ops:
  1.4 7.5 %collective-permute-start.2 = (bf16[32,768]{1,0:T(8,128)(2,1)S(1)}, bf16[32,768]{1,0:T(8,128)(2,1)S(1)}, u32[]{:S(2)}, u32[]{:S(2)}) collective-permute-start(bf16[32,768]{1,0:T(8,128)(2,1)S(1)} %get-tuple-element.28.packed_ref), channel_id=1, source_target_pairs={{0,3},{1,2},{2,1},{3,0},{4,7},{5,6},{6,5},{7,4},{8,11},{9,10},{10,... | collective-permute-start | bytes 147464 | tf_op jit(solution)/shard_map/ppermute | solution.py:234
  3.9 6.0 %collective-permute-start.1 = (bf16[32,768]{1,0:T(8,128)(2,1)S(1)}, bf16[32,768]{1,0:T(8,128)(2,1)S(1)}, u32[]{:S(2)}, u32[]{:S(2)}) collective-permute-start(bf16[32,768]{1,0:T(8,128)(2,1)S(1)} %get-tuple-element.28.packed_ref), channel_id=1, source_target_pairs={{0,13},{1,12},{2,15},{3,14},{4,9},{5,8},{6,11},{7,10},{8,5},{9,4},... | collective-permute-start | bytes 147464 | tf_op jit(solution)/shard_map/ppermute | solution.py:234
  7.8 5.1 %collective-permute-start = (bf16[32,768]{1,0:T(8,128)(2,1)S(1)}, bf16[32,768]{1,0:T(8,128)(2,1)S(1)}, u32[]{:S(2)}, u32[]{:S(2)}) collective-permute-start(bf16[32,768]{1,0:T(8,128)(2,1)S(1)} %get-tuple-element.28.packed_ref), channel_id=1, source_target_pairs={{0,9},{1,8},{2,11},{3,10},{4,13},{5,12},{6,15},{7,14},{8,1},{9,0},... | collective-permute-start | bytes 147464 | tf_op jit(solution)/shard_map/ppermute | solution.py:234
  7.8 7.9 %collective-permute-start.4 = (bf16[32,768]{1,0:T(8,128)(2,1)S(1)}, bf16[32,768]{1,0:T(8,128)(2,1)S(1)}, u32[]{:S(2)}, u32[]{:S(2)}) collective-permute-start(bf16[32,768]{1,0:T(8,128)(2,1)S(1)} %get-tuple-element.28.packed_ref), channel_id=1, source_target_pairs={{0,5},{1,4},{2,7},{3,6},{4,1},{5,0},{6,3},{7,2},{8,13},{9,12},{10,... | collective-permute-start | bytes 147464 | tf_op jit(solution)/shard_map/ppermute | solution.py:234
  12.9 1.5 %collective-permute-start.3 = (bf16[4,32,768]{2,1,0:T(8,128)(2,1)S(1)}, bf16[4,32,768]{2,1,0:T(8,128)(2,1)S(1)}, u32[]{:S(2)}, u32[]{:S(2)}) collective-permute-start(bf16[4,32,768]{2,1,0:T(8,128)(2,1)S(1)} %pad_maximum_fusion.blocks_ref), channel_id=1, source_target_pairs={{0,1},{1,0},{2,3},{3,2},{4,5},{5,4},{6,7},{7,6},{8,9},{9,8},{10,11... | collective-permute-start | bytes 589832 | tf_op jit(solution)/shard_map/ppermute | solution.py:234
  15.7 1.2 %collective-permute-start.5 = (bf16[1,32,768]{2,1,0:T(8,128)(2,1)S(1)}, bf16[1,32,768]{2,1,0:T(8,128)(2,1)S(1)}, u32[]{:S(2)}, u32[]{:S(2)}) collective-permute-start(bf16[1,32,768]{2,1,0:T(8,128)(2,1)S(1)} %bitcast.12), channel_id=1, source_target_pairs={{0,1},{1,0},{2,3},{3,2},{4,5},{5,4},{6,7},{7,6},{8,9},{9,8},{10,11... | collective-permute-start | bytes 147464 | tf_op jit(solution)/shard_map/ppermute | solution.py:234
  17.2 3.6 %collective-permute-start.6 = (f32[16,768]{1,0:T(8,128)S(1)}, f32[16,768]{1,0:T(8,128)S(1)}, u32[]{:S(2)}, u32[]{:S(2)}) collective-permute-start(f32[16,768]{1,0:T(8,128)S(1)} %partner_late.3), channel_id=1, source_target_pairs={{0,3},{1,2},{2,1},{3,0},{4,7},{5,6},{6,5},{7,4},{8,11},{9,10},{10,... | collective-permute-start | bytes 147464 | tf_op jit(solution)/shard_map/ppermute | solution.py:234

commit v7 on v2

--- a/solution.py
+++ b/solution.py
@@ -330,16 +330,21 @@
     held, held_at = early + met + [packed], lines[1:] + partners + [(0, 0)]
     near = jnp.stack(held)
     other = sent(near, core)
-    parts = [None for _ in partners]
-    for blocks, offsets in ((near, lines[1:]), (other, beyond(lines[1:], core))):
-        for k, hop in enumerate(partners):
-            parts[k] = add_part("partner", hop, offsets, sides[k], blocks, parts[k])
+    parts = [None] * len(partners)
+    for k, hop in enumerate(partners):
+        parts[k] = add_part("partner", hop, lines[1:], sides[k], near, None)
     late, parts, image = lax.optimization_barrier((line[:1], parts, image))
     late = jnp.stack(late)
     other_late = sent(late, core)
-    for blocks, offsets in ((late, lines[:1]), (other_late, beyond(lines[:1], core))):
-        for k, hop in enumerate(partners):
-            parts[k] = add_part("partner_late", hop, offsets, sides[k], blocks, parts[k])
+    middle = jnp.concatenate([other[: n_row - 2], late])
+    for k, hop in enumerate(partners):
+        places = beyond(lines[1:], core) + lines[:1]
+        parts[k] = add_part("partner_middle", hop, places, sides[k], middle, parts[k])
+    other_late, parts = lax.optimization_barrier((other_late, parts))
+    for k, hop in enumerate(partners):
+        parts[k] = add_part(
+            "partner_late", hop, beyond(lines[:1], core), sides[k], other_late, parts[k]
+        )
     parts, image = lax.optimization_barrier((parts, image))
     received = [sent(part, hop) for hop, part in zip(partners, parts)]
     own_places = lines[1:] + beyond(held_at, core) + lines[:1] + beyond(lines[:1], core)

time: 31.9 us -> 31.5 us (0.987)
  starting transfers between devices: 7.22 us -> 8.29 us
  waiting for transfers between devices: 3.17 us -> 2.16 us
  Pallas kernels: 9.89 us -> 9.48 us
    ppermute x7, starting transfers between devices: 7.22 us -> 8.29 us  [sent(): return lax.ppermute(x, ('row', 'col'), pairs)]
    ppermute x7, waiting for transfers between devices: 3.17 us -> 2.16 us  [sent(): return lax.ppermute(x, ('row', 'col'), pairs)]
    pallas_call x10 -> x9, Pallas kernels: 9.89 us -> 9.48 us  [call(): pl.pallas_call(kernel, out_shape=shapes, in_specs=[where] * len(args), ou...]
  transfers between devices with their start and end apart: 7 -> 7, of which waited for: 3 -> 3; matrix products, arithmetic and copies ran while one was open for 0% -> 0% of each run, Pallas kernels for 21% -> 20%
where the time goes in v7:
time: 31.5 us; the launch traced here: 31.3 us
  blocking collectives  10.6 us (34%)
  Pallas kernels  9.48 us (30%)
  starting transfers between devices  8.29 us (26%)
  waiting for transfers between devices  2.16 us (7%)
  between operations  0.69 us (2%)
    all_to_all x1, blocking collectives, per_device(): grams = lax.all_to_all(gram, ('row', 'col'), 0, 0)  10.6 us
    pallas_call x9, Pallas kernels, call(): pl.pallas_call(kernel, out_shape=shapes, in_specs=[where] * len(args), ou...  9.48 us
    ppermute x7, starting transfers between devices, sent(): return lax.ppermute(x, ('row', 'col'), pairs)  8.29 us
    ppermute x7, waiting for transfers between devices, sent(): return lax.ppermute(x, ('row', 'col'), pairs)  2.16 us
  transfers between devices with their start and end apart: 7, of which 3 were waited for; matrix products, arithmetic and copies ran while one was open for 0% of the time, Pallas kernels for 20%

profile of v7, /device:TPU:0, one launch (start us, length us, event | category | flops | bytes accessed | tf_op | source)
XLA Modules:
  0.0 31.3 jit_solution(15834211258899179888)
XLA Ops:
  0.6 0.8 %pack.1 = (bf16[32,768]{1,0:T(8,128)(2,1)S(1)}, bf16[16,768]{1,0:T(8,128)(2,1)S(1)}, f32[1,768]{1,0:T(1,128)S(1)}, s32[8,2,16]{2,1,0:T(2,128)S(1)}) custom-call(bf16[16,768]{1,0:T(8,128)(2,1)} %frames_ref.1, bf16[16,768]{1,0:T(8,128)(2,1)} %vectors_in.1, f32[768]{0:T(1024)} %degrees_ref.1, s32[8,2,16]{2,1,0:T(2,128)} %bitcast.16), custom_call_target="tpu_custom_call" | custom-call | tf_op jit(solution)/shard_map/pack/pallas_call | solution.py:247
  1.4 2.4 %collective-permute-start.2 = (bf16[32,768]{1,0:T(8,128)(2,1)S(1)}, bf16[32,768]{1,0:T(8,128)(2,1)S(1)}, u32[]{:S(2)}, u32[]{:S(2)}) collective-permute-start(bf16[32,768]{1,0:T(8,128)(2,1)S(1)} %get-tuple-element.27.packed_ref), channel_id=1, source_target_pairs={{0,3},{1,2},{2,1},{3,0},{4,7},{5,6},{6,5},{7,4},{8,11},{9,10},{10,... | collective-permute-start | bytes 147464 | tf_op jit(solution)/shard_map/ppermute | solution.py:230
  3.9 2.9 %collective-permute-start.1 = (bf16[32,768]{1,0:T(8,128)(2,1)S(1)}, bf16[32,768]{1,0:T(8,128)(2,1)S(1)}, u32[]{:S(2)}, u32[]{:S(2)}) collective-permute-start(bf16[32,768]{1,0:T(8,128)(2,1)S(1)} %get-tuple-element.27.packed_ref), channel_id=1, source_target_pairs={{0,9},{1,8},{2,11},{3,10},{4,13},{5,12},{6,15},{7,14},{8,1},{9,0},... | collective-permute-start | bytes 147464 | tf_op jit(solution)/shard_map/ppermute | solution.py:230
  6.8 1.0 %collective-permute-start = (bf16[32,768]{1,0:T(8,128)(2,1)S(1)}, bf16[32,768]{1,0:T(8,128)(2,1)S(1)}, u32[]{:S(2)}, u32[]{:S(2)}) collective-permute-start(bf16[32,768]{1,0:T(8,128)(2,1)S(1)} %get-tuple-element.27.packed_ref), channel_id=1, source_target_pairs={{0,5},{1,4},{2,7},{3,6},{4,1},{5,0},{6,3},{7,2},{8,13},{9,12},{10,... | collective-permute-start | bytes 147464 | tf_op jit(solution)/shard_map/ppermute | solution.py:230
  7.8 0.5 %collective-permute-start.4 = (bf16[32,768]{1,0:T(8,128)(2,1)S(1)}, bf16[32,768]{1,0:T(8,128)(2,1)S(1)}, u32[]{:S(2)}, u32[]{:S(2)}) collective-permute-start(bf16[32,768]{1,0:T(8,128)(2,1)S(1)} %get-tuple-element.27.packed_ref), channel_id=1, source_target_pairs={{0,13},{1,12},{2,15},{3,14},{4,9},{5,8},{6,11},{7,10},{8,5},{9,4},... | collective-permute-start | bytes 147464 | tf_op jit(solution)/shard_map/ppermute | solution.py:230
  8.3 0.7 %own.1 = (bf16[64,768]{1,0:T(8,128)(2,1)S(1)}, f32[16,768]{1,0:T(8,128)S(1)}) custom-call(bf16[32,768]{1,0:T(8,128)(2,1)S(1)} %get-tuple-element.27.packed_ref), custom_call_target="tpu_custom_call" | custom-call | tf_op jit(solution)/shard_map/own/pallas_call | solution.py:247
  8.9 0.0 collective-permute-done.2
  9.0 0.9 %meet.1 = (f32[16,768]{1,0:T(8,128)S(1)}, bf16[64,768]{1,0:T(8,128)(2,1)S(1)}) custom-call(s32[8,2,16]{2,1,0:T(2,128)S(1)} %get-tuple-element.26.table_ref, bf16[64,768]{1,0:T(8,128)(2,1)S(1)} %get-tuple-element.28.side_ref, bf16[1,32,768]{2,1,0:T(8,128)(2,1)S(1)} %bitcast.10, ...), custom_call_target="tpu_custom_call", output_to_operand_aliasing={{0}: (3, {})} | custom-call | tf_op jit(solution)/shard_map/meet/pallas_call | solution.py:247
  9.8 0.0 collective-permute-done.1
  9.8 0.9 %collective-permute-done = bf16[32,768]{1,0:T(8,128)(2,1)S(1)} collective-permute-done((bf16[32,768]{1,0:T(8,128)(2,1)S(1)}, bf16[32,768]{1,0:T(8,128)(2,1)S(1)}, u32[]{:S(2)}, u32[]{:S(2)}) %collective-permute-start) | collective-permute-done | bytes 49184 | tf_op jit(solution)/shard_map/ppermute | solution.py:230
  10.7 0.2 collective-permute-start.3
  10.9 1.3 %partner.1.before_ref = f32[16,768]{1,0:T(8,128)S(1)} custom-call(s32[8,2,16]{2,1,0:T(2,128)S(1)} %get-tuple-element.26.table_ref, bf16[64,768]{1,0:T(8,128)(2,1)S(1)} %get-tuple-element.35.side_ref, bf16[4,32,768]{2,1,0:T(8,128)(2,1)S(1)} %pad_maximum_fusion.blocks_ref), custom_call_target="tpu_custom_call" | custom-call | tf_op jit(solution)/shard_map/partner/pallas_call | solution.py:247
  12.2 0.9 %collective-permute-done.4 = bf16[32,768]{1,0:T(8,128)(2,1)S(1)} collective-permute-done((bf16[32,768]{1,0:T(8,128)(2,1)S(1)}, bf16[32,768]{1,0:T(8,128)(2,1)S(1)}, u32[]{:S(2)}, u32[]{:S(2)}) %collective-permute-start.4) | collective-permute-done | bytes 49184 | tf_op jit(solution)/shard_map/ppermute | solution.py:230
  13.1 0.7 %collective-permute-start.5 = (bf16[1,32,768]{2,1,0:T(8,128)(2,1)S(1)}, bf16[1,32,768]{2,1,0:T(8,128)(2,1)S(1)}, u32[]{:S(2)}, u32[]{:S(2)}) collective-permute-start(bf16[1,32,768]{2,1,0:T(8,128)(2,1)S(1)} %bitcast.12), channel_id=1, source_target_pairs={{0,1},{1,0},{2,3},{3,2},{4,5},{5,4},{6,7},{7,6},{8,9},{9,8},{10,11... | collective-permute-start | bytes 147464 | tf_op jit(solution)/shard_map/ppermute | solution.py:230
  13.8 0.0 collective-permute-done.3
  13.8 0.9 %partner_middle.1.before_ref = f32[16,768]{1,0:T(8,128)S(1)} custom-call(s32[8,2,16]{2,1,0:T(2,128)S(1)} %get-tuple-element.26.table_ref, bf16[64,768]{1,0:T(8,128)(2,1)S(1)} %get-tuple-element.35.side_ref, bf16[3,32,768]{2,1,0:T(8,128)(2,1)S(1)} %pad_maximum_fusion.1.blocks_ref, f32[16,768]{1,0:T(8,128)S(1)} %partner.1.before_ref), custom_call_target="tpu_custom_call", output_to_operand_aliasing={{}: (3, {})} | custom-call | tf_op jit(solution)/shard_map/partner_middle/pallas_call | solution.py:247
  14.7 0.0 collective-permute-done.5.blocks_ref
  14.7 0.9 %partner_late.1 = f32[16,768]{1,0:T(8,128)S(1)} custom-call(s32[8,2,16]{2,1,0:T(2,128)S(1)} %get-tuple-element.26.table_ref, bf16[64,768]{1,0:T(8,128)(2,1)S(1)} %get-tuple-element.35.side_ref, bf16[1,32,768]{2,1,0:T(8,128)(2,1)S(1)} %collective-permute-done.5.blocks_ref, f32[16,768]{1,0:T(8,128)S(1)} %partner_middle.1.before_ref), custom_call_target="tpu_custom_call", output_to_operand_aliasing={{}: (3, {})} | custom-call | tf_op jit(solution)/shard_map/partner_late/pallas_call | solution.py:247
  15.6 0.6 %collective-permute-start.6 = (f32[16,768]{1,0:T(8,128)S(1)}, f32[16,768]{1,0:T(8,128)S(1)}, u32[]{:S(2)}, u32[]{:S(2)}) collective-permute-start(f32[16,768]{1,0:T(8,128)S(1)} %partner_late.1), channel_id=1, source_target_pairs={{0,3},{1,2},{2,1},{3,0},{4,7},{5,6},{6,5},{7,4},{8,11},{9,10},{10,... | collective-permute-start | bytes 147464 | tf_op jit(solution)/shard_map/ppermute | solution.py:230
  16.2 2.4 %add_own.1.refs_0_ = f32[16,768]{1,0:T(8,128)S(1)} custom-call(s32[8,2,16]{2,1,0:T(2,128)S(1)} %get-tuple-element.26.table_ref, bf16[64,768]{1,0:T(8,128)(2,1)S(1)} %get-tuple-element.28.side_ref, bf16[8,32,768]{2,1,0:T(8,128)(2,1)S(1)} %constant_dynamic-update-slice_fusion.blocks_ref, ...), custom_call_target="tpu_custom_call", output_to_operand_aliasing={{}: (3, {})} | custom-call | tf_op jit(solution)/shard_map/add_own/pallas_call | solution.py:247
  18.7 0.4 %collective-permute-done.6.refs_1_ = f32[16,768]{1,0:T(8,128)S(1)} collective-permute-done((f32[16,768]{1,0:T(8,128)S(1)}, f32[16,768]{1,0:T(8,128)S(1)}, u32[]{:S(2)}, u32[]{:S(2)}) %collective-permute-start.6) | collective-permute-done | bytes 49184 | tf_op jit(solution)/shard_map/ppermute | solution.py:230
  19.1 0.4 %last.1 = (f32[16,768]{1,0:T(8,128)S(1)}, f32[16,8,128]{2,1,0:T(8,128)S(1)}) custom-call(bf16[16,768]{1,0:T(8,128)(2,1)S(1)} %get-tuple-element.24.vectors_ref, f32[1,768]{1,0:T(1,128)S(1)} %get-tuple-element.25.root_ref, f32[16,768]{1,0:T(8,128)S(1)} %add_own.1.refs_0_, f32[16,768]{1,0:T(8,128)S(1)} %collective-permute-done.6.refs_1_), custom_call_target="tpu_custom_call" | custom-call | tf_op jit(solution)/shard_map/last/pallas_call | solution.py:247
  19.4 10.6 %all_to_all.5.grams_ref = f32[16,8,128]{2,1,0:T(8,128)S(1)} all-to-all(f32[16,8,128]{2,1,0:T(8,128)S(1)} %get-tuple-element.44), channel_id=1, replica_groups=mesh['grp'=2,'row'=4,'col'=4] {'row','col'}, dimensions={0} | all-to-all | bytes 131072 | tf_op jit(solution)/shard_map/all_to_all | solution.py:362
  30.1 1.3 %finish.1 = (f32[16,768]{1,0:T(8,128)}, f32[16,16]{1,0:T(8,128)}) custom-call(f32[16,8,128]{2,1,0:T(8,128)S(1)} %all_to_all.5.grams_ref, f32[16,768]{1,0:T(8,128)S(1)} %get-tuple-element.45.applied_ref), custom_call_target="tpu_custom_call" | custom-call | tf_op jit(solution)/shard_map/finish/pallas_call | solution.py:247
  (8 shorter events, 0.1 us)
Async XLA Ops:
  1.4 7.5 %collective-permute-start.2 = (bf16[32,768]{1,0:T(8,128)(2,1)S(1)}, bf16[32,768]{1,0:T(8,128)(2,1)S(1)}, u32[]{:S(2)}, u32[]{:S(2)}) collective-permute-start(bf16[32,768]{1,0:T(8,128)(2,1)S(1)} %get-tuple-element.27.packed_ref), channel_id=1, source_target_pairs={{0,3},{1,2},{2,1},{3,0},{4,7},{5,6},{6,5},{7,4},{8,11},{9,10},{10,... | collective-permute-start | bytes 147464 | tf_op jit(solution)/shard_map/ppermute | solution.py:230
  3.9 6.0 %collective-permute-start.1 = (bf16[32,768]{1,0:T(8,128)(2,1)S(1)}, bf16[32,768]{1,0:T(8,128)(2,1)S(1)}, u32[]{:S(2)}, u32[]{:S(2)}) collective-permute-start(bf16[32,768]{1,0:T(8,128)(2,1)S(1)} %get-tuple-element.27.packed_ref), channel_id=1, source_target_pairs={{0,9},{1,8},{2,11},{3,10},{4,13},{5,12},{6,15},{7,14},{8,1},{9,0},... | collective-permute-start | bytes 147464 | tf_op jit(solution)/shard_map/ppermute | solution.py:230
  6.8 3.9 %collective-permute-start = (bf16[32,768]{1,0:T(8,128)(2,1)S(1)}, bf16[32,768]{1,0:T(8,128)(2,1)S(1)}, u32[]{:S(2)}, u32[]{:S(2)}) collective-permute-start(bf16[32,768]{1,0:T(8,128)(2,1)S(1)} %get-tuple-element.27.packed_ref), channel_id=1, source_target_pairs={{0,5},{1,4},{2,7},{3,6},{4,1},{5,0},{6,3},{7,2},{8,13},{9,12},{10,... | collective-permute-start | bytes 147464 | tf_op jit(solution)/shard_map/ppermute | solution.py:230
  7.8 5.3 %collective-permute-start.4 = (bf16[32,768]{1,0:T(8,128)(2,1)S(1)}, bf16[32,768]{1,0:T(8,128)(2,1)S(1)}, u32[]{:S(2)}, u32[]{:S(2)}) collective-permute-start(bf16[32,768]{1,0:T(8,128)(2,1)S(1)} %get-tuple-element.27.packed_ref), channel_id=1, source_target_pairs={{0,13},{1,12},{2,15},{3,14},{4,9},{5,8},{6,11},{7,10},{8,5},{9,4},... | collective-permute-start | bytes 147464 | tf_op jit(solution)/shard_map/ppermute | solution.py:230
  10.7 3.0 %collective-permute-start.3 = (bf16[4,32,768]{2,1,0:T(8,128)(2,1)S(1)}, bf16[4,32,768]{2,1,0:T(8,128)(2,1)S(1)}, u32[]{:S(2)}, u32[]{:S(2)}) collective-permute-start(bf16[4,32,768]{2,1,0:T(8,128)(2,1)S(1)} %pad_maximum_fusion.blocks_ref), channel_id=1, source_target_pairs={{0,1},{1,0},{2,3},{3,2},{4,5},{5,4},{6,7},{7,6},{8,9},{9,8},{10,11... | collective-permute-start | bytes 589832 | tf_op jit(solution)/shard_map/ppermute | solution.py:230
  13.1 1.6 %collective-permute-start.5 = (bf16[1,32,768]{2,1,0:T(8,128)(2,1)S(1)}, bf16[1,32,768]{2,1,0:T(8,128)(2,1)S(1)}, u32[]{:S(2)}, u32[]{:S(2)}) collective-permute-start(bf16[1,32,768]{2,1,0:T(8,128)(2,1)S(1)} %bitcast.12), channel_id=1, source_target_pairs={{0,1},{1,0},{2,3},{3,2},{4,5},{5,4},{6,7},{7,6},{8,9},{9,8},{10,11... | collective-permute-start | bytes 147464 | tf_op jit(solution)/shard_map/ppermute | solution.py:230
  15.6 3.5 %collective-permute-start.6 = (f32[16,768]{1,0:T(8,128)S(1)}, f32[16,768]{1,0:T(8,128)S(1)}, u32[]{:S(2)}, u32[]{:S(2)}) collective-permute-start(f32[16,768]{1,0:T(8,128)S(1)} %partner_late.1), channel_id=1, source_target_pairs={{0,3},{1,2},{2,1},{3,0},{4,7},{5,6},{6,5},{7,4},{8,11},{9,10},{10,... | collective-permute-start | bytes 147464 | tf_op jit(solution)/shard_map/ppermute | solution.py:230

commit v8 on v7

--- a/solution.py
+++ b/solution.py
@@ -74,36 +74,30 @@
     return jnp.dot(v, kern, preferred_element_type=jnp.float32)
 
 
-def own_kernel(packed_ref, side_ref, image_ref):
+def own_kernel(targets, sizes, table_ref, packed_ref, side_ref, image_ref, masks_ref):
+    n_row, n_col = sizes
+    my_row, my_col = lax.axis_index("row"), lax.axis_index("col")
+    first, second = table_ref[:, 0, :], table_ref[:, 1, :]
+    for t, target in enumerate(targets):
+        block = (my_row ^ target[0]) * n_col + (my_col ^ target[1])
+        other = jnp.where(first == block, second, jnp.where(second == block, first, -1))
+        for word in range(n_row * n_col // 16):
+            bit = jnp.zeros(other.shape, jnp.float32)
+            for b in range(16):
+                bit = jnp.where(other == 16 * word + b, float(1 << b), bit)
+            masks_ref[t, word] = jnp.sum(bit).astype(jnp.int32)
     side_ref[...] = own_side(packed_ref[: packed_ref.shape[0] // 2, :])
     image_ref[...] = tile_image(side_ref, [packed_ref[...]])
 
 
-def add_blocks(target, places, sizes, table_ref, side_ref, blocks_ref, image_ref, list_ref):
-    n_row, n_col = sizes
+def add_blocks(target, places, sizes, masks_ref, side_ref, blocks_ref, image_ref, list_ref):
     my_row, my_col = lax.axis_index("row"), lax.axis_index("col")
-
-    def number(offset):
-        return (my_row ^ offset[0]) * n_col + (my_col ^ offset[1])
-
-    first, second = table_ref[:, 0, :], table_ref[:, 1, :]
-    me = number(target)
-    other = jnp.where(first == me, second, jnp.where(second == me, first, -1))
-    words = []
-    for start in range(0, n_row * n_col, 16):
-        bit = jnp.zeros(other.shape, jnp.float32)
-        for b in range(16):
-            bit = jnp.where(other == start + b, float(1 << b), bit)
-        words.append(jnp.sum(bit).astype(jnp.int32))
 
     count = jnp.int32(0)
     for step, place in enumerate(places):
-        block = number(place)
-        word = words[0]
-        for w in range(1, len(words)):
-            word = jnp.where(block // 16 == w, words[w], word)
+        block = (my_row ^ place[0]) * sizes[1] + (my_col ^ place[1])
         list_ref[count] = step
-        count += (word >> (block % 16)) & 1
+        count += (masks_ref[target, block // 16] >> (block % 16)) & 1
 
     def add_group(start, size):
         blocks = [blocks_ref[list_ref[start + k]] for k in range(size)]
@@ -130,23 +124,23 @@
 
 
 def meet_kernel(
-    places, sizes, table_ref, side_ref, blocks_ref, before_ref, image_ref, partner_side_ref, list_ref
+    places, sizes, masks_ref, side_ref, blocks_ref, before_ref, image_ref, partner_side_ref, list_ref
 ):
     partner_side_ref[...] = own_side(blocks_ref[0, : blocks_ref.shape[1] // 2, :])
     image_ref[...] = before_ref[...]
-    add_blocks((0, 0), places, sizes, table_ref, side_ref, blocks_ref, image_ref, list_ref)
-
-
-def first_kernel(target, places, sizes, table_ref, side_ref, blocks_ref, image_ref, list_ref):
+    add_blocks(0, places, sizes, masks_ref, side_ref, blocks_ref, image_ref, list_ref)
+
+
+def first_kernel(target, places, sizes, masks_ref, side_ref, blocks_ref, image_ref, list_ref):
     image_ref[...] = jnp.zeros_like(image_ref)
-    add_blocks(target, places, sizes, table_ref, side_ref, blocks_ref, image_ref, list_ref)
+    add_blocks(target, places, sizes, masks_ref, side_ref, blocks_ref, image_ref, list_ref)
 
 
 def part_kernel(
-    target, places, sizes, table_ref, side_ref, blocks_ref, before_ref, image_ref, list_ref
+    target, places, sizes, masks_ref, side_ref, blocks_ref, before_ref, image_ref, list_ref
 ):
     image_ref[...] = before_ref[...]
-    add_blocks(target, places, sizes, table_ref, side_ref, blocks_ref, image_ref, list_ref)
+    add_blocks(target, places, sizes, masks_ref, side_ref, blocks_ref, image_ref, list_ref)
 
 
 def last_kernel(vectors_ref, root_ref, *refs):
@@ -241,14 +235,17 @@
     devices = n_row * n_col
     sizes = (n_row, n_col)
     vmem = pl.BlockSpec(memory_space=pltpu.VMEM)
-
-    def call(kernel, name, outs, *args, limit=24, where=vmem, **keywords):
-        shapes = [jax.ShapeDtypeStruct(*out) for out in outs]
+    smem = pl.BlockSpec(memory_space=pltpu.SMEM)
+
+    def call(kernel, name, outs, *args, limit=24, where=vmem, to=vmem, **keywords):
+        shapes = [jax.ShapeDtypeStruct(*out) if isinstance(out, tuple) else out for out in outs]
+        where = where if isinstance(where, list) else [where] * len(args)
+        to = to if isinstance(to, list) else [to] * len(outs)
         return pl.pallas_call(
             kernel,
             out_shape=shapes,
-            in_specs=[where] * len(args),
-            out_specs=[vmem] * len(outs),
+            in_specs=where,
+            out_specs=to,
             compiler_params=pltpu.CompilerParams(vmem_limit_bytes=limit * MIB),
             name=name,
             **keywords,
@@ -289,8 +286,9 @@
             functools.partial(kernel, places, sizes),
             name,
             outs,
-            table,
+            masks,
             *args,
+            where=[smem] + [vmem] * len(args),
             scratch_shapes=[pltpu.SMEM((len(places) + 1,), jnp.int32)],
             **keywords,
         )
@@ -299,7 +297,7 @@
         kernel = part_kernel if part is not None else first_kernel
         before = [] if part is None else [part]
         (part,) = call_blocks(
-            functools.partial(kernel, target),
+            functools.partial(kernel, targets.index(target)),
             name,
             [image_type],
             places,
@@ -311,7 +309,15 @@
         return part
 
     side_type = ((3 * ncv + 16, rows), jnp.bfloat16)
-    side, image = call(own_kernel, "own", [side_type, image_type], packed)
+    targets = [(0, 0)] + partners
+    side, image, masks = call(
+        functools.partial(own_kernel, targets, sizes),
+        "own",
+        [side_type, image_type, pltpu.SMEM((len(targets), devices // 16), jnp.int32)],
+        table,
+        packed,
+        to=[vmem, vmem, smem],
+    )
     met, image = lax.optimization_barrier((met, image))
     sides = []
     for hop, block in zip(partners, met):

time: 31.5 us -> 32 us (1.016)
  Pallas kernels: 9.48 us -> 6.75 us
  waiting for transfers between devices: 2.16 us -> 4.2 us
  blocking collectives: 10.6 us -> 11.7 us
    pallas_call x9, Pallas kernels: 9.48 us -> 6.75 us  [call(): pl.pallas_call(kernel, out_shape=shapes, in_specs=where, out_specs=to, co...]
    ppermute x7, waiting for transfers between devices: 2.16 us -> 4.2 us  [sent(): return lax.ppermute(x, ('row', 'col'), pairs)]
    all_to_all x1, blocking collectives: 10.6 us -> 11.7 us  [per_device(): grams = lax.all_to_all(gram, ('row', 'col'), 0, 0)]
  transfers between devices with their start and end apart: 7 -> 7, of which waited for: 3 -> 3; matrix products, arithmetic and copies ran while one was open for 0% -> 0% of each run, Pallas kernels for 20% -> 13%
where the time goes in v8:
time: 32 us
  blocking collectives  11.7 us (37%)
  starting transfers between devices  8.51 us (27%)
  Pallas kernels  6.75 us (21%)
  waiting for transfers between devices  4.2 us (13%)
  between operations  0.72 us (2%)
    all_to_all x1, blocking collectives, per_device(): grams = lax.all_to_all(gram, ('row', 'col'), 0, 0)  11.7 us
    ppermute x7, starting transfers between devices, sent(): return lax.ppermute(x, ('row', 'col'), pairs)  8.51 us
    pallas_call x9, Pallas kernels, call(): pl.pallas_call(kernel, out_shape=shapes, in_specs=where, out_specs=to, co...  6.75 us
    ppermute x7, waiting for transfers between devices, sent(): return lax.ppermute(x, ('row', 'col'), pairs)  4.2 us
  transfers between devices with their start and end apart: 7, of which 3 were waited for; matrix products, arithmetic and copies ran while one was open for 0% of the time, Pallas kernels for 13%

profile of v8, /device:TPU:0, one launch (start us, length us, event | category | flops | bytes accessed | tf_op | source)
XLA Modules:
  0.0 32.0 jit_solution(10739318704683150125)
XLA Ops:
  0.6 0.8 %pack.1 = (bf16[32,768]{1,0:T(8,128)(2,1)S(1)}, bf16[16,768]{1,0:T(8,128)(2,1)S(1)}, f32[1,768]{1,0:T(1,128)S(1)}, s32[8,2,16]{2,1,0:T(2,128)S(1)}) custom-call(bf16[16,768]{1,0:T(8,128)(2,1)} %frames_ref.1, bf16[16,768]{1,0:T(8,128)(2,1)} %vectors_in.1, f32[768]{0:T(1024)} %degrees_ref.1, s32[8,2,16]{2,1,0:T(2,128)} %bitcast.16), custom_call_target="tpu_custom_call" | custom-call | tf_op jit(solution)/shard_map/pack/pallas_call | solution.py:244
  1.4 2.4 %collective-permute-start.2 = (bf16[32,768]{1,0:T(8,128)(2,1)S(1)}, bf16[32,768]{1,0:T(8,128)(2,1)S(1)}, u32[]{:S(2)}, u32[]{:S(2)}) collective-permute-start(bf16[32,768]{1,0:T(8,128)(2,1)S(1)} %get-tuple-element.28.packed_ref), channel_id=1, source_target_pairs={{0,3},{1,2},{2,1},{3,0},{4,7},{5,6},{6,5},{7,4},{8,11},{9,10},{10,... | collective-permute-start | bytes 147464 | tf_op jit(solution)/shard_map/ppermute | solution.py:224
  3.9 2.9 %collective-permute-start.1 = (bf16[32,768]{1,0:T(8,128)(2,1)S(1)}, bf16[32,768]{1,0:T(8,128)(2,1)S(1)}, u32[]{:S(2)}, u32[]{:S(2)}) collective-permute-start(bf16[32,768]{1,0:T(8,128)(2,1)S(1)} %get-tuple-element.28.packed_ref), channel_id=1, source_target_pairs={{0,9},{1,8},{2,11},{3,10},{4,13},{5,12},{6,15},{7,14},{8,1},{9,0},... | collective-permute-start | bytes 147464 | tf_op jit(solution)/shard_map/ppermute | solution.py:224
  6.8 1.0 %collective-permute-start = (bf16[32,768]{1,0:T(8,128)(2,1)S(1)}, bf16[32,768]{1,0:T(8,128)(2,1)S(1)}, u32[]{:S(2)}, u32[]{:S(2)}) collective-permute-start(bf16[32,768]{1,0:T(8,128)(2,1)S(1)} %get-tuple-element.28.packed_ref), channel_id=1, source_target_pairs={{0,5},{1,4},{2,7},{3,6},{4,1},{5,0},{6,3},{7,2},{8,13},{9,12},{10,... | collective-permute-start | bytes 147464 | tf_op jit(solution)/shard_map/ppermute | solution.py:224
  7.8 0.5 %collective-permute-start.4 = (bf16[32,768]{1,0:T(8,128)(2,1)S(1)}, bf16[32,768]{1,0:T(8,128)(2,1)S(1)}, u32[]{:S(2)}, u32[]{:S(2)}) collective-permute-start(bf16[32,768]{1,0:T(8,128)(2,1)S(1)} %get-tuple-element.28.packed_ref), channel_id=1, source_target_pairs={{0,13},{1,12},{2,15},{3,14},{4,9},{5,8},{6,11},{7,10},{8,5},{9,4},... | collective-permute-start | bytes 147464 | tf_op jit(solution)/shard_map/ppermute | solution.py:224
  8.3 0.7 %own.1 = (bf16[64,768]{1,0:T(8,128)(2,1)S(1)}, f32[16,768]{1,0:T(8,128)S(1)}, s32[2,1]{1,0:T(2,128)S(4)}) custom-call(s32[8,2,16]{2,1,0:T(2,128)S(1)} %get-tuple-element.27.table_ref, bf16[32,768]{1,0:T(8,128)(2,1)S(1)} %get-tuple-element.28.packed_ref), custom_call_target="tpu_custom_call" | custom-call | tf_op jit(solution)/shard_map/own/pallas_call | solution.py:244
  9.0 0.0 collective-permute-done.2
  9.1 0.0 collective-permute-done.1
  9.1 1.6 %collective-permute-done = bf16[32,768]{1,0:T(8,128)(2,1)S(1)} collective-permute-done((bf16[32,768]{1,0:T(8,128)(2,1)S(1)}, bf16[32,768]{1,0:T(8,128)(2,1)S(1)}, u32[]{:S(2)}, u32[]{:S(2)}) %collective-permute-start) | collective-permute-done | bytes 49184 | tf_op jit(solution)/shard_map/ppermute | solution.py:224
  10.7 0.2 collective-permute-start.3
  10.9 2.2 %collective-permute-done.4 = bf16[32,768]{1,0:T(8,128)(2,1)S(1)} collective-permute-done((bf16[32,768]{1,0:T(8,128)(2,1)S(1)}, bf16[32,768]{1,0:T(8,128)(2,1)S(1)}, u32[]{:S(2)}, u32[]{:S(2)}) %collective-permute-start.4) | collective-permute-done | bytes 49184 | tf_op jit(solution)/shard_map/ppermute | solution.py:224
  13.1 0.7 %collective-permute-start.5 = (bf16[1,32,768]{2,1,0:T(8,128)(2,1)S(1)}, bf16[1,32,768]{2,1,0:T(8,128)(2,1)S(1)}, u32[]{:S(2)}, u32[]{:S(2)}) collective-permute-start(bf16[1,32,768]{2,1,0:T(8,128)(2,1)S(1)} %bitcast.12), channel_id=1, source_target_pairs={{0,1},{1,0},{2,3},{3,2},{4,5},{5,4},{6,7},{7,6},{8,9},{9,8},{10,11... | collective-permute-start | bytes 147464 | tf_op jit(solution)/shard_map/ppermute | solution.py:224
  13.8 0.0 collective-permute-done.3
  13.8 1.2 %partner_middle.1.before_ref = f32[16,768]{1,0:T(8,128)S(1)} custom-call(s32[2,1]{1,0:T(2,128)S(4)} %get-tuple-element.29.masks_ref, bf16[64,768]{1,0:T(8,128)(2,1)S(1)} %get-tuple-element.37.side_ref, bf16[3,32,768]{2,1,0:T(8,128)(2,1)S(1)} %pad_maximum_fusion.1.blocks_ref, f32[16,768]{1,0:T(8,128)S(1)} %partner.1.before_ref), custom_call_target="tpu_custom_call", output_to_operand_aliasing={{}: (3, {})} | custom-call | tf_op jit(solution)/shard_map/partner_middle/pallas_call | solution.py:244
  15.0 0.0 collective-permute-done.5.blocks_ref
  15.0 0.8 %collective-permute-start.6 = (f32[16,768]{1,0:T(8,128)S(1)}, f32[16,768]{1,0:T(8,128)S(1)}, u32[]{:S(2)}, u32[]{:S(2)}) collective-permute-start(f32[16,768]{1,0:T(8,128)S(1)} %partner_late.1), channel_id=1, source_target_pairs={{0,3},{1,2},{2,1},{3,0},{4,7},{5,6},{6,5},{7,4},{8,11},{9,10},{10,... | collective-permute-start | bytes 147464 | tf_op jit(solution)/shard_map/ppermute | solution.py:224
  15.9 2.3 %add_own.1.refs_0_ = f32[16,768]{1,0:T(8,128)S(1)} custom-call(s32[2,1]{1,0:T(2,128)S(4)} %get-tuple-element.29.masks_ref, bf16[64,768]{1,0:T(8,128)(2,1)S(1)} %get-tuple-element.30.side_ref, bf16[8,32,768]{2,1,0:T(8,128)(2,1)S(1)} %constant_dynamic-update-slice_fusion.blocks_ref, ...), custom_call_target="tpu_custom_call", output_to_operand_aliasing={{}: (3, {})} | custom-call | tf_op jit(solution)/shard_map/add_own/pallas_call | solution.py:244
  18.2 0.4 %collective-permute-done.6.refs_1_ = f32[16,768]{1,0:T(8,128)S(1)} collective-permute-done((f32[16,768]{1,0:T(8,128)S(1)}, f32[16,768]{1,0:T(8,128)S(1)}, u32[]{:S(2)}, u32[]{:S(2)}) %collective-permute-start.6) | collective-permute-done | bytes 49184 | tf_op jit(solution)/shard_map/ppermute | solution.py:224
  18.6 0.4 %last.1 = (f32[16,768]{1,0:T(8,128)S(1)}, f32[16,8,128]{2,1,0:T(8,128)S(1)}) custom-call(bf16[16,768]{1,0:T(8,128)(2,1)S(1)} %get-tuple-element.25.vectors_ref, f32[1,768]{1,0:T(1,128)S(1)} %get-tuple-element.26.root_ref, f32[16,768]{1,0:T(8,128)S(1)} %add_own.1.refs_0_, f32[16,768]{1,0:T(8,128)S(1)} %collective-permute-done.6.refs_1_), custom_call_target="tpu_custom_call" | custom-call | tf_op jit(solution)/shard_map/last/pallas_call | solution.py:244
  19.0 11.7 %all_to_all.5.grams_ref = f32[16,8,128]{2,1,0:T(8,128)S(1)} all-to-all(f32[16,8,128]{2,1,0:T(8,128)S(1)} %get-tuple-element.46), channel_id=1, replica_groups=mesh['grp'=2,'row'=4,'col'=4] {'row','col'}, dimensions={0} | all-to-all | bytes 131072 | tf_op jit(solution)/shard_map/all_to_all | solution.py:368
  30.7 1.3 %finish.1 = (f32[16,768]{1,0:T(8,128)}, f32[16,16]{1,0:T(8,128)}) custom-call(f32[16,8,128]{2,1,0:T(8,128)S(1)} %all_to_all.5.grams_ref, f32[16,768]{1,0:T(8,128)S(1)} %get-tuple-element.47.applied_ref), custom_call_target="tpu_custom_call" | custom-call | tf_op jit(solution)/shard_map/finish/pallas_call | solution.py:244
  (11 shorter events, 0.2 us)
Async XLA Ops:
  1.4 7.5 %collective-permute-start.2 = (bf16[32,768]{1,0:T(8,128)(2,1)S(1)}, bf16[32,768]{1,0:T(8,128)(2,1)S(1)}, u32[]{:S(2)}, u32[]{:S(2)}) collective-permute-start(bf16[32,768]{1,0:T(8,128)(2,1)S(1)} %get-tuple-element.28.packed_ref), channel_id=1, source_target_pairs={{0,3},{1,2},{2,1},{3,0},{4,7},{5,6},{6,5},{7,4},{8,11},{9,10},{10,... | collective-permute-start | bytes 147464 | tf_op jit(solution)/shard_map/ppermute | solution.py:224
  3.9 5.2 %collective-permute-start.1 = (bf16[32,768]{1,0:T(8,128)(2,1)S(1)}, bf16[32,768]{1,0:T(8,128)(2,1)S(1)}, u32[]{:S(2)}, u32[]{:S(2)}) collective-permute-start(bf16[32,768]{1,0:T(8,128)(2,1)S(1)} %get-tuple-element.28.packed_ref), channel_id=1, source_target_pairs={{0,9},{1,8},{2,11},{3,10},{4,13},{5,12},{6,15},{7,14},{8,1},{9,0},... | collective-permute-start | bytes 147464 | tf_op jit(solution)/shard_map/ppermute | solution.py:224
  6.8 3.9 %collective-permute-start = (bf16[32,768]{1,0:T(8,128)(2,1)S(1)}, bf16[32,768]{1,0:T(8,128)(2,1)S(1)}, u32[]{:S(2)}, u32[]{:S(2)}) collective-permute-start(bf16[32,768]{1,0:T(8,128)(2,1)S(1)} %get-tuple-element.28.packed_ref), channel_id=1, source_target_pairs={{0,5},{1,4},{2,7},{3,6},{4,1},{5,0},{6,3},{7,2},{8,13},{9,12},{10,... | collective-permute-start | bytes 147464 | tf_op jit(solution)/shard_map/ppermute | solution.py:224
  7.8 5.3 %collective-permute-start.4 = (bf16[32,768]{1,0:T(8,128)(2,1)S(1)}, bf16[32,768]{1,0:T(8,128)(2,1)S(1)}, u32[]{:S(2)}, u32[]{:S(2)}) collective-permute-start(bf16[32,768]{1,0:T(8,128)(2,1)S(1)} %get-tuple-element.28.packed_ref), channel_id=1, source_target_pairs={{0,13},{1,12},{2,15},{3,14},{4,9},{5,8},{6,11},{7,10},{8,5},{9,4},... | collective-permute-start | bytes 147464 | tf_op jit(solution)/shard_map/ppermute | solution.py:224
  10.7 3.0 %collective-permute-start.3 = (bf16[4,32,768]{2,1,0:T(8,128)(2,1)S(1)}, bf16[4,32,768]{2,1,0:T(8,128)(2,1)S(1)}, u32[]{:S(2)}, u32[]{:S(2)}) collective-permute-start(bf16[4,32,768]{2,1,0:T(8,128)(2,1)S(1)} %pad_maximum_fusion.blocks_ref), channel_id=1, source_target_pairs={{0,1},{1,0},{2,3},{3,2},{4,5},{5,4},{6,7},{7,6},{8,9},{9,8},{10,11... | collective-permute-start | bytes 589832 | tf_op jit(solution)/shard_map/ppermute | solution.py:224
  13.1 1.9 %collective-permute-start.5 = (bf16[1,32,768]{2,1,0:T(8,128)(2,1)S(1)}, bf16[1,32,768]{2,1,0:T(8,128)(2,1)S(1)}, u32[]{:S(2)}, u32[]{:S(2)}) collective-permute-start(bf16[1,32,768]{2,1,0:T(8,128)(2,1)S(1)} %bitcast.12), channel_id=1, source_target_pairs={{0,1},{1,0},{2,3},{3,2},{4,5},{5,4},{6,7},{7,6},{8,9},{9,8},{10,11... | collective-permute-start | bytes 147464 | tf_op jit(solution)/shard_map/ppermute | solution.py:224
  15.0 3.6 %collective-permute-start.6 = (f32[16,768]{1,0:T(8,128)S(1)}, f32[16,768]{1,0:T(8,128)S(1)}, u32[]{:S(2)}, u32[]{:S(2)}) collective-permute-start(f32[16,768]{1,0:T(8,128)S(1)} %partner_late.1), channel_id=1, source_target_pairs={{0,3},{1,2},{2,1},{3,0},{4,7},{5,6},{6,5},{7,4},{8,11},{9,10},{10,... | collective-permute-start | bytes 147464 | tf_op jit(solution)/shard_map/ppermute | solution.py:224

commit v9 on v8

--- a/solution.py
+++ b/solution.py
@@ -149,12 +149,15 @@
     n = vectors_ref.shape[0]
     applied = image * root_ref[...]
     applied_ref[...] = applied
-    both = jnp.concatenate([applied, vectors_ref[...].astype(jnp.float32)], axis=0)
-    gram = lax.dot_general(
-        both, both, NT, precision=lax.Precision.HIGHEST, preferred_element_type=jnp.float32
-    )
+    high, mid, low = split3(applied)
+    pieces = jnp.concatenate(
+        [high, mid, low, vectors_ref[...].astype(jnp.float32)], axis=0
+    ).astype(jnp.bfloat16)
+    product = lax.dot_general(pieces, pieces, NT, preferred_element_type=jnp.float32)
+    rows = jnp.concatenate([product[:n] + product[n : 2 * n] + product[2 * n : 3 * n], product[3 * n :]], axis=0)
+    gram = rows[:, :n] + rows[:, n : 2 * n] + rows[:, 2 * n : 3 * n]
     wide = jnp.concatenate(
-        [gram[:n, :n], gram[n:, :], jnp.zeros((n, n), jnp.float32)], axis=1
+        [gram[:n, :], gram[n:, :], rows[n:, 3 * n :], jnp.zeros((n, n), jnp.float32)], axis=1
     )
     tile = jnp.concatenate([wide[: n // 2, :], wide[n // 2 :, :]], axis=1)
     for device in range(gram_ref.shape[0]):
@@ -180,21 +183,30 @@
         for j in range(n)
     ]
     right = [jnp.where(lane % half == row + 8 * t, 1.0, 0.0) for t in tiles]
-    pivots = [jnp.ones(shape, jnp.float32) for t in tiles]
-    for k in range(n):
+    done = [jnp.zeros(shape, jnp.float32) for t in tiles]
+    for k in range(0, n, 2):
         top, at = k // 8, k % 8
-        pivot = columns[k][top][at : at + 1, :]
-        pivots[top] = jnp.where(row == at, pivot, pivots[top])
-        if k == n - 1:
+        left, next_left = columns[k], columns[k + 1]
+        a, b = left[top][at : at + 1, :], left[top][at + 1 : at + 2, :]
+        d = next_left[top][at + 1 : at + 2, :]
+        det = a * d - b * b
+        root = lax.rsqrt(a)
+        line, next_line = right[top][at : at + 1, :], right[top][at + 1 : at + 2, :]
+        lower = (next_line - line * (b * root * root)) * (lax.rsqrt(det) * a * root)
+        done[top] = jnp.where(row == at, line * root, jnp.where(row == at + 1, lower, done[top]))
+        if k + 2 == n:
             break
-        scale = 1.0 / pivot
-        factor = {t: columns[k][t] * scale for t in tiles if t >= top}
-        factor[top] = jnp.where(row > at, factor[top], 0.0)
-        for column in columns[k + 1 :] + [right]:
-            line = column[top][at : at + 1, :]
+        scale = 1.0 / det
+        p, q, s = d * scale, b * scale, a * scale
+        factor = {t: left[t] * p - next_left[t] * q for t in tiles if t >= top}
+        next_factor = {t: next_left[t] * s - left[t] * q for t in tiles if t >= top}
+        factor[top] = jnp.where(row > at + 1, factor[top], 0.0)
+        next_factor[top] = jnp.where(row > at + 1, next_factor[top], 0.0)
+        for column in columns[k + 2 :] + [right]:
+            line, next_line = column[top][at : at + 1, :], column[top][at + 1 : at + 2, :]
             for t in factor:
-                column[t] = column[t] - factor[t] * line
-    result = jnp.concatenate([r * lax.rsqrt(p) for r, p in zip(right, pivots)], axis=0)
+                column[t] = column[t] - (factor[t] * line + next_factor[t] * next_line)
+    result = jnp.concatenate(done, axis=0)
     return result[:, :n], result[:, half : half + n]
 
 

time: 32 us -> 31.3 us (0.978); the launches traced: 32 us -> 30.9 us
  waiting for transfers between devices: 4.2 us -> 3.38 us
  Pallas kernels: 6.75 us -> 7.39 us
  blocking collectives: 11.7 us -> 11.1 us
    ppermute x7, waiting for transfers between devices: 4.2 us -> 3.38 us  [sent(): return lax.ppermute(x, ('row', 'col'), pairs)]
    pallas_call x9, Pallas kernels: 6.75 us -> 7.39 us  [call(): pl.pallas_call(kernel, out_shape=shapes, in_specs=where, out_specs=to, co...]
    all_to_all x1, blocking collectives: 11.7 us -> 11.1 us  [per_device(): grams = lax.all_to_all(gram, ('row', 'col'), 0, 0)]
  transfers between devices with their start and end apart: 7 -> 7, of which waited for: 3 -> 4; matrix products, arithmetic and copies ran while one was open for 0% -> 0% of each run, Pallas kernels for 13% -> 16%
where the time goes in v9:
time: 31.3 us; the launch traced here: 30.9 us
  blocking collectives  11.1 us (35%)
  starting transfers between devices  8.24 us (26%)
  Pallas kernels  7.39 us (24%)
  waiting for transfers between devices  3.38 us (11%)
  between operations  0.71 us (2%)
    all_to_all x1, blocking collectives, per_device(): grams = lax.all_to_all(gram, ('row', 'col'), 0, 0)  11.1 us
    ppermute x7, starting transfers between devices, sent(): return lax.ppermute(x, ('row', 'col'), pairs)  8.24 us
    pallas_call x9, Pallas kernels, call(): pl.pallas_call(kernel, out_shape=shapes, in_specs=where, out_specs=to, co...  7.39 us
    ppermute x7, waiting for transfers between devices, sent(): return lax.ppermute(x, ('row', 'col'), pairs)  3.38 us
  transfers between devices with their start and end apart: 7, of which 4 were waited for; matrix products, arithmetic and copies ran while one was open for 0% of the time, Pallas kernels for 16%

profile of v9, /device:TPU:0, one launch (start us, length us, event | category | flops | bytes accessed | tf_op | source)
XLA Modules:
  0.0 30.9 jit_solution(17803437770186095055)
XLA Ops:
  0.6 0.8 %pack.1 = (bf16[32,768]{1,0:T(8,128)(2,1)S(1)}, bf16[16,768]{1,0:T(8,128)(2,1)S(1)}, f32[1,768]{1,0:T(1,128)S(1)}, s32[8,2,16]{2,1,0:T(2,128)S(1)}) custom-call(bf16[16,768]{1,0:T(8,128)(2,1)} %frames_ref.1, bf16[16,768]{1,0:T(8,128)(2,1)} %vectors_in.1, f32[768]{0:T(1024)} %degrees_ref.1, s32[8,2,16]{2,1,0:T(2,128)} %bitcast.16), custom_call_target="tpu_custom_call" | custom-call | tf_op jit(solution)/shard_map/pack/pallas_call | solution.py:256
  1.4 2.4 %collective-permute-start.2 = (bf16[32,768]{1,0:T(8,128)(2,1)S(1)}, bf16[32,768]{1,0:T(8,128)(2,1)S(1)}, u32[]{:S(2)}, u32[]{:S(2)}) collective-permute-start(bf16[32,768]{1,0:T(8,128)(2,1)S(1)} %get-tuple-element.28.packed_ref), channel_id=1, source_target_pairs={{0,3},{1,2},{2,1},{3,0},{4,7},{5,6},{6,5},{7,4},{8,11},{9,10},{10,... | collective-permute-start | bytes 147464 | tf_op jit(solution)/shard_map/ppermute | solution.py:236
  3.9 2.9 %collective-permute-start.1 = (bf16[32,768]{1,0:T(8,128)(2,1)S(1)}, bf16[32,768]{1,0:T(8,128)(2,1)S(1)}, u32[]{:S(2)}, u32[]{:S(2)}) collective-permute-start(bf16[32,768]{1,0:T(8,128)(2,1)S(1)} %get-tuple-element.28.packed_ref), channel_id=1, source_target_pairs={{0,9},{1,8},{2,11},{3,10},{4,13},{5,12},{6,15},{7,14},{8,1},{9,0},... | collective-permute-start | bytes 147464 | tf_op jit(solution)/shard_map/ppermute | solution.py:236
  6.8 1.0 %collective-permute-start = (bf16[32,768]{1,0:T(8,128)(2,1)S(1)}, bf16[32,768]{1,0:T(8,128)(2,1)S(1)}, u32[]{:S(2)}, u32[]{:S(2)}) collective-permute-start(bf16[32,768]{1,0:T(8,128)(2,1)S(1)} %get-tuple-element.28.packed_ref), channel_id=1, source_target_pairs={{0,5},{1,4},{2,7},{3,6},{4,1},{5,0},{6,3},{7,2},{8,13},{9,12},{10,... | collective-permute-start | bytes 147464 | tf_op jit(solution)/shard_map/ppermute | solution.py:236
  7.8 0.5 %collective-permute-start.4 = (bf16[32,768]{1,0:T(8,128)(2,1)S(1)}, bf16[32,768]{1,0:T(8,128)(2,1)S(1)}, u32[]{:S(2)}, u32[]{:S(2)}) collective-permute-start(bf16[32,768]{1,0:T(8,128)(2,1)S(1)} %get-tuple-element.28.packed_ref), channel_id=1, source_target_pairs={{0,13},{1,12},{2,15},{3,14},{4,9},{5,8},{6,11},{7,10},{8,5},{9,4},... | collective-permute-start | bytes 147464 | tf_op jit(solution)/shard_map/ppermute | solution.py:236
  8.3 0.7 %own.1 = (bf16[64,768]{1,0:T(8,128)(2,1)S(1)}, f32[16,768]{1,0:T(8,128)S(1)}, s32[2,1]{1,0:T(2,128)S(4)}) custom-call(s32[8,2,16]{2,1,0:T(2,128)S(1)} %get-tuple-element.27.table_ref, bf16[32,768]{1,0:T(8,128)(2,1)S(1)} %get-tuple-element.28.packed_ref), custom_call_target="tpu_custom_call" | custom-call | tf_op jit(solution)/shard_map/own/pallas_call | solution.py:256
  9.0 0.0 collective-permute-done.2
  9.0 0.7 %meet.1 = (f32[16,768]{1,0:T(8,128)S(1)}, bf16[64,768]{1,0:T(8,128)(2,1)S(1)}) custom-call(s32[2,1]{1,0:T(2,128)S(4)} %get-tuple-element.29.masks_ref, bf16[64,768]{1,0:T(8,128)(2,1)S(1)} %get-tuple-element.30.side_ref, bf16[1,32,768]{2,1,0:T(8,128)(2,1)S(1)} %bitcast.10, f32[16,768]{1,0:T(8,128)S(1)} %get-tuple-element.33.before_ref), custom_call_target="tpu_custom_call", output_to_operand_aliasing={{0}: (3, {})} | custom-call | tf_op jit(solution)/shard_map/meet/pallas_call | solution.py:256
  9.7 0.0 collective-permute-done.1
  9.7 1.0 %collective-permute-done = bf16[32,768]{1,0:T(8,128)(2,1)S(1)} collective-permute-done((bf16[32,768]{1,0:T(8,128)(2,1)S(1)}, bf16[32,768]{1,0:T(8,128)(2,1)S(1)}, u32[]{:S(2)}, u32[]{:S(2)}) %collective-permute-start) | collective-permute-done | bytes 49184 | tf_op jit(solution)/shard_map/ppermute | solution.py:236
  10.7 0.2 collective-permute-start.3
  10.9 0.7 %partner.1.before_ref = f32[16,768]{1,0:T(8,128)S(1)} custom-call(s32[2,1]{1,0:T(2,128)S(4)} %get-tuple-element.29.masks_ref, bf16[64,768]{1,0:T(8,128)(2,1)S(1)} %get-tuple-element.37.side_ref, bf16[4,32,768]{2,1,0:T(8,128)(2,1)S(1)} %pad_maximum_fusion.blocks_ref), custom_call_target="tpu_custom_call" | custom-call | tf_op jit(solution)/shard_map/partner/pallas_call | solution.py:256
  11.6 1.5 %collective-permute-done.4 = bf16[32,768]{1,0:T(8,128)(2,1)S(1)} collective-permute-done((bf16[32,768]{1,0:T(8,128)(2,1)S(1)}, bf16[32,768]{1,0:T(8,128)(2,1)S(1)}, u32[]{:S(2)}, u32[]{:S(2)}) %collective-permute-start.4) | collective-permute-done | bytes 49184 | tf_op jit(solution)/shard_map/ppermute | solution.py:236
  13.1 0.7 %collective-permute-start.5 = (bf16[1,32,768]{2,1,0:T(8,128)(2,1)S(1)}, bf16[1,32,768]{2,1,0:T(8,128)(2,1)S(1)}, u32[]{:S(2)}, u32[]{:S(2)}) collective-permute-start(bf16[1,32,768]{2,1,0:T(8,128)(2,1)S(1)} %bitcast.12), channel_id=1, source_target_pairs={{0,1},{1,0},{2,3},{3,2},{4,5},{5,4},{6,7},{7,6},{8,9},{9,8},{10,11... | collective-permute-start | bytes 147464 | tf_op jit(solution)/shard_map/ppermute | solution.py:236
  13.8 0.0 collective-permute-done.3
  13.8 0.1 partner_middle.1.before_ref
  13.9 0.8 %collective-permute-done.5.blocks_ref = bf16[1,32,768]{2,1,0:T(8,128)(2,1)S(1)} collective-permute-done((bf16[1,32,768]{2,1,0:T(8,128)(2,1)S(1)}, bf16[1,32,768]{2,1,0:T(8,128)(2,1)S(1)}, u32[]{:S(2)}, u32[]{:S(2)}) %collective-permute-start.5) | collective-permute-done | bytes 49184 | tf_op jit(solution)/shard_map/ppermute | solution.py:236
  14.7 0.5 %collective-permute-start.6 = (f32[16,768]{1,0:T(8,128)S(1)}, f32[16,768]{1,0:T(8,128)S(1)}, u32[]{:S(2)}, u32[]{:S(2)}) collective-permute-start(f32[16,768]{1,0:T(8,128)S(1)} %partner_late.1), channel_id=1, source_target_pairs={{0,3},{1,2},{2,1},{3,0},{4,7},{5,6},{6,5},{7,4},{8,11},{9,10},{10,... | collective-permute-start | bytes 147464 | tf_op jit(solution)/shard_map/ppermute | solution.py:236
  15.2 2.8 %add_own.1.refs_0_ = f32[16,768]{1,0:T(8,128)S(1)} custom-call(s32[2,1]{1,0:T(2,128)S(4)} %get-tuple-element.29.masks_ref, bf16[64,768]{1,0:T(8,128)(2,1)S(1)} %get-tuple-element.30.side_ref, bf16[8,32,768]{2,1,0:T(8,128)(2,1)S(1)} %constant_dynamic-update-slice_fusion.blocks_ref, ...), custom_call_target="tpu_custom_call", output_to_operand_aliasing={{}: (3, {})} | custom-call | tf_op jit(solution)/shard_map/add_own/pallas_call | solution.py:256
  18.0 0.1 collective-permute-done.6.refs_1_
  18.2 0.4 %last.1 = (f32[16,768]{1,0:T(8,128)S(1)}, f32[16,8,128]{2,1,0:T(8,128)S(1)}) custom-call(bf16[16,768]{1,0:T(8,128)(2,1)S(1)} %get-tuple-element.25.vectors_ref, f32[1,768]{1,0:T(1,128)S(1)} %get-tuple-element.26.root_ref, f32[16,768]{1,0:T(8,128)S(1)} %add_own.1.refs_0_, f32[16,768]{1,0:T(8,128)S(1)} %collective-permute-done.6.refs_1_), custom_call_target="tpu_custom_call" | custom-call | tf_op jit(solution)/shard_map/last/pallas_call | solution.py:256
  18.5 11.1 %all_to_all.5.grams_ref = f32[16,8,128]{2,1,0:T(8,128)S(1)} all-to-all(f32[16,8,128]{2,1,0:T(8,128)S(1)} %get-tuple-element.46), channel_id=1, replica_groups=mesh['grp'=2,'row'=4,'col'=4] {'row','col'}, dimensions={0} | all-to-all | bytes 131072 | tf_op jit(solution)/shard_map/all_to_all | solution.py:380
  29.7 1.3 %finish.1 = (f32[16,768]{1,0:T(8,128)}, f32[16,16]{1,0:T(8,128)}) custom-call(f32[16,8,128]{2,1,0:T(8,128)S(1)} %all_to_all.5.grams_ref, f32[16,768]{1,0:T(8,128)S(1)} %get-tuple-element.47.applied_ref), custom_call_target="tpu_custom_call" | custom-call | tf_op jit(solution)/shard_map/finish/pallas_call | solution.py:256
  (9 shorter events, 0.1 us)
Async XLA Ops:
  1.4 7.5 %collective-permute-start.2 = (bf16[32,768]{1,0:T(8,128)(2,1)S(1)}, bf16[32,768]{1,0:T(8,128)(2,1)S(1)}, u32[]{:S(2)}, u32[]{:S(2)}) collective-permute-start(bf16[32,768]{1,0:T(8,128)(2,1)S(1)} %get-tuple-element.28.packed_ref), channel_id=1, source_target_pairs={{0,3},{1,2},{2,1},{3,0},{4,7},{5,6},{6,5},{7,4},{8,11},{9,10},{10,... | collective-permute-start | bytes 147464 | tf_op jit(solution)/shard_map/ppermute | solution.py:236
  3.9 5.8 %collective-permute-start.1 = (bf16[32,768]{1,0:T(8,128)(2,1)S(1)}, bf16[32,768]{1,0:T(8,128)(2,1)S(1)}, u32[]{:S(2)}, u32[]{:S(2)}) collective-permute-start(bf16[32,768]{1,0:T(8,128)(2,1)S(1)} %get-tuple-element.28.packed_ref), channel_id=1, source_target_pairs={{0,9},{1,8},{2,11},{3,10},{4,13},{5,12},{6,15},{7,14},{8,1},{9,0},... | collective-permute-start | bytes 147464 | tf_op jit(solution)/shard_map/ppermute | solution.py:236
  6.8 3.9 %collective-permute-start = (bf16[32,768]{1,0:T(8,128)(2,1)S(1)}, bf16[32,768]{1,0:T(8,128)(2,1)S(1)}, u32[]{:S(2)}, u32[]{:S(2)}) collective-permute-start(bf16[32,768]{1,0:T(8,128)(2,1)S(1)} %get-tuple-element.28.packed_ref), channel_id=1, source_target_pairs={{0,5},{1,4},{2,7},{3,6},{4,1},{5,0},{6,3},{7,2},{8,13},{9,12},{10,... | collective-permute-start | bytes 147464 | tf_op jit(solution)/shard_map/ppermute | solution.py:236
  7.8 5.3 %collective-permute-start.4 = (bf16[32,768]{1,0:T(8,128)(2,1)S(1)}, bf16[32,768]{1,0:T(8,128)(2,1)S(1)}, u32[]{:S(2)}, u32[]{:S(2)}) collective-permute-start(bf16[32,768]{1,0:T(8,128)(2,1)S(1)} %get-tuple-element.28.packed_ref), channel_id=1, source_target_pairs={{0,13},{1,12},{2,15},{3,14},{4,9},{5,8},{6,11},{7,10},{8,5},{9,4},... | collective-permute-start | bytes 147464 | tf_op jit(solution)/shard_map/ppermute | solution.py:236
  10.7 3.0 %collective-permute-start.3 = (bf16[4,32,768]{2,1,0:T(8,128)(2,1)S(1)}, bf16[4,32,768]{2,1,0:T(8,128)(2,1)S(1)}, u32[]{:S(2)}, u32[]{:S(2)}) collective-permute-start(bf16[4,32,768]{2,1,0:T(8,128)(2,1)S(1)} %pad_maximum_fusion.blocks_ref), channel_id=1, source_target_pairs={{0,1},{1,0},{2,3},{3,2},{4,5},{5,4},{6,7},{7,6},{8,9},{9,8},{10,11... | collective-permute-start | bytes 589832 | tf_op jit(solution)/shard_map/ppermute | solution.py:236
  13.1 1.6 %collective-permute-start.5 = (bf16[1,32,768]{2,1,0:T(8,128)(2,1)S(1)}, bf16[1,32,768]{2,1,0:T(8,128)(2,1)S(1)}, u32[]{:S(2)}, u32[]{:S(2)}) collective-permute-start(bf16[1,32,768]{2,1,0:T(8,128)(2,1)S(1)} %bitcast.12), channel_id=1, source_target_pairs={{0,1},{1,0},{2,3},{3,2},{4,5},{5,4},{6,7},{7,6},{8,9},{9,8},{10,11... | collective-permute-start | bytes 147464 | tf_op jit(solution)/shard_map/ppermute | solution.py:236
  14.7 3.5 %collective-permute-start.6 = (f32[16,768]{1,0:T(8,128)S(1)}, f32[16,768]{1,0:T(8,128)S(1)}, u32[]{:S(2)}, u32[]{:S(2)}) collective-permute-start(f32[16,768]{1,0:T(8,128)S(1)} %partner_late.1), channel_id=1, source_target_pairs={{0,3},{1,2},{2,1},{3,0},{4,7},{5,6},{6,5},{7,4},{8,11},{9,10},{10,... | collective-permute-start | bytes 147464 | tf_op jit(solution)/shard_map/ppermute | solution.py:236

commit v10 on v8

--- a/solution.py
+++ b/solution.py
@@ -103,24 +103,20 @@
         blocks = [blocks_ref[list_ref[start + k]] for k in range(size)]
         image_ref[...] += tile_image(side_ref, blocks)
 
-    def add_triple(group, _):
-        add_group(3 * group, 3)
+    fours = jnp.maximum(count // 4 - (count % 4 == 1).astype(jnp.int32), 0)
+    rest = count - 4 * fours
+
+    def add_four(group, _):
+        add_group(4 * group, 4)
         return 0
 
-    def add_pair(group, _):
-        add_group(3 * triples + 2 * group, 2)
-        return 0
-
-    triples = jnp.maximum(count // 3 - (count % 3 == 1).astype(jnp.int32), 0)
-    rest = count - 3 * triples
+    if len(places) >= 4:
+        lax.fori_loop(0, fours, add_four, 0)
     if len(places) >= 3:
-        lax.fori_loop(0, triples, add_triple, 0)
+        pl.when(rest >= 3)(lambda: add_group(4 * fours, 3))
     if len(places) >= 2:
-        lax.fori_loop(0, rest // 2, add_pair, 0)
-
-    @pl.when(rest == 1)
-    def _():
-        add_group(0, 1)
+        pl.when(rest % 3 == 2)(lambda: add_group(count - 2, 2))
+    pl.when(rest == 1)(lambda: add_group(count - 1, 1))
 
 
 def meet_kernel(

time: 32 us -> 31.7 us (level)
  waiting for transfers between devices: 4.2 us -> 5.36 us
  blocking collectives: 11.7 us -> 10.6 us
  starting transfers between devices: 8.51 us -> 8.01 us
    ppermute x7, waiting for transfers between devices: 4.2 us -> 5.36 us  [sent(): return lax.ppermute(x, ('row', 'col'), pairs)]
    all_to_all x1, blocking collectives: 11.7 us -> 10.6 us  [per_device(): grams = lax.all_to_all(gram, ('row', 'col'), 0, 0)]
    ppermute x7, starting transfers between devices: 8.51 us -> 8.01 us  [sent(): return lax.ppermute(x, ('row', 'col'), pairs)]
  transfers between devices with their start and end apart: 7 -> 7, of which waited for: 3 -> 3; matrix products, arithmetic and copies ran while one was open for 0% -> 0% of each run, Pallas kernels for 13% -> 14%
where the time goes in v10:
time: 31.7 us; the launch traced here: 31.5 us
  blocking collectives  10.6 us (33%)
  starting transfers between devices  8.01 us (25%)
  Pallas kernels  6.74 us (21%)
  waiting for transfers between devices  5.36 us (17%)
  between operations  0.73 us (2%)
    all_to_all x1, blocking collectives, per_device(): grams = lax.all_to_all(gram, ('row', 'col'), 0, 0)  10.6 us
    ppermute x7, starting transfers between devices, sent(): return lax.ppermute(x, ('row', 'col'), pairs)  8.01 us
    pallas_call x9, Pallas kernels, call(): pl.pallas_call(kernel, out_shape=shapes, in_specs=where, out_specs=to, co...  6.74 us
    ppermute x7, waiting for transfers between devices, sent(): return lax.ppermute(x, ('row', 'col'), pairs)  5.36 us
  transfers between devices with their start and end apart: 7, of which 3 were waited for; matrix products, arithmetic and copies ran while one was open for 0% of the time, Pallas kernels for 14%

profile of v10, /device:TPU:0, one launch (start us, length us, event | category | flops | bytes accessed | tf_op | source)
XLA Modules:
  0.0 31.5 jit_solution(18135383244939366000)
XLA Ops:
  0.6 0.8 %pack.1 = (bf16[32,768]{1,0:T(8,128)(2,1)S(1)}, bf16[16,768]{1,0:T(8,128)(2,1)S(1)}, f32[1,768]{1,0:T(1,128)S(1)}, s32[8,2,16]{2,1,0:T(2,128)S(1)}) custom-call(bf16[16,768]{1,0:T(8,128)(2,1)} %frames_ref.1, bf16[16,768]{1,0:T(8,128)(2,1)} %vectors_in.1, f32[768]{0:T(1024)} %degrees_ref.1, s32[8,2,16]{2,1,0:T(2,128)} %bitcast.16), custom_call_target="tpu_custom_call" | custom-call | tf_op jit(solution)/shard_map/pack/pallas_call | solution.py:240
  1.4 2.4 %collective-permute-start.2 = (bf16[32,768]{1,0:T(8,128)(2,1)S(1)}, bf16[32,768]{1,0:T(8,128)(2,1)S(1)}, u32[]{:S(2)}, u32[]{:S(2)}) collective-permute-start(bf16[32,768]{1,0:T(8,128)(2,1)S(1)} %get-tuple-element.28.packed_ref), channel_id=1, source_target_pairs={{0,3},{1,2},{2,1},{3,0},{4,7},{5,6},{6,5},{7,4},{8,11},{9,10},{10,... | collective-permute-start | bytes 147464 | tf_op jit(solution)/shard_map/ppermute | solution.py:220
  3.9 2.9 %collective-permute-start.1 = (bf16[32,768]{1,0:T(8,128)(2,1)S(1)}, bf16[32,768]{1,0:T(8,128)(2,1)S(1)}, u32[]{:S(2)}, u32[]{:S(2)}) collective-permute-start(bf16[32,768]{1,0:T(8,128)(2,1)S(1)} %get-tuple-element.28.packed_ref), channel_id=1, source_target_pairs={{0,9},{1,8},{2,11},{3,10},{4,13},{5,12},{6,15},{7,14},{8,1},{9,0},... | collective-permute-start | bytes 147464 | tf_op jit(solution)/shard_map/ppermute | solution.py:220
  6.8 1.0 %collective-permute-start = (bf16[32,768]{1,0:T(8,128)(2,1)S(1)}, bf16[32,768]{1,0:T(8,128)(2,1)S(1)}, u32[]{:S(2)}, u32[]{:S(2)}) collective-permute-start(bf16[32,768]{1,0:T(8,128)(2,1)S(1)} %get-tuple-element.28.packed_ref), channel_id=1, source_target_pairs={{0,5},{1,4},{2,7},{3,6},{4,1},{5,0},{6,3},{7,2},{8,13},{9,12},{10,... | collective-permute-start | bytes 147464 | tf_op jit(solution)/shard_map/ppermute | solution.py:220
  7.8 0.5 %collective-permute-start.4 = (bf16[32,768]{1,0:T(8,128)(2,1)S(1)}, bf16[32,768]{1,0:T(8,128)(2,1)S(1)}, u32[]{:S(2)}, u32[]{:S(2)}) collective-permute-start(bf16[32,768]{1,0:T(8,128)(2,1)S(1)} %get-tuple-element.28.packed_ref), channel_id=1, source_target_pairs={{0,13},{1,12},{2,15},{3,14},{4,9},{5,8},{6,11},{7,10},{8,5},{9,4},... | collective-permute-start | bytes 147464 | tf_op jit(solution)/shard_map/ppermute | solution.py:220
  8.3 0.7 %own.1 = (bf16[64,768]{1,0:T(8,128)(2,1)S(1)}, f32[16,768]{1,0:T(8,128)S(1)}, s32[2,1]{1,0:T(2,128)S(4)}) custom-call(s32[8,2,16]{2,1,0:T(2,128)S(1)} %get-tuple-element.27.table_ref, bf16[32,768]{1,0:T(8,128)(2,1)S(1)} %get-tuple-element.28.packed_ref), custom_call_target="tpu_custom_call" | custom-call | tf_op jit(solution)/shard_map/own/pallas_call | solution.py:240
  9.0 0.0 collective-permute-done.2
  9.1 0.0 collective-permute-done.1
  9.1 1.6 %collective-permute-done = bf16[32,768]{1,0:T(8,128)(2,1)S(1)} collective-permute-done((bf16[32,768]{1,0:T(8,128)(2,1)S(1)}, bf16[32,768]{1,0:T(8,128)(2,1)S(1)}, u32[]{:S(2)}, u32[]{:S(2)}) %collective-permute-start) | collective-permute-done | bytes 49184 | tf_op jit(solution)/shard_map/ppermute | solution.py:220
  10.7 0.2 collective-permute-start.3
  10.9 0.7 %partner.1.before_ref = f32[16,768]{1,0:T(8,128)S(1)} custom-call(s32[2,1]{1,0:T(2,128)S(4)} %get-tuple-element.29.masks_ref, bf16[64,768]{1,0:T(8,128)(2,1)S(1)} %get-tuple-element.37.side_ref, bf16[4,32,768]{2,1,0:T(8,128)(2,1)S(1)} %pad_maximum_fusion.blocks_ref), custom_call_target="tpu_custom_call" | custom-call | tf_op jit(solution)/shard_map/partner/pallas_call | solution.py:240
  11.6 1.5 %collective-permute-done.4 = bf16[32,768]{1,0:T(8,128)(2,1)S(1)} collective-permute-done((bf16[32,768]{1,0:T(8,128)(2,1)S(1)}, bf16[32,768]{1,0:T(8,128)(2,1)S(1)}, u32[]{:S(2)}, u32[]{:S(2)}) %collective-permute-start.4) | collective-permute-done | bytes 49184 | tf_op jit(solution)/shard_map/ppermute | solution.py:220
  13.1 0.7 %collective-permute-start.5 = (bf16[1,32,768]{2,1,0:T(8,128)(2,1)S(1)}, bf16[1,32,768]{2,1,0:T(8,128)(2,1)S(1)}, u32[]{:S(2)}, u32[]{:S(2)}) collective-permute-start(bf16[1,32,768]{2,1,0:T(8,128)(2,1)S(1)} %bitcast.12), channel_id=1, source_target_pairs={{0,1},{1,0},{2,3},{3,2},{4,5},{5,4},{6,7},{7,6},{8,9},{9,8},{10,11... | collective-permute-start | bytes 147464 | tf_op jit(solution)/shard_map/ppermute | solution.py:220
  13.8 0.0 collective-permute-done.3
  13.8 1.6 %partner_middle.1.before_ref = f32[16,768]{1,0:T(8,128)S(1)} custom-call(s32[2,1]{1,0:T(2,128)S(4)} %get-tuple-element.29.masks_ref, bf16[64,768]{1,0:T(8,128)(2,1)S(1)} %get-tuple-element.37.side_ref, bf16[3,32,768]{2,1,0:T(8,128)(2,1)S(1)} %pad_maximum_fusion.1.blocks_ref, f32[16,768]{1,0:T(8,128)S(1)} %partner.1.before_ref), custom_call_target="tpu_custom_call", output_to_operand_aliasing={{}: (3, {})} | custom-call | tf_op jit(solution)/shard_map/partner_middle/pallas_call | solution.py:240
  15.4 0.0 collective-permute-done.5.blocks_ref
  15.5 0.3 %collective-permute-start.6 = (f32[16,768]{1,0:T(8,128)S(1)}, f32[16,768]{1,0:T(8,128)S(1)}, u32[]{:S(2)}, u32[]{:S(2)}) collective-permute-start(f32[16,768]{1,0:T(8,128)S(1)} %partner_late.1), channel_id=1, source_target_pairs={{0,3},{1,2},{2,1},{3,0},{4,7},{5,6},{6,5},{7,4},{8,11},{9,10},{10,... | collective-permute-start | bytes 147464 | tf_op jit(solution)/shard_map/ppermute | solution.py:220
  15.9 1.2 %add_own.1.refs_0_ = f32[16,768]{1,0:T(8,128)S(1)} custom-call(s32[2,1]{1,0:T(2,128)S(4)} %get-tuple-element.29.masks_ref, bf16[64,768]{1,0:T(8,128)(2,1)S(1)} %get-tuple-element.30.side_ref, bf16[8,32,768]{2,1,0:T(8,128)(2,1)S(1)} %constant_dynamic-update-slice_fusion.blocks_ref, ...), custom_call_target="tpu_custom_call", output_to_operand_aliasing={{}: (3, {})} | custom-call | tf_op jit(solution)/shard_map/add_own/pallas_call | solution.py:240
  17.1 2.2 %collective-permute-done.6.refs_1_ = f32[16,768]{1,0:T(8,128)S(1)} collective-permute-done((f32[16,768]{1,0:T(8,128)S(1)}, f32[16,768]{1,0:T(8,128)S(1)}, u32[]{:S(2)}, u32[]{:S(2)}) %collective-permute-start.6) | collective-permute-done | bytes 49184 | tf_op jit(solution)/shard_map/ppermute | solution.py:220
  19.3 0.4 %last.1 = (f32[16,768]{1,0:T(8,128)S(1)}, f32[16,8,128]{2,1,0:T(8,128)S(1)}) custom-call(bf16[16,768]{1,0:T(8,128)(2,1)S(1)} %get-tuple-element.25.vectors_ref, f32[1,768]{1,0:T(1,128)S(1)} %get-tuple-element.26.root_ref, f32[16,768]{1,0:T(8,128)S(1)} %add_own.1.refs_0_, f32[16,768]{1,0:T(8,128)S(1)} %collective-permute-done.6.refs_1_), custom_call_target="tpu_custom_call" | custom-call | tf_op jit(solution)/shard_map/last/pallas_call | solution.py:240
  19.7 10.6 %all_to_all.5.grams_ref = f32[16,8,128]{2,1,0:T(8,128)S(1)} all-to-all(f32[16,8,128]{2,1,0:T(8,128)S(1)} %get-tuple-element.46), channel_id=1, replica_groups=mesh['grp'=2,'row'=4,'col'=4] {'row','col'}, dimensions={0} | all-to-all | bytes 131072 | tf_op jit(solution)/shard_map/all_to_all | solution.py:364
  30.2 1.3 %finish.1 = (f32[16,768]{1,0:T(8,128)}, f32[16,16]{1,0:T(8,128)}) custom-call(f32[16,8,128]{2,1,0:T(8,128)S(1)} %all_to_all.5.grams_ref, f32[16,768]{1,0:T(8,128)S(1)} %get-tuple-element.47.applied_ref), custom_call_target="tpu_custom_call" | custom-call | tf_op jit(solution)/shard_map/finish/pallas_call | solution.py:240
  (10 shorter events, 0.2 us)
Async XLA Ops:
  1.4 7.5 %collective-permute-start.2 = (bf16[32,768]{1,0:T(8,128)(2,1)S(1)}, bf16[32,768]{1,0:T(8,128)(2,1)S(1)}, u32[]{:S(2)}, u32[]{:S(2)}) collective-permute-start(bf16[32,768]{1,0:T(8,128)(2,1)S(1)} %get-tuple-element.28.packed_ref), channel_id=1, source_target_pairs={{0,3},{1,2},{2,1},{3,0},{4,7},{5,6},{6,5},{7,4},{8,11},{9,10},{10,... | collective-permute-start | bytes 147464 | tf_op jit(solution)/shard_map/ppermute | solution.py:220
  3.9 5.2 %collective-permute-start.1 = (bf16[32,768]{1,0:T(8,128)(2,1)S(1)}, bf16[32,768]{1,0:T(8,128)(2,1)S(1)}, u32[]{:S(2)}, u32[]{:S(2)}) collective-permute-start(bf16[32,768]{1,0:T(8,128)(2,1)S(1)} %get-tuple-element.28.packed_ref), channel_id=1, source_target_pairs={{0,9},{1,8},{2,11},{3,10},{4,13},{5,12},{6,15},{7,14},{8,1},{9,0},... | collective-permute-start | bytes 147464 | tf_op jit(solution)/shard_map/ppermute | solution.py:220
  6.8 3.9 %collective-permute-start = (bf16[32,768]{1,0:T(8,128)(2,1)S(1)}, bf16[32,768]{1,0:T(8,128)(2,1)S(1)}, u32[]{:S(2)}, u32[]{:S(2)}) collective-permute-start(bf16[32,768]{1,0:T(8,128)(2,1)S(1)} %get-tuple-element.28.packed_ref), channel_id=1, source_target_pairs={{0,5},{1,4},{2,7},{3,6},{4,1},{5,0},{6,3},{7,2},{8,13},{9,12},{10,... | collective-permute-start | bytes 147464 | tf_op jit(solution)/shard_map/ppermute | solution.py:220
  7.8 5.3 %collective-permute-start.4 = (bf16[32,768]{1,0:T(8,128)(2,1)S(1)}, bf16[32,768]{1,0:T(8,128)(2,1)S(1)}, u32[]{:S(2)}, u32[]{:S(2)}) collective-permute-start(bf16[32,768]{1,0:T(8,128)(2,1)S(1)} %get-tuple-element.28.packed_ref), channel_id=1, source_target_pairs={{0,13},{1,12},{2,15},{3,14},{4,9},{5,8},{6,11},{7,10},{8,5},{9,4},... | collective-permute-start | bytes 147464 | tf_op jit(solution)/shard_map/ppermute | solution.py:220
  10.7 3.0 %collective-permute-start.3 = (bf16[4,32,768]{2,1,0:T(8,128)(2,1)S(1)}, bf16[4,32,768]{2,1,0:T(8,128)(2,1)S(1)}, u32[]{:S(2)}, u32[]{:S(2)}) collective-permute-start(bf16[4,32,768]{2,1,0:T(8,128)(2,1)S(1)} %pad_maximum_fusion.blocks_ref), channel_id=1, source_target_pairs={{0,1},{1,0},{2,3},{3,2},{4,5},{5,4},{6,7},{7,6},{8,9},{9,8},{10,11... | collective-permute-start | bytes 589832 | tf_op jit(solution)/shard_map/ppermute | solution.py:220
  13.1 2.3 %collective-permute-start.5 = (bf16[1,32,768]{2,1,0:T(8,128)(2,1)S(1)}, bf16[1,32,768]{2,1,0:T(8,128)(2,1)S(1)}, u32[]{:S(2)}, u32[]{:S(2)}) collective-permute-start(bf16[1,32,768]{2,1,0:T(8,128)(2,1)S(1)} %bitcast.12), channel_id=1, source_target_pairs={{0,1},{1,0},{2,3},{3,2},{4,5},{5,4},{6,7},{7,6},{8,9},{9,8},{10,11... | collective-permute-start | bytes 147464 | tf_op jit(solution)/shard_map/ppermute | solution.py:220
  15.5 3.8 %collective-permute-start.6 = (f32[16,768]{1,0:T(8,128)S(1)}, f32[16,768]{1,0:T(8,128)S(1)}, u32[]{:S(2)}, u32[]{:S(2)}) collective-permute-start(f32[16,768]{1,0:T(8,128)S(1)} %partner_late.1), channel_id=1, source_target_pairs={{0,3},{1,2},{2,1},{3,0},{4,7},{5,6},{6,5},{7,4},{8,11},{9,10},{10,... | collective-permute-start | bytes 147464 | tf_op jit(solution)/shard_map/ppermute | solution.py:220

commit v11 on v10

--- a/solution.py
+++ b/solution.py
@@ -119,12 +119,8 @@
     pl.when(rest == 1)(lambda: add_group(count - 1, 1))
 
 
-def meet_kernel(
-    places, sizes, masks_ref, side_ref, blocks_ref, before_ref, image_ref, partner_side_ref, list_ref
-):
-    partner_side_ref[...] = own_side(blocks_ref[0, : blocks_ref.shape[1] // 2, :])
-    image_ref[...] = before_ref[...]
-    add_blocks(0, places, sizes, masks_ref, side_ref, blocks_ref, image_ref, list_ref)
+def side_kernel(block_ref, side_ref):
+    side_ref[...] = own_side(block_ref[: block_ref.shape[0] // 2, :])
 
 
 def first_kernel(target, places, sizes, masks_ref, side_ref, blocks_ref, image_ref, list_ref):
@@ -315,20 +311,8 @@
         to=[vmem, vmem, smem],
     )
     met, image = lax.optimization_barrier((met, image))
-    sides = []
-    for hop, block in zip(partners, met):
-        image, partner_side = call_blocks(
-            meet_kernel,
-            "meet",
-            [image_type, side_type],
-            [hop],
-            side,
-            block[None],
-            image,
-            input_output_aliases={3: 0},
-        )
-        sides.append(partner_side)
-    early, image = lax.optimization_barrier((line[1:], image))
+    sides = [call(side_kernel, "side", [side_type], block)[0] for block in met]
+    early, sides = lax.optimization_barrier((line[1:], sides))
     held, held_at = early + met + [packed], lines[1:] + partners + [(0, 0)]
     near = jnp.stack(held)
     other = sent(near, core)
@@ -349,8 +333,8 @@
         )
     parts, image = lax.optimization_barrier((parts, image))
     received = [sent(part, hop) for hop, part in zip(partners, parts)]
-    own_places = lines[1:] + beyond(held_at, core) + lines[:1] + beyond(lines[:1], core)
-    blocks = jnp.concatenate([near[: n_row - 2], other, late, other_late])
+    own_places = held_at[:-1] + beyond(held_at, core) + lines[:1] + beyond(lines[:1], core)
+    blocks = jnp.concatenate([near[:-1], other, late, other_late])
     image = add_part("add_own", (0, 0), own_places, side, blocks, image)
     applied, gram = call(
         last_kernel,

time: 31.7 us -> 31.2 us (0.984)
  Pallas kernels: 6.74 us -> 8.31 us
  waiting for transfers between devices: 5.36 us -> 3.89 us
  blocking collectives: 10.6 us -> 9.98 us
    pallas_call x9, Pallas kernels: 6.74 us -> 8.31 us  [call(): pl.pallas_call(kernel, out_shape=shapes, in_specs=where, out_specs=to, co...]
    ppermute x7, waiting for transfers between devices: 5.36 us -> 3.89 us  [sent(): return lax.ppermute(x, ('row', 'col'), pairs)]
    all_to_all x1, blocking collectives: 10.6 us -> 9.98 us  [per_device(): grams = lax.all_to_all(gram, ('row', 'col'), 0, 0)]
  transfers between devices with their start and end apart: 7 -> 7, of which waited for: 3 -> 3; matrix products, arithmetic and copies ran while one was open for 0% -> 0% of each run, Pallas kernels for 14% -> 17%
where the time goes in v11:
time: 31.2 us; the launch traced here: 31.3 us
  blocking collectives  9.98 us (32%)
  Pallas kernels  8.31 us (27%)
  starting transfers between devices  8.26 us (26%)
  waiting for transfers between devices  3.89 us (12%)
  between operations  0.74 us (2%)
    all_to_all x1, blocking collectives, per_device(): grams = lax.all_to_all(gram, ('row', 'col'), 0, 0)  9.98 us
    pallas_call x9, Pallas kernels, call(): pl.pallas_call(kernel, out_shape=shapes, in_specs=where, out_specs=to, co...  8.31 us
    ppermute x7, starting transfers between devices, sent(): return lax.ppermute(x, ('row', 'col'), pairs)  8.26 us
    ppermute x7, waiting for transfers between devices, sent(): return lax.ppermute(x, ('row', 'col'), pairs)  3.89 us
  transfers between devices with their start and end apart: 7, of which 3 were waited for; matrix products, arithmetic and copies ran while one was open for 0% of the time, Pallas kernels for 17%

profile of v11, /device:TPU:0, one launch (start us, length us, event | category | flops | bytes accessed | tf_op | source)
XLA Modules:
  0.0 31.3 jit_solution(17134732680567928553)
XLA Ops:
  0.6 0.8 %pack.1 = (bf16[32,768]{1,0:T(8,128)(2,1)S(1)}, bf16[16,768]{1,0:T(8,128)(2,1)S(1)}, f32[1,768]{1,0:T(1,128)S(1)}, s32[8,2,16]{2,1,0:T(2,128)S(1)}) custom-call(bf16[16,768]{1,0:T(8,128)(2,1)} %frames_ref.1, bf16[16,768]{1,0:T(8,128)(2,1)} %vectors_in.1, f32[768]{0:T(1024)} %degrees_ref.1, s32[8,2,16]{2,1,0:T(2,128)} %bitcast.16), custom_call_target="tpu_custom_call" | custom-call | tf_op jit(solution)/shard_map/pack/pallas_call | solution.py:236
  1.4 2.4 %collective-permute-start.2 = (bf16[32,768]{1,0:T(8,128)(2,1)S(1)}, bf16[32,768]{1,0:T(8,128)(2,1)S(1)}, u32[]{:S(2)}, u32[]{:S(2)}) collective-permute-start(bf16[32,768]{1,0:T(8,128)(2,1)S(1)} %get-tuple-element.26.packed_ref), channel_id=1, source_target_pairs={{0,3},{1,2},{2,1},{3,0},{4,7},{5,6},{6,5},{7,4},{8,11},{9,10},{10,... | collective-permute-start | bytes 147464 | tf_op jit(solution)/shard_map/ppermute | solution.py:216
  3.9 2.9 %collective-permute-start.1 = (bf16[32,768]{1,0:T(8,128)(2,1)S(1)}, bf16[32,768]{1,0:T(8,128)(2,1)S(1)}, u32[]{:S(2)}, u32[]{:S(2)}) collective-permute-start(bf16[32,768]{1,0:T(8,128)(2,1)S(1)} %get-tuple-element.26.packed_ref), channel_id=1, source_target_pairs={{0,9},{1,8},{2,11},{3,10},{4,13},{5,12},{6,15},{7,14},{8,1},{9,0},... | collective-permute-start | bytes 147464 | tf_op jit(solution)/shard_map/ppermute | solution.py:216
  6.8 1.0 %collective-permute-start = (bf16[32,768]{1,0:T(8,128)(2,1)S(1)}, bf16[32,768]{1,0:T(8,128)(2,1)S(1)}, u32[]{:S(2)}, u32[]{:S(2)}) collective-permute-start(bf16[32,768]{1,0:T(8,128)(2,1)S(1)} %get-tuple-element.26.packed_ref), channel_id=1, source_target_pairs={{0,5},{1,4},{2,7},{3,6},{4,1},{5,0},{6,3},{7,2},{8,13},{9,12},{10,... | collective-permute-start | bytes 147464 | tf_op jit(solution)/shard_map/ppermute | solution.py:216
  7.8 0.5 %collective-permute-start.4 = (bf16[32,768]{1,0:T(8,128)(2,1)S(1)}, bf16[32,768]{1,0:T(8,128)(2,1)S(1)}, u32[]{:S(2)}, u32[]{:S(2)}) collective-permute-start(bf16[32,768]{1,0:T(8,128)(2,1)S(1)} %get-tuple-element.26.packed_ref), channel_id=1, source_target_pairs={{0,13},{1,12},{2,15},{3,14},{4,9},{5,8},{6,11},{7,10},{8,5},{9,4},... | collective-permute-start | bytes 147464 | tf_op jit(solution)/shard_map/ppermute | solution.py:216
  8.3 0.7 %own.1 = (bf16[64,768]{1,0:T(8,128)(2,1)S(1)}, f32[16,768]{1,0:T(8,128)S(1)}, s32[2,1]{1,0:T(2,128)S(4)}) custom-call(s32[8,2,16]{2,1,0:T(2,128)S(1)} %get-tuple-element.25.table_ref, bf16[32,768]{1,0:T(8,128)(2,1)S(1)} %get-tuple-element.26.packed_ref), custom_call_target="tpu_custom_call" | custom-call | tf_op jit(solution)/shard_map/own/pallas_call | solution.py:236
  9.0 0.0 collective-permute-done.2.block_ref
  9.0 0.0 collective-permute-done.1
  9.0 1.7 %collective-permute-done = bf16[32,768]{1,0:T(8,128)(2,1)S(1)} collective-permute-done((bf16[32,768]{1,0:T(8,128)(2,1)S(1)}, bf16[32,768]{1,0:T(8,128)(2,1)S(1)}, u32[]{:S(2)}, u32[]{:S(2)}) %collective-permute-start) | collective-permute-done | bytes 49184 | tf_op jit(solution)/shard_map/ppermute | solution.py:216
  10.7 0.2 collective-permute-start.3
  10.9 0.7 %partner.1.before_ref = f32[16,768]{1,0:T(8,128)S(1)} custom-call(s32[2,1]{1,0:T(2,128)S(4)} %get-tuple-element.27.masks_ref, bf16[64,768]{1,0:T(8,128)(2,1)S(1)} %side.1.side_ref, bf16[4,32,768]{2,1,0:T(8,128)(2,1)S(1)} %pad_maximum_fusion.blocks_ref), custom_call_target="tpu_custom_call" | custom-call | tf_op jit(solution)/shard_map/partner/pallas_call | solution.py:236
  11.6 1.5 %collective-permute-done.4 = bf16[32,768]{1,0:T(8,128)(2,1)S(1)} collective-permute-done((bf16[32,768]{1,0:T(8,128)(2,1)S(1)}, bf16[32,768]{1,0:T(8,128)(2,1)S(1)}, u32[]{:S(2)}, u32[]{:S(2)}) %collective-permute-start.4) | collective-permute-done | bytes 49184 | tf_op jit(solution)/shard_map/ppermute | solution.py:216
  13.1 0.7 %collective-permute-start.5 = (bf16[1,32,768]{2,1,0:T(8,128)(2,1)S(1)}, bf16[1,32,768]{2,1,0:T(8,128)(2,1)S(1)}, u32[]{:S(2)}, u32[]{:S(2)}) collective-permute-start(bf16[1,32,768]{2,1,0:T(8,128)(2,1)S(1)} %bitcast.12), channel_id=1, source_target_pairs={{0,1},{1,0},{2,3},{3,2},{4,5},{5,4},{6,7},{7,6},{8,9},{9,8},{10,11... | collective-permute-start | bytes 147464 | tf_op jit(solution)/shard_map/ppermute | solution.py:216
  13.8 0.0 collective-permute-done.3
  13.8 0.1 partner_middle.1.before_ref
  13.9 0.7 %collective-permute-done.5.blocks_ref = bf16[1,32,768]{2,1,0:T(8,128)(2,1)S(1)} collective-permute-done((bf16[1,32,768]{2,1,0:T(8,128)(2,1)S(1)}, bf16[1,32,768]{2,1,0:T(8,128)(2,1)S(1)}, u32[]{:S(2)}, u32[]{:S(2)}) %collective-permute-start.5) | collective-permute-done | bytes 49184 | tf_op jit(solution)/shard_map/ppermute | solution.py:216
  14.6 0.7 %partner_late.1 = f32[16,768]{1,0:T(8,128)S(1)} custom-call(s32[2,1]{1,0:T(2,128)S(4)} %get-tuple-element.27.masks_ref, bf16[64,768]{1,0:T(8,128)(2,1)S(1)} %side.1.side_ref, bf16[1,32,768]{2,1,0:T(8,128)(2,1)S(1)} %collective-permute-done.5.blocks_ref, f32[16,768]{1,0:T(8,128)S(1)} %partner_middle.1.before_ref), custom_call_target="tpu_custom_call", output_to_operand_aliasing={{}: (3, {})} | custom-call | tf_op jit(solution)/shard_map/partner_late/pallas_call | solution.py:236
  15.3 0.6 %collective-permute-start.6 = (f32[16,768]{1,0:T(8,128)S(1)}, f32[16,768]{1,0:T(8,128)S(1)}, u32[]{:S(2)}, u32[]{:S(2)}) collective-permute-start(f32[16,768]{1,0:T(8,128)S(1)} %partner_late.1), channel_id=1, source_target_pairs={{0,3},{1,2},{2,1},{3,0},{4,7},{5,6},{6,5},{7,4},{8,11},{9,10},{10,... | collective-permute-start | bytes 147464 | tf_op jit(solution)/shard_map/ppermute | solution.py:216
  15.9 3.7 %add_own.1.refs_0_ = f32[16,768]{1,0:T(8,128)S(1)} custom-call(s32[2,1]{1,0:T(2,128)S(4)} %get-tuple-element.27.masks_ref, bf16[64,768]{1,0:T(8,128)(2,1)S(1)} %get-tuple-element.28.side_ref, bf16[9,32,768]{2,1,0:T(8,128)(2,1)S(1)} %constant_dynamic-update-slice_fusion.blocks_ref, ...), custom_call_target="tpu_custom_call", output_to_operand_aliasing={{}: (3, {})} | custom-call | tf_op jit(solution)/shard_map/add_own/pallas_call | solution.py:236
  19.7 0.0 collective-permute-done.6.refs_1_
  19.7 0.4 %last.1 = (f32[16,768]{1,0:T(8,128)S(1)}, f32[16,8,128]{2,1,0:T(8,128)S(1)}) custom-call(bf16[16,768]{1,0:T(8,128)(2,1)S(1)} %get-tuple-element.23.vectors_ref, f32[1,768]{1,0:T(1,128)S(1)} %get-tuple-element.24.root_ref, f32[16,768]{1,0:T(8,128)S(1)} %add_own.1.refs_0_, f32[16,768]{1,0:T(8,128)S(1)} %collective-permute-done.6.refs_1_), custom_call_target="tpu_custom_call" | custom-call | tf_op jit(solution)/shard_map/last/pallas_call | solution.py:236
  20.0 10.0 %all_to_all.5.grams_ref = f32[16,8,128]{2,1,0:T(8,128)S(1)} all-to-all(f32[16,8,128]{2,1,0:T(8,128)S(1)} %get-tuple-element.42), channel_id=1, replica_groups=mesh['grp'=2,'row'=4,'col'=4] {'row','col'}, dimensions={0} | all-to-all | bytes 131072 | tf_op jit(solution)/shard_map/all_to_all | solution.py:348
  30.0 1.3 %finish.1 = (f32[16,768]{1,0:T(8,128)}, f32[16,16]{1,0:T(8,128)}) custom-call(f32[16,8,128]{2,1,0:T(8,128)S(1)} %all_to_all.5.grams_ref, f32[16,768]{1,0:T(8,128)S(1)} %get-tuple-element.43.applied_ref), custom_call_target="tpu_custom_call" | custom-call | tf_op jit(solution)/shard_map/finish/pallas_call | solution.py:236
  (10 shorter events, 0.1 us)
Async XLA Ops:
  1.4 7.5 %collective-permute-start.2 = (bf16[32,768]{1,0:T(8,128)(2,1)S(1)}, bf16[32,768]{1,0:T(8,128)(2,1)S(1)}, u32[]{:S(2)}, u32[]{:S(2)}) collective-permute-start(bf16[32,768]{1,0:T(8,128)(2,1)S(1)} %get-tuple-element.26.packed_ref), channel_id=1, source_target_pairs={{0,3},{1,2},{2,1},{3,0},{4,7},{5,6},{6,5},{7,4},{8,11},{9,10},{10,... | collective-permute-start | bytes 147464 | tf_op jit(solution)/shard_map/ppermute | solution.py:216
  3.9 5.2 %collective-permute-start.1 = (bf16[32,768]{1,0:T(8,128)(2,1)S(1)}, bf16[32,768]{1,0:T(8,128)(2,1)S(1)}, u32[]{:S(2)}, u32[]{:S(2)}) collective-permute-start(bf16[32,768]{1,0:T(8,128)(2,1)S(1)} %get-tuple-element.26.packed_ref), channel_id=1, source_target_pairs={{0,9},{1,8},{2,11},{3,10},{4,13},{5,12},{6,15},{7,14},{8,1},{9,0},... | collective-permute-start | bytes 147464 | tf_op jit(solution)/shard_map/ppermute | solution.py:216
  6.8 3.9 %collective-permute-start = (bf16[32,768]{1,0:T(8,128)(2,1)S(1)}, bf16[32,768]{1,0:T(8,128)(2,1)S(1)}, u32[]{:S(2)}, u32[]{:S(2)}) collective-permute-start(bf16[32,768]{1,0:T(8,128)(2,1)S(1)} %get-tuple-element.26.packed_ref), channel_id=1, source_target_pairs={{0,5},{1,4},{2,7},{3,6},{4,1},{5,0},{6,3},{7,2},{8,13},{9,12},{10,... | collective-permute-start | bytes 147464 | tf_op jit(solution)/shard_map/ppermute | solution.py:216
  7.8 5.3 %collective-permute-start.4 = (bf16[32,768]{1,0:T(8,128)(2,1)S(1)}, bf16[32,768]{1,0:T(8,128)(2,1)S(1)}, u32[]{:S(2)}, u32[]{:S(2)}) collective-permute-start(bf16[32,768]{1,0:T(8,128)(2,1)S(1)} %get-tuple-element.26.packed_ref), channel_id=1, source_target_pairs={{0,13},{1,12},{2,15},{3,14},{4,9},{5,8},{6,11},{7,10},{8,5},{9,4},... | collective-permute-start | bytes 147464 | tf_op jit(solution)/shard_map/ppermute | solution.py:216
  10.7 3.0 %collective-permute-start.3 = (bf16[4,32,768]{2,1,0:T(8,128)(2,1)S(1)}, bf16[4,32,768]{2,1,0:T(8,128)(2,1)S(1)}, u32[]{:S(2)}, u32[]{:S(2)}) collective-permute-start(bf16[4,32,768]{2,1,0:T(8,128)(2,1)S(1)} %pad_maximum_fusion.blocks_ref), channel_id=1, source_target_pairs={{0,1},{1,0},{2,3},{3,2},{4,5},{5,4},{6,7},{7,6},{8,9},{9,8},{10,11... | collective-permute-start | bytes 589832 | tf_op jit(solution)/shard_map/ppermute | solution.py:216
  13.1 1.6 %collective-permute-start.5 = (bf16[1,32,768]{2,1,0:T(8,128)(2,1)S(1)}, bf16[1,32,768]{2,1,0:T(8,128)(2,1)S(1)}, u32[]{:S(2)}, u32[]{:S(2)}) collective-permute-start(bf16[1,32,768]{2,1,0:T(8,128)(2,1)S(1)} %bitcast.12), channel_id=1, source_target_pairs={{0,1},{1,0},{2,3},{3,2},{4,5},{5,4},{6,7},{7,6},{8,9},{9,8},{10,11... | collective-permute-start | bytes 147464 | tf_op jit(solution)/shard_map/ppermute | solution.py:216
  15.3 4.3 %collective-permute-start.6 = (f32[16,768]{1,0:T(8,128)S(1)}, f32[16,768]{1,0:T(8,128)S(1)}, u32[]{:S(2)}, u32[]{:S(2)}) collective-permute-start(f32[16,768]{1,0:T(8,128)S(1)} %partner_late.1), channel_id=1, source_target_pairs={{0,3},{1,2},{2,1},{3,0},{4,7},{5,6},{6,5},{7,4},{8,11},{9,10},{10,... | collective-permute-start | bytes 147464 | tf_op jit(solution)/shard_map/ppermute | solution.py:216

commit v12 on v10

--- a/solution.py
+++ b/solution.py
@@ -335,6 +335,7 @@
     parts = [None] * len(partners)
     for k, hop in enumerate(partners):
         parts[k] = add_part("partner", hop, lines[1:], sides[k], near, None)
+    image = add_part("add_early", (0, 0), lines[1:], side, near, image)
     late, parts, image = lax.optimization_barrier((line[:1], parts, image))
     late = jnp.stack(late)
     other_late = sent(late, core)
@@ -349,8 +350,8 @@
         )
     parts, image = lax.optimization_barrier((parts, image))
     received = [sent(part, hop) for hop, part in zip(partners, parts)]
-    own_places = lines[1:] + beyond(held_at, core) + lines[:1] + beyond(lines[:1], core)
-    blocks = jnp.concatenate([near[: n_row - 2], other, late, other_late])
+    own_places = beyond(held_at, core) + lines[:1] + beyond(lines[:1], core)
+    blocks = jnp.concatenate([other, late, other_late])
     image = add_part("add_own", (0, 0), own_places, side, blocks, image)
     applied, gram = call(
         last_kernel,

time: 31.7 us -> 35 us (1.10); the launches traced: 31.5 us -> 34.4 us
  starting transfers between devices: 8.01 us -> 10.3 us
  blocking collectives: 10.6 us -> 11.5 us
  waiting for transfers between devices: 5.36 us -> 4.72 us
    ppermute x7, starting transfers between devices: 8.01 us -> 10.3 us  [sent(): return lax.ppermute(x, ('row', 'col'), pairs)]
    all_to_all x1, blocking collectives: 10.6 us -> 11.5 us  [per_device(): grams = lax.all_to_all(gram, ('row', 'col'), 0, 0)]
    ppermute x7, waiting for transfers between devices: 5.36 us -> 4.72 us  [sent(): return lax.ppermute(x, ('row', 'col'), pairs)]
    pallas_call x9 -> x10, Pallas kernels: 6.74 us -> 6.96 us  [call(): pl.pallas_call(kernel, out_shape=shapes, in_specs=where, out_specs=to, co...]
  transfers between devices with their start and end apart: 7 -> 7, of which waited for: 3 -> 4; matrix products, arithmetic and copies ran while one was open for 0% -> 0% of each run, Pallas kernels for 14% -> 13%
where the time goes in v12:
time: 35 us; the launch traced here: 34.4 us
  blocking collectives  11.5 us (33%)
  starting transfers between devices  10.3 us (29%)
  Pallas kernels  6.96 us (20%)
  waiting for transfers between devices  4.72 us (13%)
  between operations  0.7 us (2%)
    all_to_all x1, blocking collectives, per_device(): grams = lax.all_to_all(gram, ('row', 'col'), 0, 0)  11.5 us
    ppermute x7, starting transfers between devices, sent(): return lax.ppermute(x, ('row', 'col'), pairs)  10.3 us
    pallas_call x10, Pallas kernels, call(): pl.pallas_call(kernel, out_shape=shapes, in_specs=where, out_specs=to, co...  6.96 us
    ppermute x7, waiting for transfers between devices, sent(): return lax.ppermute(x, ('row', 'col'), pairs)  4.72 us
  transfers between devices with their start and end apart: 7, of which 4 were waited for; matrix products, arithmetic and copies ran while one was open for 0% of the time, Pallas kernels for 13%

profile of v12, /device:TPU:0, one launch (start us, length us, event | category | flops | bytes accessed | tf_op | source)
XLA Modules:
  0.0 34.4 jit_solution(11590904858436633999)
XLA Ops:
  0.6 0.8 %pack.1 = (bf16[32,768]{1,0:T(8,128)(2,1)S(1)}, bf16[16,768]{1,0:T(8,128)(2,1)S(1)}, f32[1,768]{1,0:T(1,128)S(1)}, s32[8,2,16]{2,1,0:T(2,128)S(1)}) custom-call(bf16[16,768]{1,0:T(8,128)(2,1)} %frames_ref.1, bf16[16,768]{1,0:T(8,128)(2,1)} %vectors_in.1, f32[768]{0:T(1024)} %degrees_ref.1, s32[8,2,16]{2,1,0:T(2,128)} %bitcast.14), custom_call_target="tpu_custom_call" | custom-call | tf_op jit(solution)/shard_map/pack/pallas_call | solution.py:240
  1.4 2.4 %collective-permute-start.2 = (bf16[32,768]{1,0:T(8,128)(2,1)S(1)}, bf16[32,768]{1,0:T(8,128)(2,1)S(1)}, u32[]{:S(2)}, u32[]{:S(2)}) collective-permute-start(bf16[32,768]{1,0:T(8,128)(2,1)S(1)} %get-tuple-element.28.packed_ref), channel_id=1, source_target_pairs={{0,3},{1,2},{2,1},{3,0},{4,7},{5,6},{6,5},{7,4},{8,11},{9,10},{10,... | collective-permute-start | bytes 147464 | tf_op jit(solution)/shard_map/ppermute | solution.py:220
  3.9 2.9 %collective-permute-start.1 = (bf16[32,768]{1,0:T(8,128)(2,1)S(1)}, bf16[32,768]{1,0:T(8,128)(2,1)S(1)}, u32[]{:S(2)}, u32[]{:S(2)}) collective-permute-start(bf16[32,768]{1,0:T(8,128)(2,1)S(1)} %get-tuple-element.28.packed_ref), channel_id=1, source_target_pairs={{0,9},{1,8},{2,11},{3,10},{4,13},{5,12},{6,15},{7,14},{8,1},{9,0},... | collective-permute-start | bytes 147464 | tf_op jit(solution)/shard_map/ppermute | solution.py:220
  6.8 1.0 %collective-permute-start = (bf16[32,768]{1,0:T(8,128)(2,1)S(1)}, bf16[32,768]{1,0:T(8,128)(2,1)S(1)}, u32[]{:S(2)}, u32[]{:S(2)}) collective-permute-start(bf16[32,768]{1,0:T(8,128)(2,1)S(1)} %get-tuple-element.28.packed_ref), channel_id=1, source_target_pairs={{0,5},{1,4},{2,7},{3,6},{4,1},{5,0},{6,3},{7,2},{8,13},{9,12},{10,... | collective-permute-start | bytes 147464 | tf_op jit(solution)/shard_map/ppermute | solution.py:220
  7.8 0.7 %own.1 = (bf16[64,768]{1,0:T(8,128)(2,1)S(1)}, f32[16,768]{1,0:T(8,128)S(1)}, s32[2,1]{1,0:T(2,128)S(4)}) custom-call(s32[8,2,16]{2,1,0:T(2,128)S(1)} %get-tuple-element.27.table_ref, bf16[32,768]{1,0:T(8,128)(2,1)S(1)} %get-tuple-element.28.packed_ref), custom_call_target="tpu_custom_call" | custom-call | tf_op jit(solution)/shard_map/own/pallas_call | solution.py:240
  8.5 0.0 collective-permute-done.2
  8.5 0.0 collective-permute-done.1
  8.6 2.1 %collective-permute-done = bf16[32,768]{1,0:T(8,128)(2,1)S(1)} collective-permute-done((bf16[32,768]{1,0:T(8,128)(2,1)S(1)}, bf16[32,768]{1,0:T(8,128)(2,1)S(1)}, u32[]{:S(2)}, u32[]{:S(2)}) %collective-permute-start) | collective-permute-done | bytes 49184 | tf_op jit(solution)/shard_map/ppermute | solution.py:220
  10.7 0.2 collective-permute-start.3
  10.9 2.3 %collective-permute-start.4 = (bf16[32,768]{1,0:T(8,128)(2,1)S(1)}, bf16[32,768]{1,0:T(8,128)(2,1)S(1)}, u32[]{:S(2)}, u32[]{:S(2)}) collective-permute-start(bf16[32,768]{1,0:T(8,128)(2,1)S(1)} %get-tuple-element.28.packed_ref), channel_id=1, source_target_pairs={{0,13},{1,12},{2,15},{3,14},{4,9},{5,8},{6,11},{7,10},{8,5},{9,4},... | collective-permute-start | bytes 147464 | tf_op jit(solution)/shard_map/ppermute | solution.py:220
  13.3 0.7 %add_early.1.before_ref = f32[16,768]{1,0:T(8,128)S(1)} custom-call(s32[2,1]{1,0:T(2,128)S(4)} %get-tuple-element.29.masks_ref, bf16[64,768]{1,0:T(8,128)(2,1)S(1)} %get-tuple-element.30.side_ref, bf16[4,32,768]{2,1,0:T(8,128)(2,1)S(1)} %pad_maximum_fusion.1.blocks_ref, f32[16,768]{1,0:T(8,128)S(1)} %get-tuple-element.38.before_ref), custom_call_target="tpu_custom_call", output_to_operand_aliasing={{}: (3, {})} | custom-call | tf_op jit(solution)/shard_map/add_early/pallas_call | solution.py:240
  13.9 0.7 %partner.1.before_ref = f32[16,768]{1,0:T(8,128)S(1)} custom-call(s32[2,1]{1,0:T(2,128)S(4)} %get-tuple-element.29.masks_ref, bf16[64,768]{1,0:T(8,128)(2,1)S(1)} %get-tuple-element.37.side_ref, bf16[4,32,768]{2,1,0:T(8,128)(2,1)S(1)} %pad_maximum_fusion.1.blocks_ref), custom_call_target="tpu_custom_call" | custom-call | tf_op jit(solution)/shard_map/partner/pallas_call | solution.py:240
  14.6 1.7 %collective-permute-done.4 = bf16[32,768]{1,0:T(8,128)(2,1)S(1)} collective-permute-done((bf16[32,768]{1,0:T(8,128)(2,1)S(1)}, bf16[32,768]{1,0:T(8,128)(2,1)S(1)}, u32[]{:S(2)}, u32[]{:S(2)}) %collective-permute-start.4) | collective-permute-done | bytes 49184 | tf_op jit(solution)/shard_map/ppermute | solution.py:220
  16.4 0.4 %collective-permute-start.5 = (bf16[1,32,768]{2,1,0:T(8,128)(2,1)S(1)}, bf16[1,32,768]{2,1,0:T(8,128)(2,1)S(1)}, u32[]{:S(2)}, u32[]{:S(2)}) collective-permute-start(bf16[1,32,768]{2,1,0:T(8,128)(2,1)S(1)} %bitcast.9), channel_id=1, source_target_pairs={{0,1},{1,0},{2,3},{3,2},{4,5},{5,4},{6,7},{7,6},{8,9},{9,8},{10,11... | collective-permute-start | bytes 147464 | tf_op jit(solution)/shard_map/ppermute | solution.py:220
  16.7 0.0 collective-permute-done.3
  16.8 0.7 %partner_middle.1.before_ref = f32[16,768]{1,0:T(8,128)S(1)} custom-call(s32[2,1]{1,0:T(2,128)S(4)} %get-tuple-element.29.masks_ref, bf16[64,768]{1,0:T(8,128)(2,1)S(1)} %get-tuple-element.37.side_ref, bf16[3,32,768]{2,1,0:T(8,128)(2,1)S(1)} %pad_maximum_fusion.2.blocks_ref, f32[16,768]{1,0:T(8,128)S(1)} %partner.1.before_ref), custom_call_target="tpu_custom_call", output_to_operand_aliasing={{}: (3, {})} | custom-call | tf_op jit(solution)/shard_map/partner_middle/pallas_call | solution.py:240
  17.5 0.1 collective-permute-done.5.blocks_ref
  17.6 1.1 %collective-permute-start.6 = (f32[16,768]{1,0:T(8,128)S(1)}, f32[16,768]{1,0:T(8,128)S(1)}, u32[]{:S(2)}, u32[]{:S(2)}) collective-permute-start(f32[16,768]{1,0:T(8,128)S(1)} %partner_late.1), channel_id=1, source_target_pairs={{0,3},{1,2},{2,1},{3,0},{4,7},{5,6},{6,5},{7,4},{8,11},{9,10},{10,... | collective-permute-start | bytes 147464 | tf_op jit(solution)/shard_map/ppermute | solution.py:220
  18.8 1.6 %add_own.1.refs_0_ = f32[16,768]{1,0:T(8,128)S(1)} custom-call(s32[2,1]{1,0:T(2,128)S(4)} %get-tuple-element.29.masks_ref, bf16[64,768]{1,0:T(8,128)(2,1)S(1)} %get-tuple-element.30.side_ref, bf16[6,32,768]{2,1,0:T(8,128)(2,1)S(1)} %pad_maximum_fusion.blocks_ref, f32[16,768]{1,0:T(8,128)S(1)} %add_early.1.before_ref), custom_call_target="tpu_custom_call", output_to_operand_aliasing={{}: (3, {})} | custom-call | tf_op jit(solution)/shard_map/add_own/pallas_call | solution.py:240
  20.4 0.8 %collective-permute-done.6.refs_1_ = f32[16,768]{1,0:T(8,128)S(1)} collective-permute-done((f32[16,768]{1,0:T(8,128)S(1)}, f32[16,768]{1,0:T(8,128)S(1)}, u32[]{:S(2)}, u32[]{:S(2)}) %collective-permute-start.6) | collective-permute-done | bytes 49184 | tf_op jit(solution)/shard_map/ppermute | solution.py:220
  21.2 0.4 %last.1 = (f32[16,768]{1,0:T(8,128)S(1)}, f32[16,8,128]{2,1,0:T(8,128)S(1)}) custom-call(bf16[16,768]{1,0:T(8,128)(2,1)S(1)} %get-tuple-element.25.vectors_ref, f32[1,768]{1,0:T(1,128)S(1)} %get-tuple-element.26.root_ref, f32[16,768]{1,0:T(8,128)S(1)} %add_own.1.refs_0_, f32[16,768]{1,0:T(8,128)S(1)} %collective-permute-done.6.refs_1_), custom_call_target="tpu_custom_call" | custom-call | tf_op jit(solution)/shard_map/last/pallas_call | solution.py:240
  21.5 11.5 %all_to_all.5.grams_ref = f32[16,8,128]{2,1,0:T(8,128)S(1)} all-to-all(f32[16,8,128]{2,1,0:T(8,128)S(1)} %get-tuple-element.46), channel_id=1, replica_groups=mesh['grp'=2,'row'=4,'col'=4] {'row','col'}, dimensions={0} | all-to-all | bytes 131072 | tf_op jit(solution)/shard_map/all_to_all | solution.py:365
  33.1 1.3 %finish.1 = (f32[16,768]{1,0:T(8,128)}, f32[16,16]{1,0:T(8,128)}) custom-call(f32[16,8,128]{2,1,0:T(8,128)S(1)} %all_to_all.5.grams_ref, f32[16,768]{1,0:T(8,128)S(1)} %get-tuple-element.47.applied_ref), custom_call_target="tpu_custom_call" | custom-call | tf_op jit(solution)/shard_map/finish/pallas_call | solution.py:240
  (6 shorter events, 0.1 us)
Async XLA Ops:
  1.4 7.0 %collective-permute-start.2 = (bf16[32,768]{1,0:T(8,128)(2,1)S(1)}, bf16[32,768]{1,0:T(8,128)(2,1)S(1)}, u32[]{:S(2)}, u32[]{:S(2)}) collective-permute-start(bf16[32,768]{1,0:T(8,128)(2,1)S(1)} %get-tuple-element.28.packed_ref), channel_id=1, source_target_pairs={{0,3},{1,2},{2,1},{3,0},{4,7},{5,6},{6,5},{7,4},{8,11},{9,10},{10,... | collective-permute-start | bytes 147464 | tf_op jit(solution)/shard_map/ppermute | solution.py:220
  3.9 4.7 %collective-permute-start.1 = (bf16[32,768]{1,0:T(8,128)(2,1)S(1)}, bf16[32,768]{1,0:T(8,128)(2,1)S(1)}, u32[]{:S(2)}, u32[]{:S(2)}) collective-permute-start(bf16[32,768]{1,0:T(8,128)(2,1)S(1)} %get-tuple-element.28.packed_ref), channel_id=1, source_target_pairs={{0,9},{1,8},{2,11},{3,10},{4,13},{5,12},{6,15},{7,14},{8,1},{9,0},... | collective-permute-start | bytes 147464 | tf_op jit(solution)/shard_map/ppermute | solution.py:220
  6.8 3.9 %collective-permute-start = (bf16[32,768]{1,0:T(8,128)(2,1)S(1)}, bf16[32,768]{1,0:T(8,128)(2,1)S(1)}, u32[]{:S(2)}, u32[]{:S(2)}) collective-permute-start(bf16[32,768]{1,0:T(8,128)(2,1)S(1)} %get-tuple-element.28.packed_ref), channel_id=1, source_target_pairs={{0,5},{1,4},{2,7},{3,6},{4,1},{5,0},{6,3},{7,2},{8,13},{9,12},{10,... | collective-permute-start | bytes 147464 | tf_op jit(solution)/shard_map/ppermute | solution.py:220
  10.7 6.0 %collective-permute-start.3 = (bf16[4,32,768]{2,1,0:T(8,128)(2,1)S(1)}, bf16[4,32,768]{2,1,0:T(8,128)(2,1)S(1)}, u32[]{:S(2)}, u32[]{:S(2)}) collective-permute-start(bf16[4,32,768]{2,1,0:T(8,128)(2,1)S(1)} %pad_maximum_fusion.1.blocks_ref), channel_id=1, source_target_pairs={{0,1},{1,0},{2,3},{3,2},{4,5},{5,4},{6,7},{7,6},{8,9},{9,8},{10,11... | collective-permute-start | bytes 589832 | tf_op jit(solution)/shard_map/ppermute | solution.py:220
  10.9 5.5 %collective-permute-start.4 = (bf16[32,768]{1,0:T(8,128)(2,1)S(1)}, bf16[32,768]{1,0:T(8,128)(2,1)S(1)}, u32[]{:S(2)}, u32[]{:S(2)}) collective-permute-start(bf16[32,768]{1,0:T(8,128)(2,1)S(1)} %get-tuple-element.28.packed_ref), channel_id=1, source_target_pairs={{0,13},{1,12},{2,15},{3,14},{4,9},{5,8},{6,11},{7,10},{8,5},{9,4},... | collective-permute-start | bytes 147464 | tf_op jit(solution)/shard_map/ppermute | solution.py:220
  16.4 1.2 %collective-permute-start.5 = (bf16[1,32,768]{2,1,0:T(8,128)(2,1)S(1)}, bf16[1,32,768]{2,1,0:T(8,128)(2,1)S(1)}, u32[]{:S(2)}, u32[]{:S(2)}) collective-permute-start(bf16[1,32,768]{2,1,0:T(8,128)(2,1)S(1)} %bitcast.9), channel_id=1, source_target_pairs={{0,1},{1,0},{2,3},{3,2},{4,5},{5,4},{6,7},{7,6},{8,9},{9,8},{10,11... | collective-permute-start | bytes 147464 | tf_op jit(solution)/shard_map/ppermute | solution.py:220
  17.6 3.6 %collective-permute-start.6 = (f32[16,768]{1,0:T(8,128)S(1)}, f32[16,768]{1,0:T(8,128)S(1)}, u32[]{:S(2)}, u32[]{:S(2)}) collective-permute-start(f32[16,768]{1,0:T(8,128)S(1)} %partner_late.1), channel_id=1, source_target_pairs={{0,3},{1,2},{2,1},{3,0},{4,7},{5,6},{6,5},{7,4},{8,11},{9,10},{10,... | collective-permute-start | bytes 147464 | tf_op jit(solution)/shard_map/ppermute | solution.py:220

commit v13 on v10

--- a/solution.py
+++ b/solution.py
@@ -110,6 +110,9 @@
         add_group(4 * group, 4)
         return 0
 
+    if len(places) >= 5:
+        pl.when(count == 5)(lambda: add_group(0, 5))
+        rest = jnp.where(count == 5, 0, rest)
     if len(places) >= 4:
         lax.fori_loop(0, fours, add_four, 0)
     if len(places) >= 3:

time: 31.7 us -> 31 us (0.978)
  waiting for transfers between devices: 5.36 us -> 3.99 us
  Pallas kernels: 6.74 us -> 7.51 us
  blocking collectives: 10.6 us -> 10.2 us
    ppermute x7, waiting for transfers between devices: 5.36 us -> 3.99 us  [sent(): return lax.ppermute(x, ('row', 'col'), pairs)]
    pallas_call x9, Pallas kernels: 6.74 us -> 7.51 us  [call(): pl.pallas_call(kernel, out_shape=shapes, in_specs=where, out_specs=to, co...]
    all_to_all x1, blocking collectives: 10.6 us -> 10.2 us  [per_device(): grams = lax.all_to_all(gram, ('row', 'col'), 0, 0)]
  transfers between devices with their start and end apart: 7 -> 7, of which waited for: 3 -> 4; matrix products, arithmetic and copies ran while one was open for 0% -> 0% of each run, Pallas kernels for 14% -> 14%
where the time goes in v13:
time: 31 us; the launch traced here: 30.7 us
  blocking collectives  10.2 us (33%)
  starting transfers between devices  8.18 us (26%)
  Pallas kernels  7.51 us (24%)
  waiting for transfers between devices  3.99 us (13%)
  between operations  0.72 us (2%)
    all_to_all x1, blocking collectives, per_device(): grams = lax.all_to_all(gram, ('row', 'col'), 0, 0)  10.2 us
    ppermute x7, starting transfers between devices, sent(): return lax.ppermute(x, ('row', 'col'), pairs)  8.18 us
    pallas_call x9, Pallas kernels, call(): pl.pallas_call(kernel, out_shape=shapes, in_specs=where, out_specs=to, co...  7.51 us
    ppermute x7, waiting for transfers between devices, sent(): return lax.ppermute(x, ('row', 'col'), pairs)  3.99 us
  transfers between devices with their start and end apart: 7, of which 4 were waited for; matrix products, arithmetic and copies ran while one was open for 0% of the time, Pallas kernels for 14%

profile of v13, /device:TPU:0, one launch (start us, length us, event | category | flops | bytes accessed | tf_op | source)
XLA Modules:
  0.0 30.7 jit_solution(17401654844458938331)
XLA Ops:
  0.6 0.8 %pack.1 = (bf16[32,768]{1,0:T(8,128)(2,1)S(1)}, bf16[16,768]{1,0:T(8,128)(2,1)S(1)}, f32[1,768]{1,0:T(1,128)S(1)}, s32[8,2,16]{2,1,0:T(2,128)S(1)}) custom-call(bf16[16,768]{1,0:T(8,128)(2,1)} %frames_ref.1, bf16[16,768]{1,0:T(8,128)(2,1)} %vectors_in.1, f32[768]{0:T(1024)} %degrees_ref.1, s32[8,2,16]{2,1,0:T(2,128)} %bitcast.16), custom_call_target="tpu_custom_call" | custom-call | tf_op jit(solution)/shard_map/pack/pallas_call | solution.py:243
  1.4 2.4 %collective-permute-start.2 = (bf16[32,768]{1,0:T(8,128)(2,1)S(1)}, bf16[32,768]{1,0:T(8,128)(2,1)S(1)}, u32[]{:S(2)}, u32[]{:S(2)}) collective-permute-start(bf16[32,768]{1,0:T(8,128)(2,1)S(1)} %get-tuple-element.28.packed_ref), channel_id=1, source_target_pairs={{0,3},{1,2},{2,1},{3,0},{4,7},{5,6},{6,5},{7,4},{8,11},{9,10},{10,... | collective-permute-start | bytes 147464 | tf_op jit(solution)/shard_map/ppermute | solution.py:223
  3.9 2.9 %collective-permute-start.1 = (bf16[32,768]{1,0:T(8,128)(2,1)S(1)}, bf16[32,768]{1,0:T(8,128)(2,1)S(1)}, u32[]{:S(2)}, u32[]{:S(2)}) collective-permute-start(bf16[32,768]{1,0:T(8,128)(2,1)S(1)} %get-tuple-element.28.packed_ref), channel_id=1, source_target_pairs={{0,9},{1,8},{2,11},{3,10},{4,13},{5,12},{6,15},{7,14},{8,1},{9,0},... | collective-permute-start | bytes 147464 | tf_op jit(solution)/shard_map/ppermute | solution.py:223
  6.8 1.0 %collective-permute-start = (bf16[32,768]{1,0:T(8,128)(2,1)S(1)}, bf16[32,768]{1,0:T(8,128)(2,1)S(1)}, u32[]{:S(2)}, u32[]{:S(2)}) collective-permute-start(bf16[32,768]{1,0:T(8,128)(2,1)S(1)} %get-tuple-element.28.packed_ref), channel_id=1, source_target_pairs={{0,5},{1,4},{2,7},{3,6},{4,1},{5,0},{6,3},{7,2},{8,13},{9,12},{10,... | collective-permute-start | bytes 147464 | tf_op jit(solution)/shard_map/ppermute | solution.py:223
  7.8 0.5 %collective-permute-start.4 = (bf16[32,768]{1,0:T(8,128)(2,1)S(1)}, bf16[32,768]{1,0:T(8,128)(2,1)S(1)}, u32[]{:S(2)}, u32[]{:S(2)}) collective-permute-start(bf16[32,768]{1,0:T(8,128)(2,1)S(1)} %get-tuple-element.28.packed_ref), channel_id=1, source_target_pairs={{0,13},{1,12},{2,15},{3,14},{4,9},{5,8},{6,11},{7,10},{8,5},{9,4},... | collective-permute-start | bytes 147464 | tf_op jit(solution)/shard_map/ppermute | solution.py:223
  8.3 0.7 %own.1 = (bf16[64,768]{1,0:T(8,128)(2,1)S(1)}, f32[16,768]{1,0:T(8,128)S(1)}, s32[2,1]{1,0:T(2,128)S(4)}) custom-call(s32[8,2,16]{2,1,0:T(2,128)S(1)} %get-tuple-element.27.table_ref, bf16[32,768]{1,0:T(8,128)(2,1)S(1)} %get-tuple-element.28.packed_ref), custom_call_target="tpu_custom_call" | custom-call | tf_op jit(solution)/shard_map/own/pallas_call | solution.py:243
  9.0 0.0 collective-permute-done.2
  9.1 0.0 collective-permute-done.1
  9.1 1.6 %collective-permute-done = bf16[32,768]{1,0:T(8,128)(2,1)S(1)} collective-permute-done((bf16[32,768]{1,0:T(8,128)(2,1)S(1)}, bf16[32,768]{1,0:T(8,128)(2,1)S(1)}, u32[]{:S(2)}, u32[]{:S(2)}) %collective-permute-start) | collective-permute-done | bytes 49184 | tf_op jit(solution)/shard_map/ppermute | solution.py:223
  10.7 0.2 collective-permute-start.3
  10.9 0.7 %partner.1.before_ref = f32[16,768]{1,0:T(8,128)S(1)} custom-call(s32[2,1]{1,0:T(2,128)S(4)} %get-tuple-element.29.masks_ref, bf16[64,768]{1,0:T(8,128)(2,1)S(1)} %get-tuple-element.37.side_ref, bf16[4,32,768]{2,1,0:T(8,128)(2,1)S(1)} %pad_maximum_fusion.blocks_ref), custom_call_target="tpu_custom_call" | custom-call | tf_op jit(solution)/shard_map/partner/pallas_call | solution.py:243
  11.6 1.5 %collective-permute-done.4 = bf16[32,768]{1,0:T(8,128)(2,1)S(1)} collective-permute-done((bf16[32,768]{1,0:T(8,128)(2,1)S(1)}, bf16[32,768]{1,0:T(8,128)(2,1)S(1)}, u32[]{:S(2)}, u32[]{:S(2)}) %collective-permute-start.4) | collective-permute-done | bytes 49184 | tf_op jit(solution)/shard_map/ppermute | solution.py:223
  13.1 0.7 %collective-permute-start.5 = (bf16[1,32,768]{2,1,0:T(8,128)(2,1)S(1)}, bf16[1,32,768]{2,1,0:T(8,128)(2,1)S(1)}, u32[]{:S(2)}, u32[]{:S(2)}) collective-permute-start(bf16[1,32,768]{2,1,0:T(8,128)(2,1)S(1)} %bitcast.12), channel_id=1, source_target_pairs={{0,1},{1,0},{2,3},{3,2},{4,5},{5,4},{6,7},{7,6},{8,9},{9,8},{10,11... | collective-permute-start | bytes 147464 | tf_op jit(solution)/shard_map/ppermute | solution.py:223
  13.8 0.0 collective-permute-done.3
  13.8 0.7 %partner_middle.1.before_ref = f32[16,768]{1,0:T(8,128)S(1)} custom-call(s32[2,1]{1,0:T(2,128)S(4)} %get-tuple-element.29.masks_ref, bf16[64,768]{1,0:T(8,128)(2,1)S(1)} %get-tuple-element.37.side_ref, bf16[3,32,768]{2,1,0:T(8,128)(2,1)S(1)} %pad_maximum_fusion.1.blocks_ref, f32[16,768]{1,0:T(8,128)S(1)} %partner.1.before_ref), custom_call_target="tpu_custom_call", output_to_operand_aliasing={{}: (3, {})} | custom-call | tf_op jit(solution)/shard_map/partner_middle/pallas_call | solution.py:243
  14.6 0.1 collective-permute-done.5.blocks_ref
  14.6 0.7 %partner_late.1 = f32[16,768]{1,0:T(8,128)S(1)} custom-call(s32[2,1]{1,0:T(2,128)S(4)} %get-tuple-element.29.masks_ref, bf16[64,768]{1,0:T(8,128)(2,1)S(1)} %get-tuple-element.37.side_ref, bf16[1,32,768]{2,1,0:T(8,128)(2,1)S(1)} %collective-permute-done.5.blocks_ref, f32[16,768]{1,0:T(8,128)S(1)} %partner_middle.1.before_ref), custom_call_target="tpu_custom_call", output_to_operand_aliasing={{}: (3, {})} | custom-call | tf_op jit(solution)/shard_map/partner_late/pallas_call | solution.py:243
  15.3 0.5 %collective-permute-start.6 = (f32[16,768]{1,0:T(8,128)S(1)}, f32[16,768]{1,0:T(8,128)S(1)}, u32[]{:S(2)}, u32[]{:S(2)}) collective-permute-start(f32[16,768]{1,0:T(8,128)S(1)} %partner_late.1), channel_id=1, source_target_pairs={{0,3},{1,2},{2,1},{3,0},{4,7},{5,6},{6,5},{7,4},{8,11},{9,10},{10,... | collective-permute-start | bytes 147464 | tf_op jit(solution)/shard_map/ppermute | solution.py:223
  15.9 2.2 %add_own.1.refs_0_ = f32[16,768]{1,0:T(8,128)S(1)} custom-call(s32[2,1]{1,0:T(2,128)S(4)} %get-tuple-element.29.masks_ref, bf16[64,768]{1,0:T(8,128)(2,1)S(1)} %get-tuple-element.30.side_ref, bf16[8,32,768]{2,1,0:T(8,128)(2,1)S(1)} %constant_dynamic-update-slice_fusion.blocks_ref, ...), custom_call_target="tpu_custom_call", output_to_operand_aliasing={{}: (3, {})} | custom-call | tf_op jit(solution)/shard_map/add_own/pallas_call | solution.py:243
  18.1 0.8 %collective-permute-done.6.refs_1_ = f32[16,768]{1,0:T(8,128)S(1)} collective-permute-done((f32[16,768]{1,0:T(8,128)S(1)}, f32[16,768]{1,0:T(8,128)S(1)}, u32[]{:S(2)}, u32[]{:S(2)}) %collective-permute-start.6) | collective-permute-done | bytes 49184 | tf_op jit(solution)/shard_map/ppermute | solution.py:223
  18.8 0.4 %last.1 = (f32[16,768]{1,0:T(8,128)S(1)}, f32[16,8,128]{2,1,0:T(8,128)S(1)}) custom-call(bf16[16,768]{1,0:T(8,128)(2,1)S(1)} %get-tuple-element.25.vectors_ref, f32[1,768]{1,0:T(1,128)S(1)} %get-tuple-element.26.root_ref, f32[16,768]{1,0:T(8,128)S(1)} %add_own.1.refs_0_, f32[16,768]{1,0:T(8,128)S(1)} %collective-permute-done.6.refs_1_), custom_call_target="tpu_custom_call" | custom-call | tf_op jit(solution)/shard_map/last/pallas_call | solution.py:243
  19.2 10.2 %all_to_all.5.grams_ref = f32[16,8,128]{2,1,0:T(8,128)S(1)} all-to-all(f32[16,8,128]{2,1,0:T(8,128)S(1)} %get-tuple-element.46), channel_id=1, replica_groups=mesh['grp'=2,'row'=4,'col'=4] {'row','col'}, dimensions={0} | all-to-all | bytes 131072 | tf_op jit(solution)/shard_map/all_to_all | solution.py:367
  29.4 1.3 %finish.1 = (f32[16,768]{1,0:T(8,128)}, f32[16,16]{1,0:T(8,128)}) custom-call(f32[16,8,128]{2,1,0:T(8,128)S(1)} %all_to_all.5.grams_ref, f32[16,768]{1,0:T(8,128)S(1)} %get-tuple-element.47.applied_ref), custom_call_target="tpu_custom_call" | custom-call | tf_op jit(solution)/shard_map/finish/pallas_call | solution.py:243
  (9 shorter events, 0.1 us)
Async XLA Ops:
  1.4 7.5 %collective-permute-start.2 = (bf16[32,768]{1,0:T(8,128)(2,1)S(1)}, bf16[32,768]{1,0:T(8,128)(2,1)S(1)}, u32[]{:S(2)}, u32[]{:S(2)}) collective-permute-start(bf16[32,768]{1,0:T(8,128)(2,1)S(1)} %get-tuple-element.28.packed_ref), channel_id=1, source_target_pairs={{0,3},{1,2},{2,1},{3,0},{4,7},{5,6},{6,5},{7,4},{8,11},{9,10},{10,... | collective-permute-start | bytes 147464 | tf_op jit(solution)/shard_map/ppermute | solution.py:223
  3.9 5.2 %collective-permute-start.1 = (bf16[32,768]{1,0:T(8,128)(2,1)S(1)}, bf16[32,768]{1,0:T(8,128)(2,1)S(1)}, u32[]{:S(2)}, u32[]{:S(2)}) collective-permute-start(bf16[32,768]{1,0:T(8,128)(2,1)S(1)} %get-tuple-element.28.packed_ref), channel_id=1, source_target_pairs={{0,9},{1,8},{2,11},{3,10},{4,13},{5,12},{6,15},{7,14},{8,1},{9,0},... | collective-permute-start | bytes 147464 | tf_op jit(solution)/shard_map/ppermute | solution.py:223
  6.8 3.9 %collective-permute-start = (bf16[32,768]{1,0:T(8,128)(2,1)S(1)}, bf16[32,768]{1,0:T(8,128)(2,1)S(1)}, u32[]{:S(2)}, u32[]{:S(2)}) collective-permute-start(bf16[32,768]{1,0:T(8,128)(2,1)S(1)} %get-tuple-element.28.packed_ref), channel_id=1, source_target_pairs={{0,5},{1,4},{2,7},{3,6},{4,1},{5,0},{6,3},{7,2},{8,13},{9,12},{10,... | collective-permute-start | bytes 147464 | tf_op jit(solution)/shard_map/ppermute | solution.py:223
  7.8 5.3 %collective-permute-start.4 = (bf16[32,768]{1,0:T(8,128)(2,1)S(1)}, bf16[32,768]{1,0:T(8,128)(2,1)S(1)}, u32[]{:S(2)}, u32[]{:S(2)}) collective-permute-start(bf16[32,768]{1,0:T(8,128)(2,1)S(1)} %get-tuple-element.28.packed_ref), channel_id=1, source_target_pairs={{0,13},{1,12},{2,15},{3,14},{4,9},{5,8},{6,11},{7,10},{8,5},{9,4},... | collective-permute-start | bytes 147464 | tf_op jit(solution)/shard_map/ppermute | solution.py:223
  10.7 3.0 %collective-permute-start.3 = (bf16[4,32,768]{2,1,0:T(8,128)(2,1)S(1)}, bf16[4,32,768]{2,1,0:T(8,128)(2,1)S(1)}, u32[]{:S(2)}, u32[]{:S(2)}) collective-permute-start(bf16[4,32,768]{2,1,0:T(8,128)(2,1)S(1)} %pad_maximum_fusion.blocks_ref), channel_id=1, source_target_pairs={{0,1},{1,0},{2,3},{3,2},{4,5},{5,4},{6,7},{7,6},{8,9},{9,8},{10,11... | collective-permute-start | bytes 589832 | tf_op jit(solution)/shard_map/ppermute | solution.py:223
  13.1 1.6 %collective-permute-start.5 = (bf16[1,32,768]{2,1,0:T(8,128)(2,1)S(1)}, bf16[1,32,768]{2,1,0:T(8,128)(2,1)S(1)}, u32[]{:S(2)}, u32[]{:S(2)}) collective-permute-start(bf16[1,32,768]{2,1,0:T(8,128)(2,1)S(1)} %bitcast.12), channel_id=1, source_target_pairs={{0,1},{1,0},{2,3},{3,2},{4,5},{5,4},{6,7},{7,6},{8,9},{9,8},{10,11... | collective-permute-start | bytes 147464 | tf_op jit(solution)/shard_map/ppermute | solution.py:223
  15.3 3.5 %collective-permute-start.6 = (f32[16,768]{1,0:T(8,128)S(1)}, f32[16,768]{1,0:T(8,128)S(1)}, u32[]{:S(2)}, u32[]{:S(2)}) collective-permute-start(f32[16,768]{1,0:T(8,128)S(1)} %partner_late.1), channel_id=1, source_target_pairs={{0,3},{1,2},{2,1},{3,0},{4,7},{5,6},{6,5},{7,4},{8,11},{9,10},{10,... | collective-permute-start | bytes 147464 | tf_op jit(solution)/shard_map/ppermute | solution.py:223

commit v14 on v10

--- a/solution.py
+++ b/solution.py
@@ -28,17 +28,17 @@
 ):
     ncv = frames_ref.shape[0]
     copies = [
-        pltpu.make_async_copy(vectors_in, vectors_ref, sems.at[0]),
-        pltpu.make_async_copy(degrees_ref, degree_ref, sems.at[1]),
+        pltpu.make_async_copy(degrees_ref, degree_ref, sems.at[0]),
+        pltpu.make_async_copy(vectors_in, vectors_ref, sems.at[1]),
         pltpu.make_async_copy(frames_ref, packed_ref.at[pl.ds(0, ncv)], sems.at[2]),
         pltpu.make_async_copy(table_in, table_ref, sems.at[3]),
     ]
     for copy in copies:
         copy.start()
     copies[0].wait()
-    copies[1].wait()
     root = lax.rsqrt(degree_ref[...])[None, :]
     root_ref[...] = root
+    copies[1].wait()
     packed_ref[ncv:, :] = (vectors_ref[...].astype(jnp.float32) * root).astype(jnp.bfloat16)
     copies[2].wait()
     copies[3].wait()

time: 31.7 us -> 31.6 us (level)
  Pallas kernels: 6.74 us -> 5.83 us
  waiting for transfers between devices: 5.36 us -> 5.69 us
    pallas_call x9, Pallas kernels: 6.74 us -> 5.83 us  [call(): pl.pallas_call(kernel, out_shape=shapes, in_specs=where, out_specs=to, co...]
    all_to_all x1, blocking collectives: 10.6 us -> 10.9 us  [per_device(): grams = lax.all_to_all(gram, ('row', 'col'), 0, 0)]
    ppermute x7, waiting for transfers between devices: 5.36 us -> 5.69 us  [sent(): return lax.ppermute(x, ('row', 'col'), pairs)]
  transfers between devices with their start and end apart: 7 -> 7, of which waited for: 3 -> 4; matrix products, arithmetic and copies ran while one was open for 0% -> 0% of each run, Pallas kernels for 14% -> 9%
where the time goes in v14:
time: 31.6 us; the launch traced here: 31.4 us
  blocking collectives  10.9 us (34%)
  starting transfers between devices  8.18 us (26%)
  Pallas kernels  5.83 us (18%)
  waiting for transfers between devices  5.69 us (18%)
  between operations  0.72 us (2%)
    all_to_all x1, blocking collectives, per_device(): grams = lax.all_to_all(gram, ('row', 'col'), 0, 0)  10.9 us
    ppermute x7, starting transfers between devices, sent(): return lax.ppermute(x, ('row', 'col'), pairs)  8.18 us
    pallas_call x9, Pallas kernels, call(): pl.pallas_call(kernel, out_shape=shapes, in_specs=where, out_specs=to, co...  5.83 us
    ppermute x7, waiting for transfers between devices, sent(): return lax.ppermute(x, ('row', 'col'), pairs)  5.69 us
  transfers between devices with their start and end apart: 7, of which 4 were waited for; matrix products, arithmetic and copies ran while one was open for 0% of the time, Pallas kernels for 9%

profile of v14, /device:TPU:0, one launch (start us, length us, event | category | flops | bytes accessed | tf_op | source)
XLA Modules:
  0.0 31.4 jit_solution(14296179440261049178)
XLA Ops:
  0.6 0.8 %pack.1 = (bf16[32,768]{1,0:T(8,128)(2,1)S(1)}, bf16[16,768]{1,0:T(8,128)(2,1)S(1)}, f32[1,768]{1,0:T(1,128)S(1)}, s32[8,2,16]{2,1,0:T(2,128)S(1)}) custom-call(bf16[16,768]{1,0:T(8,128)(2,1)} %frames_ref.1, bf16[16,768]{1,0:T(8,128)(2,1)} %vectors_in.1, f32[768]{0:T(1024)} %degrees_ref.1, s32[8,2,16]{2,1,0:T(2,128)} %bitcast.16), custom_call_target="tpu_custom_call" | custom-call | tf_op jit(solution)/shard_map/pack/pallas_call | solution.py:240
  1.4 2.4 %collective-permute-start.2 = (bf16[32,768]{1,0:T(8,128)(2,1)S(1)}, bf16[32,768]{1,0:T(8,128)(2,1)S(1)}, u32[]{:S(2)}, u32[]{:S(2)}) collective-permute-start(bf16[32,768]{1,0:T(8,128)(2,1)S(1)} %get-tuple-element.28.packed_ref), channel_id=1, source_target_pairs={{0,3},{1,2},{2,1},{3,0},{4,7},{5,6},{6,5},{7,4},{8,11},{9,10},{10,... | collective-permute-start | bytes 147464 | tf_op jit(solution)/shard_map/ppermute | solution.py:220
  3.9 2.9 %collective-permute-start.1 = (bf16[32,768]{1,0:T(8,128)(2,1)S(1)}, bf16[32,768]{1,0:T(8,128)(2,1)S(1)}, u32[]{:S(2)}, u32[]{:S(2)}) collective-permute-start(bf16[32,768]{1,0:T(8,128)(2,1)S(1)} %get-tuple-element.28.packed_ref), channel_id=1, source_target_pairs={{0,9},{1,8},{2,11},{3,10},{4,13},{5,12},{6,15},{7,14},{8,1},{9,0},... | collective-permute-start | bytes 147464 | tf_op jit(solution)/shard_map/ppermute | solution.py:220
  6.8 1.0 %collective-permute-start = (bf16[32,768]{1,0:T(8,128)(2,1)S(1)}, bf16[32,768]{1,0:T(8,128)(2,1)S(1)}, u32[]{:S(2)}, u32[]{:S(2)}) collective-permute-start(bf16[32,768]{1,0:T(8,128)(2,1)S(1)} %get-tuple-element.28.packed_ref), channel_id=1, source_target_pairs={{0,5},{1,4},{2,7},{3,6},{4,1},{5,0},{6,3},{7,2},{8,13},{9,12},{10,... | collective-permute-start | bytes 147464 | tf_op jit(solution)/shard_map/ppermute | solution.py:220
  7.8 0.5 %collective-permute-start.4 = (bf16[32,768]{1,0:T(8,128)(2,1)S(1)}, bf16[32,768]{1,0:T(8,128)(2,1)S(1)}, u32[]{:S(2)}, u32[]{:S(2)}) collective-permute-start(bf16[32,768]{1,0:T(8,128)(2,1)S(1)} %get-tuple-element.28.packed_ref), channel_id=1, source_target_pairs={{0,13},{1,12},{2,15},{3,14},{4,9},{5,8},{6,11},{7,10},{8,5},{9,4},... | collective-permute-start | bytes 147464 | tf_op jit(solution)/shard_map/ppermute | solution.py:220
  8.3 0.7 %own.1 = (bf16[64,768]{1,0:T(8,128)(2,1)S(1)}, f32[16,768]{1,0:T(8,128)S(1)}, s32[2,1]{1,0:T(2,128)S(4)}) custom-call(s32[8,2,16]{2,1,0:T(2,128)S(1)} %get-tuple-element.27.table_ref, bf16[32,768]{1,0:T(8,128)(2,1)S(1)} %get-tuple-element.28.packed_ref), custom_call_target="tpu_custom_call" | custom-call | tf_op jit(solution)/shard_map/own/pallas_call | solution.py:240
  9.0 0.0 collective-permute-done.2
  9.1 0.0 collective-permute-done.1
  9.1 1.6 %collective-permute-done = bf16[32,768]{1,0:T(8,128)(2,1)S(1)} collective-permute-done((bf16[32,768]{1,0:T(8,128)(2,1)S(1)}, bf16[32,768]{1,0:T(8,128)(2,1)S(1)}, u32[]{:S(2)}, u32[]{:S(2)}) %collective-permute-start) | collective-permute-done | bytes 49184 | tf_op jit(solution)/shard_map/ppermute | solution.py:220
  10.7 0.2 collective-permute-start.3
  10.9 0.7 %partner.1.before_ref = f32[16,768]{1,0:T(8,128)S(1)} custom-call(s32[2,1]{1,0:T(2,128)S(4)} %get-tuple-element.29.masks_ref, bf16[64,768]{1,0:T(8,128)(2,1)S(1)} %get-tuple-element.37.side_ref, bf16[4,32,768]{2,1,0:T(8,128)(2,1)S(1)} %pad_maximum_fusion.blocks_ref), custom_call_target="tpu_custom_call" | custom-call | tf_op jit(solution)/shard_map/partner/pallas_call | solution.py:240
  11.6 1.5 %collective-permute-done.4 = bf16[32,768]{1,0:T(8,128)(2,1)S(1)} collective-permute-done((bf16[32,768]{1,0:T(8,128)(2,1)S(1)}, bf16[32,768]{1,0:T(8,128)(2,1)S(1)}, u32[]{:S(2)}, u32[]{:S(2)}) %collective-permute-start.4) | collective-permute-done | bytes 49184 | tf_op jit(solution)/shard_map/ppermute | solution.py:220
  13.1 0.7 %collective-permute-start.5 = (bf16[1,32,768]{2,1,0:T(8,128)(2,1)S(1)}, bf16[1,32,768]{2,1,0:T(8,128)(2,1)S(1)}, u32[]{:S(2)}, u32[]{:S(2)}) collective-permute-start(bf16[1,32,768]{2,1,0:T(8,128)(2,1)S(1)} %bitcast.12), channel_id=1, source_target_pairs={{0,1},{1,0},{2,3},{3,2},{4,5},{5,4},{6,7},{7,6},{8,9},{9,8},{10,11... | collective-permute-start | bytes 147464 | tf_op jit(solution)/shard_map/ppermute | solution.py:220
  13.8 0.0 collective-permute-done.3
  13.8 0.1 partner_middle.1.before_ref
  13.9 0.8 %collective-permute-done.5.blocks_ref = bf16[1,32,768]{2,1,0:T(8,128)(2,1)S(1)} collective-permute-done((bf16[1,32,768]{2,1,0:T(8,128)(2,1)S(1)}, bf16[1,32,768]{2,1,0:T(8,128)(2,1)S(1)}, u32[]{:S(2)}, u32[]{:S(2)}) %collective-permute-start.5) | collective-permute-done | bytes 49184 | tf_op jit(solution)/shard_map/ppermute | solution.py:220
  14.6 0.7 %partner_late.1 = f32[16,768]{1,0:T(8,128)S(1)} custom-call(s32[2,1]{1,0:T(2,128)S(4)} %get-tuple-element.29.masks_ref, bf16[64,768]{1,0:T(8,128)(2,1)S(1)} %get-tuple-element.37.side_ref, bf16[1,32,768]{2,1,0:T(8,128)(2,1)S(1)} %collective-permute-done.5.blocks_ref, f32[16,768]{1,0:T(8,128)S(1)} %partner_middle.1.before_ref), custom_call_target="tpu_custom_call", output_to_operand_aliasing={{}: (3, {})} | custom-call | tf_op jit(solution)/shard_map/partner_late/pallas_call | solution.py:240
  15.3 0.5 %collective-permute-start.6 = (f32[16,768]{1,0:T(8,128)S(1)}, f32[16,768]{1,0:T(8,128)S(1)}, u32[]{:S(2)}, u32[]{:S(2)}) collective-permute-start(f32[16,768]{1,0:T(8,128)S(1)} %partner_late.1), channel_id=1, source_target_pairs={{0,3},{1,2},{2,1},{3,0},{4,7},{5,6},{6,5},{7,4},{8,11},{9,10},{10,... | collective-permute-start | bytes 147464 | tf_op jit(solution)/shard_map/ppermute | solution.py:220
  15.9 1.2 %add_own.1.refs_0_ = f32[16,768]{1,0:T(8,128)S(1)} custom-call(s32[2,1]{1,0:T(2,128)S(4)} %get-tuple-element.29.masks_ref, bf16[64,768]{1,0:T(8,128)(2,1)S(1)} %get-tuple-element.30.side_ref, bf16[8,32,768]{2,1,0:T(8,128)(2,1)S(1)} %constant_dynamic-update-slice_fusion.blocks_ref, ...), custom_call_target="tpu_custom_call", output_to_operand_aliasing={{}: (3, {})} | custom-call | tf_op jit(solution)/shard_map/add_own/pallas_call | solution.py:240
  17.1 1.8 %collective-permute-done.6.refs_1_ = f32[16,768]{1,0:T(8,128)S(1)} collective-permute-done((f32[16,768]{1,0:T(8,128)S(1)}, f32[16,768]{1,0:T(8,128)S(1)}, u32[]{:S(2)}, u32[]{:S(2)}) %collective-permute-start.6) | collective-permute-done | bytes 49184 | tf_op jit(solution)/shard_map/ppermute | solution.py:220
  18.9 0.4 %last.1 = (f32[16,768]{1,0:T(8,128)S(1)}, f32[16,8,128]{2,1,0:T(8,128)S(1)}) custom-call(bf16[16,768]{1,0:T(8,128)(2,1)S(1)} %get-tuple-element.25.vectors_ref, f32[1,768]{1,0:T(1,128)S(1)} %get-tuple-element.26.root_ref, f32[16,768]{1,0:T(8,128)S(1)} %add_own.1.refs_0_, f32[16,768]{1,0:T(8,128)S(1)} %collective-permute-done.6.refs_1_), custom_call_target="tpu_custom_call" | custom-call | tf_op jit(solution)/shard_map/last/pallas_call | solution.py:240
  19.2 10.9 %all_to_all.5.grams_ref = f32[16,8,128]{2,1,0:T(8,128)S(1)} all-to-all(f32[16,8,128]{2,1,0:T(8,128)S(1)} %get-tuple-element.46), channel_id=1, replica_groups=mesh['grp'=2,'row'=4,'col'=4] {'row','col'}, dimensions={0} | all-to-all | bytes 131072 | tf_op jit(solution)/shard_map/all_to_all | solution.py:364
  30.2 1.3 %finish.1 = (f32[16,768]{1,0:T(8,128)}, f32[16,16]{1,0:T(8,128)}) custom-call(f32[16,8,128]{2,1,0:T(8,128)S(1)} %all_to_all.5.grams_ref, f32[16,768]{1,0:T(8,128)S(1)} %get-tuple-element.47.applied_ref), custom_call_target="tpu_custom_call" | custom-call | tf_op jit(solution)/shard_map/finish/pallas_call | solution.py:240
  (9 shorter events, 0.1 us)
Async XLA Ops:
  1.4 7.5 %collective-permute-start.2 = (bf16[32,768]{1,0:T(8,128)(2,1)S(1)}, bf16[32,768]{1,0:T(8,128)(2,1)S(1)}, u32[]{:S(2)}, u32[]{:S(2)}) collective-permute-start(bf16[32,768]{1,0:T(8,128)(2,1)S(1)} %get-tuple-element.28.packed_ref), channel_id=1, source_target_pairs={{0,3},{1,2},{2,1},{3,0},{4,7},{5,6},{6,5},{7,4},{8,11},{9,10},{10,... | collective-permute-start | bytes 147464 | tf_op jit(solution)/shard_map/ppermute | solution.py:220
  3.9 5.2 %collective-permute-start.1 = (bf16[32,768]{1,0:T(8,128)(2,1)S(1)}, bf16[32,768]{1,0:T(8,128)(2,1)S(1)}, u32[]{:S(2)}, u32[]{:S(2)}) collective-permute-start(bf16[32,768]{1,0:T(8,128)(2,1)S(1)} %get-tuple-element.28.packed_ref), channel_id=1, source_target_pairs={{0,9},{1,8},{2,11},{3,10},{4,13},{5,12},{6,15},{7,14},{8,1},{9,0},... | collective-permute-start | bytes 147464 | tf_op jit(solution)/shard_map/ppermute | solution.py:220
  6.8 3.9 %collective-permute-start = (bf16[32,768]{1,0:T(8,128)(2,1)S(1)}, bf16[32,768]{1,0:T(8,128)(2,1)S(1)}, u32[]{:S(2)}, u32[]{:S(2)}) collective-permute-start(bf16[32,768]{1,0:T(8,128)(2,1)S(1)} %get-tuple-element.28.packed_ref), channel_id=1, source_target_pairs={{0,5},{1,4},{2,7},{3,6},{4,1},{5,0},{6,3},{7,2},{8,13},{9,12},{10,... | collective-permute-start | bytes 147464 | tf_op jit(solution)/shard_map/ppermute | solution.py:220
  7.8 5.3 %collective-permute-start.4 = (bf16[32,768]{1,0:T(8,128)(2,1)S(1)}, bf16[32,768]{1,0:T(8,128)(2,1)S(1)}, u32[]{:S(2)}, u32[]{:S(2)}) collective-permute-start(bf16[32,768]{1,0:T(8,128)(2,1)S(1)} %get-tuple-element.28.packed_ref), channel_id=1, source_target_pairs={{0,13},{1,12},{2,15},{3,14},{4,9},{5,8},{6,11},{7,10},{8,5},{9,4},... | collective-permute-start | bytes 147464 | tf_op jit(solution)/shard_map/ppermute | solution.py:220
  10.7 3.0 %collective-permute-start.3 = (bf16[4,32,768]{2,1,0:T(8,128)(2,1)S(1)}, bf16[4,32,768]{2,1,0:T(8,128)(2,1)S(1)}, u32[]{:S(2)}, u32[]{:S(2)}) collective-permute-start(bf16[4,32,768]{2,1,0:T(8,128)(2,1)S(1)} %pad_maximum_fusion.blocks_ref), channel_id=1, source_target_pairs={{0,1},{1,0},{2,3},{3,2},{4,5},{5,4},{6,7},{7,6},{8,9},{9,8},{10,11... | collective-permute-start | bytes 589832 | tf_op jit(solution)/shard_map/ppermute | solution.py:220
  13.1 1.6 %collective-permute-start.5 = (bf16[1,32,768]{2,1,0:T(8,128)(2,1)S(1)}, bf16[1,32,768]{2,1,0:T(8,128)(2,1)S(1)}, u32[]{:S(2)}, u32[]{:S(2)}) collective-permute-start(bf16[1,32,768]{2,1,0:T(8,128)(2,1)S(1)} %bitcast.12), channel_id=1, source_target_pairs={{0,1},{1,0},{2,3},{3,2},{4,5},{5,4},{6,7},{7,6},{8,9},{9,8},{10,11... | collective-permute-start | bytes 147464 | tf_op jit(solution)/shard_map/ppermute | solution.py:220
  15.3 3.5 %collective-permute-start.6 = (f32[16,768]{1,0:T(8,128)S(1)}, f32[16,768]{1,0:T(8,128)S(1)}, u32[]{:S(2)}, u32[]{:S(2)}) collective-permute-start(f32[16,768]{1,0:T(8,128)S(1)} %partner_late.1), channel_id=1, source_target_pairs={{0,3},{1,2},{2,1},{3,0},{4,7},{5,6},{6,5},{7,4},{8,11},{9,10},{10,... | collective-permute-start | bytes 147464 | tf_op jit(solution)/shard_map/ppermute | solution.py:220
